TPU v7x, 256 devices: a whole 4x4x8 slice. The times are simulated.
256 devices in a mesh: beam: 32 (over x, y, core), tensor: 8 (over z).
Axes of the slice: x: 4, y: 4, z: 8, core: 2. Of those that a mesh axis runs over, the one named last changes fastest.
Arguments:
- parents: int32 [256], P('beam'), may hold values from 0 to 255, as said below
- lengths: int32 [256], P('beam'), may hold values from 256 to 2048
- queries: bfloat16 [256, 8192], P('beam', 'tensor'), may hold values from -8 to 8
- token_keys: bfloat16 [256, 1024], P('beam', 'tensor'), may hold values from -6 to 6
- token_values: bfloat16 [256, 1024], P('beam', 'tensor'), may hold values from -6 to 6
- key_cache: bfloat16 [256, 8, 2048, 128], P('beam', 'tensor'), may hold values from -3 to 3
- cached_value_rows: bfloat16 [256, 8, 2048, 128], P('beam', 'tensor'), may hold values from -6 to 6
- output_weight: bfloat16 [8192, 8192], P('tensor', 'beam'), may hold values from -0.0625 to 0.0625
Outputs:
- projected: bfloat16 [256, 8192], P('tensor', 'beam')
Inputs may be any that keep to these rules, and one draw needn't show every extreme that they name: The parent of a new slot is one of the 32 old slots of the same query. In each aligned block of 8 new slots, exactly 2 parents lie in each aligned block of 8 old slots of that query when 8 * 8 >= 32, else at most one does.
All inputs are finite; a program needn't handle non-finite values.
Results may differ from a plain program's by a relative error of at most 0.0056.
Values may be sent and summed in bfloat16 or wider, within the bound.
No kernel may reach another device: no remote copies, remote signals or barrier semaphores. Data moves between devices by JAX's collectives and lax.ppermute only.
A program may use at most 128 MiB of HBM per device.

v0:
```python
import jax
import jax.numpy as jnp
from jax import lax
from jax.sharding import PartitionSpec as P

HEAD_SIZE = 128
BEAMS = 32


def from_behind(block, axis, distance):
    devices = range(lax.axis_size(axis))
    route = [(i - distance, i) for i in devices if i - distance in devices]
    return lax.ppermute(block, axis, route)


def attend_part(query_head_rows, fresh_key, key_rows, value_rows, row_lengths):
    score_scale = HEAD_SIZE ** (-0.5)
    scores = (
        jnp.einsum("ckgd,ckld->ckgl", query_head_rows, key_rows, preferred_element_type=jnp.float32)
        * score_scale
    )
    positions = jnp.arange(key_rows.shape[2], dtype=jnp.int32)
    valid = positions[None, None, None, :] < row_lengths[:, None, None, None]
    scores = jnp.where(valid, scores, -1e30)
    new_score = (
        jnp.einsum("ckgd,ckd->ckg", query_head_rows, fresh_key, preferred_element_type=jnp.float32)
        * score_scale
    )
    maximum = jnp.maximum(jnp.max(scores, axis=-1), new_score)
    weights = jnp.exp(scores - maximum[..., None])
    denominator = jnp.sum(weights, axis=-1)
    weighted = jnp.einsum(
        "ckgl,ckld->ckgd",
        weights.astype(jnp.bfloat16),
        value_rows,
        preferred_element_type=jnp.float32,
    )
    return (weighted, denominator, maximum)


def pick_matches(needed, capacity):
    ranking = jnp.cumsum(needed) - needed
    matches = (ranking[None, :] == jnp.arange(capacity, dtype=jnp.int32)[:, None]) & (
        needed[None, :] == 1
    )
    present = jnp.any(matches, axis=1)
    return (matches, present)


def sender_pick(window_parents, own_index, offset, reach, slot_count, capacity, beam_count):
    target_dev = own_index + offset
    within = (target_dev >= 0) & (target_dev < beam_count)
    their_parents = window_parents[
        (offset + reach) * slot_count : (offset + reach + 1) * slot_count
    ]
    needed = (within & (their_parents // slot_count == own_index)).astype(jnp.int32)
    matches, present = pick_matches(needed, capacity)
    picked_rows = jnp.sum(jnp.where(matches, (their_parents % slot_count)[None, :], 0), axis=1)
    return (picked_rows, present)


def remote_index(source, own_slots, own_index, offsets, slot_count, capacity):
    pool_slot = own_slots
    for position, offset in enumerate(offsets):
        wanted = source == own_index - offset
        wanted_int = wanted.astype(jnp.int32)
        ranking = jnp.cumsum(wanted_int) - wanted_int
        pool_slot = jnp.where(wanted, slot_count + position * capacity + ranking, pool_slot)
    return pool_slot


def lookup(table, wanted):
    slots_all = jnp.arange(table.shape[0], dtype=jnp.int32)
    return jnp.sum(jnp.where(slots_all[None, :] == wanted[:, None], table[None, :], 0), axis=1)


def body(
    parents, lengths, queries, token_keys, token_values, key_cache, cached_value_rows, output_weight
):
    slot_count = parents.shape[0]
    kv_heads = key_cache.shape[1]
    grouped_queries = queries.shape[1] // (kv_heads * HEAD_SIZE)
    beam_count = lax.axis_size("beam")
    own_index = lax.axis_index("beam")
    group_size = BEAMS // slot_count
    reach = group_size - 1
    capacity = max(1, slot_count * slot_count // BEAMS)
    offsets = [offset for offset in range(-reach, group_size) if offset != 0]
    parent_pieces = []
    length_pieces = []
    for offset in range(-reach, group_size):
        if offset == 0:
            parent_pieces.append(parents)
            length_pieces.append(lengths)
        else:
            got_parents, got_lengths = from_behind((parents, lengths), "beam", -offset)
            parent_pieces.append(got_parents)
            length_pieces.append(got_lengths)
    window_parents = jnp.concatenate(parent_pieces, axis=0)
    window_lengths = jnp.concatenate(length_pieces, axis=0)
    window_start = (own_index - reach) * slot_count
    source = parents // slot_count
    source_row = parents % slot_count
    parent_lengths = lookup(window_lengths, parents - window_start)
    query_head_rows = queries.reshape(slot_count, kv_heads, grouped_queries, HEAD_SIZE)
    fresh_key = token_keys.reshape(slot_count, kv_heads, HEAD_SIZE)
    fresh_value = token_values.reshape(slot_count, kv_heads, HEAD_SIZE)
    pool_keys = [key_cache]
    pool_values = [cached_value_rows]
    for offset in offsets:
        picked_rows, present = sender_pick(
            window_parents, own_index, offset, reach, slot_count, capacity, beam_count
        )
        present_mask = present[:, None, None, None]
        packed_keys = jnp.take(key_cache, picked_rows, axis=0)
        packed_values = jnp.take(cached_value_rows, picked_rows, axis=0)
        packed_keys = jnp.where(present_mask, packed_keys, jnp.zeros_like(packed_keys))
        packed_values = jnp.where(present_mask, packed_values, jnp.zeros_like(packed_values))
        got_keys, got_values = from_behind((packed_keys, packed_values), "beam", offset)
        pool_keys.append(got_keys)
        pool_values.append(got_values)
    pool_slot = remote_index(source, source_row, own_index, offsets, slot_count, capacity)
    key_rows = jnp.take(jnp.concatenate(pool_keys, axis=0), pool_slot, axis=0)
    value_rows = jnp.take(jnp.concatenate(pool_values, axis=0), pool_slot, axis=0)
    weighted, denominator, maximum = attend_part(
        query_head_rows, fresh_key, key_rows, value_rows, parent_lengths
    )
    score_scale = HEAD_SIZE ** (-0.5)
    new_score = (
        jnp.einsum("ckgd,ckd->ckg", query_head_rows, fresh_key, preferred_element_type=jnp.float32)
        * score_scale
    )
    new_weight = jnp.exp(new_score - maximum)
    denominator = denominator + new_weight
    rounded_new = lax.optimization_barrier(new_weight.astype(jnp.bfloat16)).astype(jnp.float32)
    weighted = weighted + rounded_new[..., None] * fresh_value[:, :, None, :].astype(jnp.float32)
    heads_out = (
        (weighted / denominator[..., None])
        .astype(jnp.bfloat16)
        .reshape(slot_count, kv_heads * grouped_queries * HEAD_SIZE)
    )
    terms = jnp.dot(
        lax.all_gather(heads_out, "beam", axis=0, tiled=True),
        output_weight,
        preferred_element_type=jnp.float32,
    )
    return lax.psum_scatter(terms, "tensor", scatter_dimension=0, tiled=True).astype(jnp.bfloat16)


def solution(mesh):
    in_specs = (
        P("beam"),
        P("beam"),
        P("beam", "tensor"),
        P("beam", "tensor"),
        P("beam", "tensor"),
        P("beam", "tensor", None, None),
        P("beam", "tensor", None, None),
        P("tensor", "beam"),
    )
    out_specs = P("tensor", "beam")
    return jax.shard_map(body, mesh=mesh, in_specs=in_specs, out_specs=out_specs, check_vma=False)
```

profile of v0, /device:TPU:1, one launch (start us, length us, event | category | flops | bytes accessed | tf_op | source)
XLA Modules:
  0.0 360.5 jit_solution(11998327252257954659)
XLA Ops:
  6.6 6.3 %collective-permute-start.6 = (s32[8]{0:T(128)}, s32[8]{0:T(128)S(1)}, u32[]{:S(2)}, u32[]{:S(2)}) collective-permute-start(s32[8]{0:T(128)} %param.12), channel_id=1, source_target_pairs={{0,24},{8,32},{16,40},{24,48},{32,56},{40,64},{48,72},{56,80},{64,... | collective-permute-start | bytes 104 | tf_op jit(solution)/shard_map/ppermute | solution.py:13
  13.0 2.3 collective-permute-start.8
  15.3 1.9 collective-permute-start.12
  17.2 3.6 %collective-permute-start.10 = (s32[8]{0:T(128)}, s32[8]{0:T(128)S(1)}, u32[]{:S(2)}, u32[]{:S(2)}) collective-permute-start(s32[8]{0:T(128)} %param.12), channel_id=1, source_target_pairs={{0,8},{8,16},{16,24},{24,32},{32,40},{40,48},{48,56},{56,64},{64,7... | collective-permute-start | bytes 104 | tf_op jit(solution)/shard_map/ppermute | solution.py:13
  20.9 1.3 collective-permute-start.16
  22.8 4.6 %constant_dynamic-update-slice_fusion = bf16[20,1,2048,128]{3,2,1,0:T(8,128)(2,1)} fusion(bf16[8,1,2048,128]{3,2,1,0:T(8,128)(2,1)} %param.17), kind=kLoop, calls=%fused_computation.72 | loop fusion | bytes 8388608
  29.9 4.4 %constant_dynamic-update-slice_fusion.1 = bf16[20,1,2048,128]{3,2,1,0:T(8,128)(2,1)} fusion(bf16[8,1,2048,128]{3,2,1,0:T(8,128)(2,1)} %param.18), kind=kLoop, calls=%fused_computation.73 | loop fusion | bytes 8388608
  34.4 1.3 collective-permute-start.14
  36.2 6.4 %collective-permute-start = (s32[8]{0:T(128)S(1)}, s32[8]{0:T(128)S(1)}, u32[]{:S(2)}, u32[]{:S(2)}) collective-permute-start(s32[8]{0:T(128)S(1)} %copy-done.7), channel_id=1, source_target_pairs={{0,24},{8,32},{16,40},{24,48},{32,56},{40,64},{48,72},{56,80},{64,... | collective-permute-start | bytes 104 | tf_op jit(solution)/shard_map/ppermute | solution.py:13
  43.0 3.8 %gather_fusion = bf16[2,2048,128]{2,1,0:T(8,128)(2,1)} fusion(bf16[8,2048,128]{2,1,0:T(8,128)(2,1)} %bitcast.236, s32[1024]{0:T(1024)S(1)} %get-tuple-element.49), kind=kCustom, calls=%fused_computation.clone | custom fusion | bytes 2097160 | tf_op jit(solution)/shard_map/jit(_take)/gather | solution.py:115
  46.9 3.9 %gather_fusion.7 = bf16[2,2048,128]{2,1,0:T(8,128)(2,1)} fusion(bf16[8,2048,128]{2,1,0:T(8,128)(2,1)} %bitcast.242, s32[1024]{0:T(1024)S(1)} %get-tuple-element.49), kind=kCustom, calls=%fused_computation.7.clone | custom fusion | bytes 2097160 | tf_op jit(solution)/shard_map/jit(_take)/gather | solution.py:116
  50.7 2.9 gather_fusion.1
  53.6 2.9 gather_fusion.8
  56.7 3.0 collective-permute-start.1
  60.1 4.3 %collective-permute-start.2 = (s32[8]{0:T(128)S(1)}, s32[8]{0:T(128)S(1)}, u32[]{:S(2)}, u32[]{:S(2)}) collective-permute-start(s32[8]{0:T(128)S(1)} %copy-done.7), channel_id=1, source_target_pairs={{0,8},{8,16},{16,24},{24,32},{32,40},{40,48},{48,56},{56,64},{64,7... | collective-permute-start | bytes 104 | tf_op jit(solution)/shard_map/ppermute | solution.py:13
  64.8 3.8 %gather_fusion.2 = bf16[2,2048,128]{2,1,0:T(8,128)(2,1)} fusion(bf16[8,2048,128]{2,1,0:T(8,128)(2,1)} %bitcast.238, s32[1024]{0:T(1024)S(1)} %get-tuple-element.47), kind=kCustom, calls=%fused_computation.3.clone | custom fusion | bytes 2097160 | tf_op jit(solution)/shard_map/jit(_take)/gather | solution.py:115
  68.6 3.9 %gather_fusion.9 = bf16[2,2048,128]{2,1,0:T(8,128)(2,1)} fusion(bf16[8,2048,128]{2,1,0:T(8,128)(2,1)} %bitcast.244, s32[1024]{0:T(1024)S(1)} %get-tuple-element.47), kind=kCustom, calls=%fused_computation.9.clone | custom fusion | bytes 2097160 | tf_op jit(solution)/shard_map/jit(_take)/gather | solution.py:116
  72.6 3.9 %gather_fusion.3 = bf16[2,2048,128]{2,1,0:T(8,128)(2,1)} fusion(bf16[8,2048,128]{2,1,0:T(8,128)(2,1)} %bitcast.239, s32[1024]{0:T(1024)S(1)} %get-tuple-element.46), kind=kCustom, calls=%fused_computation.4.clone | custom fusion | bytes 2097160 | tf_op jit(solution)/shard_map/jit(_take)/gather | solution.py:115
  76.5 3.8 %gather_fusion.10 = bf16[2,2048,128]{2,1,0:T(8,128)(2,1)} fusion(bf16[8,2048,128]{2,1,0:T(8,128)(2,1)} %bitcast.245, s32[1024]{0:T(1024)S(1)} %get-tuple-element.46), kind=kCustom, calls=%fused_computation.10.clone | custom fusion | bytes 2097160 | tf_op jit(solution)/shard_map/jit(_take)/gather | solution.py:116
  80.5 1.9 collective-permute-start.3
  82.8 1.3 collective-permute-start.4
  84.4 3.8 %gather_fusion.4 = bf16[2,2048,128]{2,1,0:T(8,128)(2,1)} fusion(bf16[8,2048,128]{2,1,0:T(8,128)(2,1)} %bitcast.240, s32[1024]{0:T(1024)S(1)} %get-tuple-element.45), kind=kCustom, calls=%fused_computation.5.clone | custom fusion | bytes 2097160 | tf_op jit(solution)/shard_map/jit(_take)/gather | solution.py:115
  88.3 3.9 %gather_fusion.11 = bf16[2,2048,128]{2,1,0:T(8,128)(2,1)} fusion(bf16[8,2048,128]{2,1,0:T(8,128)(2,1)} %bitcast.246, s32[1024]{0:T(1024)S(1)} %get-tuple-element.45), kind=kCustom, calls=%fused_computation.11.clone | custom fusion | bytes 2097160 | tf_op jit(solution)/shard_map/jit(_take)/gather | solution.py:116
  92.3 3.8 %gather_fusion.5 = bf16[2,2048,128]{2,1,0:T(8,128)(2,1)} fusion(bf16[8,2048,128]{2,1,0:T(8,128)(2,1)} %bitcast.241, s32[1024]{0:T(1024)S(1)} %get-tuple-element.44), kind=kCustom, calls=%fused_computation.6.clone | custom fusion | bytes 2097160 | tf_op jit(solution)/shard_map/jit(_take)/gather | solution.py:115
  96.1 3.8 %gather_fusion.12 = bf16[2,2048,128]{2,1,0:T(8,128)(2,1)} fusion(bf16[8,2048,128]{2,1,0:T(8,128)(2,1)} %bitcast.247, s32[1024]{0:T(1024)S(1)} %get-tuple-element.44), kind=kCustom, calls=%fused_computation.12.clone | custom fusion | bytes 2097160 | tf_op jit(solution)/shard_map/jit(_take)/gather | solution.py:116
  100.1 3.3 fusion.40
  103.4 1.7 fusion.39
  105.1 3.2 fusion.38
  108.3 1.3 fusion.37
  109.6 1.3 fusion.36
  110.9 1.3 collective-permute-start.5
  112.2 1.3 collective-permute-start.7
  113.5 1.3 collective-permute-start.9
  114.8 1.9 collective-permute-start.11
  116.7 4.9 %collective-permute-start.13 = (bf16[2,1,2048,128]{3,2,0,1:T(8,128)(2,1)}, bf16[2,1,2048,128]{3,2,0,1:T(8,128)(2,1)}, u32[]{:S(2)}, u32[]{:S(2)}) collective-permute-start(bf16[2,1,2048,128]{3,2,0,1:T(8,128)(2,1)} %get-tuple-element.29), channel_id=1, source_target_pairs={{0,8},{8,16},{16,24},{24,32},{32,40},{40,48},{48,56},{56,64},{64,7... | collective-permute-start | bytes 3145736 | tf_op jit(solution)/shard_map/ppermute | solution.py:13
  121.6 7.7 %collective-permute-start.15 = (bf16[2,1,2048,128]{3,2,0,1:T(8,128)(2,1)}, bf16[2,1,2048,128]{3,2,0,1:T(8,128)(2,1)}, u32[]{:S(2)}, u32[]{:S(2)}) collective-permute-start(bf16[2,1,2048,128]{3,2,0,1:T(8,128)(2,1)} %get-tuple-element.27), channel_id=1, source_target_pairs={{0,16},{8,24},{16,32},{24,40},{32,48},{40,56},{48,64},{56,72},{64,... | collective-permute-start | bytes 3145736 | tf_op jit(solution)/shard_map/ppermute | solution.py:13
  129.5 2.8 fusion.35
  132.5 5.1 %collective-permute-done.7 = bf16[2,1,2048,128]{3,2,0,1:T(8,128)(2,1)} collective-permute-done((bf16[2,1,2048,128]{3,2,0,1:T(8,128)(2,1)}, bf16[2,1,2048,128]{3,2,0,1:T(8,128)(2,1)}, u32[]{:S(2)}, u32[]{:S(2)}) %collective-permute-start.7) | collective-permute-done | bytes 1048608 | tf_op jit(solution)/shard_map/ppermute | solution.py:13
  137.6 10.5 %collective-permute-start.17 = (bf16[2,1,2048,128]{3,2,0,1:T(8,128)(2,1)S(1)}, bf16[2,1,2048,128]{3,2,0,1:T(8,128)(2,1)S(1)}, u32[]{:S(2)}, u32[]{:S(2)}) collective-permute-start(bf16[2,1,2048,128]{3,2,0,1:T(8,128)(2,1)S(1)} %get-tuple-element.25), channel_id=1, source_target_pairs={{0,24},{8,32},{16,40},{24,48},{32,56},{40,64},{48,72},{56,80},{64,... | collective-permute-start | bytes 3145736 | tf_op jit(solution)/shard_map/ppermute | solution.py:13
  148.1 2.3 bitcast_dynamic-update-slice_fusion.11
  150.4 25.1 %collective-permute-done.9 = bf16[2,1,2048,128]{3,2,0,1:T(8,128)(2,1)} collective-permute-done((bf16[2,1,2048,128]{3,2,0,1:T(8,128)(2,1)}, bf16[2,1,2048,128]{3,2,0,1:T(8,128)(2,1)}, u32[]{:S(2)}, u32[]{:S(2)}) %collective-permute-start.9) | collective-permute-done | bytes 1048608 | tf_op jit(solution)/shard_map/ppermute | solution.py:13
  175.5 1.3 collective-permute-start.18
  176.8 2.3 bitcast_dynamic-update-slice_fusion.10
  179.1 1.3 collective-permute-start.19
  180.4 2.3 bitcast_dynamic-update-slice_fusion.9
  182.6 1.9 collective-permute-start.20
  184.6 2.3 bitcast_dynamic-update-slice_fusion.8
  186.9 3.6 %collective-permute-start.21 = (bf16[2,1,2048,128]{3,2,0,1:T(8,128)(2,1)S(1)}, bf16[2,1,2048,128]{3,2,0,1:T(8,128)(2,1)}, u32[]{:S(2)}, u32[]{:S(2)}) collective-permute-start(bf16[2,1,2048,128]{3,2,0,1:T(8,128)(2,1)S(1)} %get-tuple-element.30), channel_id=1, source_target_pairs={{0,8},{8,16},{16,24},{24,32},{32,40},{40,48},{48,56},{56,64},{64,7... | collective-permute-start | bytes 3145736 | tf_op jit(solution)/shard_map/ppermute | solution.py:13
  190.5 2.3 bitcast_dynamic-update-slice_fusion.7
  192.8 26.9 %collective-permute-start.22 = (bf16[2,1,2048,128]{3,2,0,1:T(8,128)(2,1)S(1)}, bf16[2,1,2048,128]{3,2,0,1:T(8,128)(2,1)}, u32[]{:S(2)}, u32[]{:S(2)}) collective-permute-start(bf16[2,1,2048,128]{3,2,0,1:T(8,128)(2,1)S(1)} %get-tuple-element.28), channel_id=1, source_target_pairs={{0,16},{8,24},{16,32},{24,40},{32,48},{40,56},{48,64},{56,72},{64,... | collective-permute-start | bytes 3145736 | tf_op jit(solution)/shard_map/ppermute | solution.py:13
  220.7 7.0 %gather_fusion.6 = bf16[8,2048,128]{2,1,0:T(8,128)(2,1)} fusion(bf16[20,2048,128]{2,1,0:T(8,128)(2,1)} %bitcast.249, s32[1024]{0:T(1024)S(1)} %pad_clamp_fusion), kind=kCustom, calls=%fused_computation.1.clone | custom fusion | bytes 8388640 | tf_op jit(solution)/shard_map/jit(_take)/gather | solution.py:123
  227.8 3.5 fusion.70
  231.6 6.9 %collective-permute-start.23 = (bf16[2,1,2048,128]{3,2,0,1:T(8,128)(2,1)}, bf16[2,1,2048,128]{3,2,0,1:T(8,128)(2,1)S(1)}, u32[]{:S(2)}, u32[]{:S(2)}) collective-permute-start(bf16[2,1,2048,128]{3,2,0,1:T(8,128)(2,1)} %get-tuple-element.26), channel_id=1, source_target_pairs={{0,24},{8,32},{16,40},{24,48},{32,56},{40,64},{48,72},{56,80},{64,... | collective-permute-start | bytes 3145736 | tf_op jit(solution)/shard_map/ppermute | solution.py:13
  238.4 2.3 bitcast_dynamic-update-slice_fusion.5
  240.7 12.2 %collective-permute-done.19 = bf16[2,1,2048,128]{3,2,0,1:T(8,128)(2,1)} collective-permute-done((bf16[2,1,2048,128]{3,2,0,1:T(8,128)(2,1)}, bf16[2,1,2048,128]{3,2,0,1:T(8,128)(2,1)}, u32[]{:S(2)}, u32[]{:S(2)}) %collective-permute-start.19) | collective-permute-done | bytes 1048608 | tf_op jit(solution)/shard_map/ppermute | solution.py:13
  252.9 2.3 bitcast_dynamic-update-slice_fusion.4
  255.2 2.3 bitcast_dynamic-update-slice_fusion.3
  257.5 2.3 bitcast_dynamic-update-slice_fusion.2
  259.8 2.4 bitcast_dynamic-update-slice_fusion.1
  263.2 7.1 %gather_fusion.13 = bf16[8,2048,128]{2,1,0:T(8,128)(2,1)} fusion(bf16[20,2048,128]{2,1,0:T(8,128)(2,1)} %bitcast.248, s32[1024]{0:T(1024)S(1)} %pad_clamp_fusion), kind=kCustom, calls=%fused_computation.13.clone | custom fusion | bytes 8388640 | tf_op jit(solution)/shard_map/jit(_take)/gather | solution.py:124
  270.3 3.0 fusion.26
  273.3 45.0 %all_gather.3 = bf16[256,1024]{1,0:T(8,128)(2,1)S(1)} all-gather(bf16[8,1024]{1,0:T(8,128)(2,1)S(1)} %bitcast.250), channel_id=1, replica_groups=mesh['beam'=32,'tensor'=8] {'beam'}, dimensions={0}, use_global_device_ids=true | all-gather | bytes 540672 | tf_op jit(solution)/shard_map/all_gather | solution.py:143
  319.4 32.9 %reduce-scatter.2.cloned.1.call-done = f32[32,256]{1,0:T(8,128)} async-done(((f32[256,256]{1,0:T(8,128)}), f32[32,256]{1,0:T(8,128)}) %reduce-scatter.2.cloned.1.call-update) | async-done | bytes 32784 | tf_op jit(solution)/shard_map/reduce_scatter | solution.py:147
  352.3 1.4 convert_element_type.75
  (118 shorter events, 9.9 us)
Async XLA Ops:
  6.5 311.8 %copy-start = (bf16[1024,256]{1,0:T(8,128)(2,1)S(1)}, bf16[1024,256]{1,0:T(8,128)(2,1)}, u32[]{:S(2)}) copy-start(bf16[1024,256]{1,0:T(8,128)(2,1)} %param.19) | copy-start | bytes 1572868
  6.5 27.9 %copy-start.6 = (s32[8]{0:T(128)S(1)}, s32[8]{0:T(128)}, u32[]{:S(2)}) copy-start(s32[8]{0:T(128)} %param.12) | copy-start | bytes 100
  6.5 27.7 %copy-start.5 = (bf16[8,128]{1,0:T(8,128)(2,1)S(1)}, bf16[8,128]{1,0:T(8,128)(2,1)}, u32[]{:S(2)}) copy-start(bf16[8,128]{1,0:T(8,128)(2,1)} %param.16) | copy-start | bytes 6148
  6.5 27.7 %copy-start.8 = (bf16[8,1024]{1,0:T(8,128)(2,1)S(1)}, bf16[8,1024]{1,0:T(8,128)(2,1)}, u32[]{:S(2)}) copy-start(bf16[8,1024]{1,0:T(8,128)(2,1)} %param.14) | copy-start | bytes 49156
  6.5 27.7 %copy-start.9 = (bf16[8,128]{1,0:T(8,128)(2,1)S(1)}, bf16[8,128]{1,0:T(8,128)(2,1)}, u32[]{:S(2)}) copy-start(bf16[8,128]{1,0:T(8,128)(2,1)} %param.15) | copy-start | bytes 6148
  6.5 29.7 %copy-start.7 = (s32[8]{0:T(128)S(1)}, s32[8]{0:T(128)}, u32[]{:S(2)}) copy-start(s32[8]{0:T(128)} %param.13) | copy-start | bytes 100
  6.6 345.7 %reduce-scatter.2.cloned.1.call-start = ((), (), s32[]{:S(2)}) async-start(), calls=%async_computation.1 | async-start | bytes 294912 | tf_op jit(solution)/shard_map/reduce_scatter | solution.py:147
  6.6 27.8 %collective-permute-start.6 = (s32[8]{0:T(128)}, s32[8]{0:T(128)S(1)}, u32[]{:S(2)}, u32[]{:S(2)}) collective-permute-start(s32[8]{0:T(128)} %param.12), channel_id=1, source_target_pairs={{0,24},{8,32},{16,40},{24,48},{32,56},{40,64},{48,72},{56,80},{64,... | collective-permute-start | bytes 104 | tf_op jit(solution)/shard_map/ppermute | solution.py:13
  13.0 23.3 %collective-permute-start.8 = (s32[8]{0:T(128)}, s32[8]{0:T(128)S(1)}, u32[]{:S(2)}, u32[]{:S(2)}) collective-permute-start(s32[8]{0:T(128)} %param.12), channel_id=1, source_target_pairs={{0,16},{8,24},{16,32},{24,40},{32,48},{40,56},{48,64},{56,72},{64,... | collective-permute-start | bytes 104 | tf_op jit(solution)/shard_map/ppermute | solution.py:13
  15.3 41.5 %collective-permute-start.12 = (s32[8]{0:T(128)}, s32[8]{0:T(128)S(1)}, u32[]{:S(2)}, u32[]{:S(2)}) collective-permute-start(s32[8]{0:T(128)} %param.12), channel_id=1, source_target_pairs={{8,0},{16,8},{24,16},{32,24},{40,32},{48,40},{56,48},{64,56},{72,6... | collective-permute-start | bytes 104 | tf_op jit(solution)/shard_map/ppermute | solution.py:13
  17.2 42.9 %collective-permute-start.10 = (s32[8]{0:T(128)}, s32[8]{0:T(128)S(1)}, u32[]{:S(2)}, u32[]{:S(2)}) collective-permute-start(s32[8]{0:T(128)} %param.12), channel_id=1, source_target_pairs={{0,8},{8,16},{16,24},{24,32},{32,40},{40,48},{48,56},{56,64},{64,7... | collective-permute-start | bytes 104 | tf_op jit(solution)/shard_map/ppermute | solution.py:13
  20.9 59.6 %collective-permute-start.16 = (s32[8]{0:T(128)}, s32[8]{0:T(128)S(1)}, u32[]{:S(2)}, u32[]{:S(2)}) collective-permute-start(s32[8]{0:T(128)} %param.12), channel_id=1, source_target_pairs={{24,0},{32,8},{40,16},{48,24},{56,32},{64,40},{72,48},{80,56},{88,... | collective-permute-start | bytes 104 | tf_op jit(solution)/shard_map/ppermute | solution.py:13
  34.4 48.3 %collective-permute-start.14 = (s32[8]{0:T(128)S(1)}, s32[8]{0:T(128)S(1)}, u32[]{:S(2)}, u32[]{:S(2)}) collective-permute-start(s32[8]{0:T(128)S(1)} %copy-done.6), channel_id=1, source_target_pairs={{16,0},{24,8},{32,16},{40,24},{48,32},{56,40},{64,48},{72,56},{80,... | collective-permute-start | bytes 104 | tf_op jit(solution)/shard_map/ppermute | solution.py:13
  36.2 74.6 %collective-permute-start = (s32[8]{0:T(128)S(1)}, s32[8]{0:T(128)S(1)}, u32[]{:S(2)}, u32[]{:S(2)}) collective-permute-start(s32[8]{0:T(128)S(1)} %copy-done.7), channel_id=1, source_target_pairs={{0,24},{8,32},{16,40},{24,48},{32,56},{40,64},{48,72},{56,80},{64,... | collective-permute-start | bytes 104 | tf_op jit(solution)/shard_map/ppermute | solution.py:13
  56.7 55.4 %collective-permute-start.1 = (s32[8]{0:T(128)S(1)}, s32[8]{0:T(128)S(1)}, u32[]{:S(2)}, u32[]{:S(2)}) collective-permute-start(s32[8]{0:T(128)S(1)} %copy-done.7), channel_id=1, source_target_pairs={{0,16},{8,24},{16,32},{24,40},{32,48},{40,56},{48,64},{56,72},{64,... | collective-permute-start | bytes 104 | tf_op jit(solution)/shard_map/ppermute | solution.py:13
  60.1 53.3 %collective-permute-start.2 = (s32[8]{0:T(128)S(1)}, s32[8]{0:T(128)S(1)}, u32[]{:S(2)}, u32[]{:S(2)}) collective-permute-start(s32[8]{0:T(128)S(1)} %copy-done.7), channel_id=1, source_target_pairs={{0,8},{8,16},{16,24},{24,32},{32,40},{40,48},{48,56},{56,64},{64,7... | collective-permute-start | bytes 104 | tf_op jit(solution)/shard_map/ppermute | solution.py:13
  80.5 34.3 %collective-permute-start.3 = (s32[8]{0:T(128)S(1)}, s32[8]{0:T(128)S(1)}, u32[]{:S(2)}, u32[]{:S(2)}) collective-permute-start(s32[8]{0:T(128)S(1)} %copy-done.7), channel_id=1, source_target_pairs={{8,0},{16,8},{24,16},{32,24},{40,32},{48,40},{56,48},{64,56},{72,6... | collective-permute-start | bytes 104 | tf_op jit(solution)/shard_map/ppermute | solution.py:13
  82.8 33.9 %collective-permute-start.4 = (s32[8]{0:T(128)S(1)}, s32[8]{0:T(128)S(1)}, u32[]{:S(2)}, u32[]{:S(2)}) collective-permute-start(s32[8]{0:T(128)S(1)} %copy-done.7), channel_id=1, source_target_pairs={{16,0},{24,8},{32,16},{40,24},{48,32},{56,40},{64,48},{72,56},{80,... | collective-permute-start | bytes 104 | tf_op jit(solution)/shard_map/ppermute | solution.py:13
  99.9 8.3 %copy-start.1 = (bf16[2,2048,128]{2,1,0:T(8,128)(2,1)S(1)}, bf16[2,2048,128]{2,1,0:T(8,128)(2,1)}, u32[]{:S(2)}) copy-start(bf16[2,2048,128]{2,1,0:T(8,128)(2,1)} %gather_fusion.3) | copy-start | bytes 3145732
  99.9 8.3 %copy-start.2 = (bf16[2,2048,128]{2,1,0:T(8,128)(2,1)S(1)}, bf16[2,2048,128]{2,1,0:T(8,128)(2,1)}, u32[]{:S(2)}) copy-start(bf16[2,2048,128]{2,1,0:T(8,128)(2,1)} %gather_fusion.10) | copy-start | bytes 3145732
  99.9 9.6 %copy-start.3 = (bf16[2,2048,128]{2,1,0:T(8,128)(2,1)S(1)}, bf16[2,2048,128]{2,1,0:T(8,128)(2,1)}, u32[]{:S(2)}) copy-start(bf16[2,2048,128]{2,1,0:T(8,128)(2,1)} %gather_fusion.4) | copy-start | bytes 3145732
  99.9 9.6 %copy-start.4 = (bf16[2,2048,128]{2,1,0:T(8,128)(2,1)S(1)}, bf16[2,2048,128]{2,1,0:T(8,128)(2,1)}, u32[]{:S(2)}) copy-start(bf16[2,2048,128]{2,1,0:T(8,128)(2,1)} %gather_fusion.11) | copy-start | bytes 3145732
  110.9 10.8 %collective-permute-start.5 = (s32[8]{0:T(128)S(1)}, s32[8]{0:T(128)S(1)}, u32[]{:S(2)}, u32[]{:S(2)}) collective-permute-start(s32[8]{0:T(128)S(1)} %copy-done.7), channel_id=1, source_target_pairs={{24,0},{32,8},{40,16},{48,24},{56,32},{64,40},{72,48},{80,56},{88,... | collective-permute-start | bytes 104 | tf_op jit(solution)/shard_map/ppermute | solution.py:13
  112.2 25.4 %collective-permute-start.7 = (bf16[2,1,2048,128]{3,2,0,1:T(8,128)(2,1)}, bf16[2,1,2048,128]{3,2,0,1:T(8,128)(2,1)}, u32[]{:S(2)}, u32[]{:S(2)}) collective-permute-start(bf16[2,1,2048,128]{3,2,0,1:T(8,128)(2,1)} %get-tuple-element.35), channel_id=1, source_target_pairs={{24,0},{32,8},{40,16},{48,24},{56,32},{64,40},{72,48},{80,56},{88,... | collective-permute-start | bytes 3145736 | tf_op jit(solution)/shard_map/ppermute | solution.py:13
  113.5 62.0 %collective-permute-start.9 = (bf16[2,1,2048,128]{3,2,0,1:T(8,128)(2,1)}, bf16[2,1,2048,128]{3,2,0,1:T(8,128)(2,1)}, u32[]{:S(2)}, u32[]{:S(2)}) collective-permute-start(bf16[2,1,2048,128]{3,2,0,1:T(8,128)(2,1)} %get-tuple-element.33), channel_id=1, source_target_pairs={{16,0},{24,8},{32,16},{40,24},{48,32},{56,40},{64,48},{72,56},{80,... | collective-permute-start | bytes 3145736 | tf_op jit(solution)/shard_map/ppermute | solution.py:13
  114.8 64.3 %collective-permute-start.11 = (bf16[2,1,2048,128]{3,2,0,1:T(8,128)(2,1)}, bf16[2,1,2048,128]{3,2,0,1:T(8,128)(2,1)}, u32[]{:S(2)}, u32[]{:S(2)}) collective-permute-start(bf16[2,1,2048,128]{3,2,0,1:T(8,128)(2,1)} %get-tuple-element.31), channel_id=1, source_target_pairs={{8,0},{16,8},{24,16},{32,24},{40,32},{48,40},{56,48},{64,56},{72,6... | collective-permute-start | bytes 3145736 | tf_op jit(solution)/shard_map/ppermute | solution.py:13
  116.7 65.9 %collective-permute-start.13 = (bf16[2,1,2048,128]{3,2,0,1:T(8,128)(2,1)}, bf16[2,1,2048,128]{3,2,0,1:T(8,128)(2,1)}, u32[]{:S(2)}, u32[]{:S(2)}) collective-permute-start(bf16[2,1,2048,128]{3,2,0,1:T(8,128)(2,1)} %get-tuple-element.29), channel_id=1, source_target_pairs={{0,8},{8,16},{16,24},{24,32},{32,40},{40,48},{48,56},{56,64},{64,7... | collective-permute-start | bytes 3145736 | tf_op jit(solution)/shard_map/ppermute | solution.py:13
  121.6 65.3 %collective-permute-start.15 = (bf16[2,1,2048,128]{3,2,0,1:T(8,128)(2,1)}, bf16[2,1,2048,128]{3,2,0,1:T(8,128)(2,1)}, u32[]{:S(2)}, u32[]{:S(2)}) collective-permute-start(bf16[2,1,2048,128]{3,2,0,1:T(8,128)(2,1)} %get-tuple-element.27), channel_id=1, source_target_pairs={{0,16},{8,24},{16,32},{24,40},{32,48},{40,56},{48,64},{56,72},{64,... | collective-permute-start | bytes 3145736 | tf_op jit(solution)/shard_map/ppermute | solution.py:13
  137.6 55.2 %collective-permute-start.17 = (bf16[2,1,2048,128]{3,2,0,1:T(8,128)(2,1)S(1)}, bf16[2,1,2048,128]{3,2,0,1:T(8,128)(2,1)S(1)}, u32[]{:S(2)}, u32[]{:S(2)}) collective-permute-start(bf16[2,1,2048,128]{3,2,0,1:T(8,128)(2,1)S(1)} %get-tuple-element.25), channel_id=1, source_target_pairs={{0,24},{8,32},{16,40},{24,48},{32,56},{40,64},{48,72},{56,80},{64,... | collective-permute-start | bytes 3145736 | tf_op jit(solution)/shard_map/ppermute | solution.py:13
  175.5 56.1 %collective-permute-start.18 = (bf16[2,1,2048,128]{3,2,0,1:T(8,128)(2,1)}, bf16[2,1,2048,128]{3,2,0,1:T(8,128)(2,1)}, u32[]{:S(2)}, u32[]{:S(2)}) collective-permute-start(bf16[2,1,2048,128]{3,2,0,1:T(8,128)(2,1)} %get-tuple-element.36), channel_id=1, source_target_pairs={{24,0},{32,8},{40,16},{48,24},{56,32},{64,40},{72,48},{80,56},{88,... | collective-permute-start | bytes 3145736 | tf_op jit(solution)/shard_map/ppermute | solution.py:13
  179.1 73.8 %collective-permute-start.19 = (bf16[2,1,2048,128]{3,2,0,1:T(8,128)(2,1)}, bf16[2,1,2048,128]{3,2,0,1:T(8,128)(2,1)}, u32[]{:S(2)}, u32[]{:S(2)}) collective-permute-start(bf16[2,1,2048,128]{3,2,0,1:T(8,128)(2,1)} %get-tuple-element.34), channel_id=1, source_target_pairs={{16,0},{24,8},{32,16},{40,24},{48,32},{56,40},{64,48},{72,56},{80,... | collective-permute-start | bytes 3145736 | tf_op jit(solution)/shard_map/ppermute | solution.py:13
  182.6 72.5 %collective-permute-start.20 = (bf16[2,1,2048,128]{3,2,0,1:T(8,128)(2,1)}, bf16[2,1,2048,128]{3,2,0,1:T(8,128)(2,1)}, u32[]{:S(2)}, u32[]{:S(2)}) collective-permute-start(bf16[2,1,2048,128]{3,2,0,1:T(8,128)(2,1)} %get-tuple-element.32), channel_id=1, source_target_pairs={{8,0},{16,8},{24,16},{32,24},{40,32},{48,40},{56,48},{64,56},{72,6... | collective-permute-start | bytes 3145736 | tf_op jit(solution)/shard_map/ppermute | solution.py:13
  186.9 70.6 %collective-permute-start.21 = (bf16[2,1,2048,128]{3,2,0,1:T(8,128)(2,1)S(1)}, bf16[2,1,2048,128]{3,2,0,1:T(8,128)(2,1)}, u32[]{:S(2)}, u32[]{:S(2)}) collective-permute-start(bf16[2,1,2048,128]{3,2,0,1:T(8,128)(2,1)S(1)} %get-tuple-element.30), channel_id=1, source_target_pairs={{0,8},{8,16},{16,24},{24,32},{32,40},{40,48},{48,56},{56,64},{64,7... | collective-permute-start | bytes 3145736 | tf_op jit(solution)/shard_map/ppermute | solution.py:13
  192.8 66.9 %collective-permute-start.22 = (bf16[2,1,2048,128]{3,2,0,1:T(8,128)(2,1)S(1)}, bf16[2,1,2048,128]{3,2,0,1:T(8,128)(2,1)}, u32[]{:S(2)}, u32[]{:S(2)}) collective-permute-start(bf16[2,1,2048,128]{3,2,0,1:T(8,128)(2,1)S(1)} %get-tuple-element.28), channel_id=1, source_target_pairs={{0,16},{8,24},{16,32},{24,40},{32,48},{40,56},{48,64},{56,72},{64,... | collective-permute-start | bytes 3145736 | tf_op jit(solution)/shard_map/ppermute | solution.py:13
  231.6 30.6 %collective-permute-start.23 = (bf16[2,1,2048,128]{3,2,0,1:T(8,128)(2,1)}, bf16[2,1,2048,128]{3,2,0,1:T(8,128)(2,1)S(1)}, u32[]{:S(2)}, u32[]{:S(2)}) collective-permute-start(bf16[2,1,2048,128]{3,2,0,1:T(8,128)(2,1)} %get-tuple-element.26), channel_id=1, source_target_pairs={{0,24},{8,32},{16,40},{24,48},{32,56},{40,64},{48,72},{56,80},{64,... | collective-permute-start | bytes 3145736 | tf_op jit(solution)/shard_map/ppermute | solution.py:13
Sparse Core Ops, SparseCore 0:
  319.5 32.7 reduce-scatter.1
where the time goes:
time: 367 us; the launch traced here: 360 us
  starting transfers between devices  105 us (29%)
  local copies, waits for them, and re-layouts  92.7 us (25%)
  waiting for transfers between devices  75.3 us (21%)
  blocking collectives  45 us (12%)
  other arithmetic  21.4 us (6%)
  between operations  13.8 us (4%)
  matrix products  7.63 us (2%)
    ppermute x24, starting transfers between devices, from_behind(): return lax.ppermute(block, axis, route)  105 us
    all_gather x1, blocking collectives, body(): lax.all_gather(heads_out, 'beam', axis=0, tiled=True)  45 us
    ppermute x24, waiting for transfers between devices, from_behind(): return lax.ppermute(block, axis, route)  42.4 us
    reduce_scatter x1, waiting for transfers between devices, body(): lax.psum_scatter(terms, 'tensor', scatter_dimension=0, tiled=True)  32.9 us
    unnamed x33, local copies, waits for them, and re-layouts  32 us
    gather x6, local copies, waits for them, and re-layouts, body(): packed_values = jnp.take(cached_value_rows, picked_rows, axis=0)  22.2 us
    gather x6, local copies, waits for them, and re-layouts, body(): packed_keys = jnp.take(key_cache, picked_rows, axis=0)  22.2 us
    select_n x6, other arithmetic, body(): jnp.where(present_mask, packed_keys, jnp.zeros_like(packed_keys))  13.6 us
  transfers between devices with their start and end apart: 25, of which 4 were waited for; matrix products, arithmetic and copies ran while one was open for 30% of the time, Pallas kernels for 0%

commit v1 on v0

v1 whole, which is shorter than its diff:
```python
import jax
import jax.numpy as jnp
from jax import lax
from jax.experimental import pallas as pl
from jax.experimental.pallas import tpu as pltpu
from jax.sharding import Mesh
from jax.sharding import PartitionSpec as P

HEAD = 128
GROUPED = 8
SLOTS = 8
BEAMS = 32
POSITIONS = 2048
Q_COLS = GROUPED * HEAD
IN_COLS = Q_COLS + 3 * HEAD
OUT_COLS = Q_COLS + HEAD
BEAM_AXES = ("x", "y", "core")
F32 = jnp.float32
BF16 = jnp.bfloat16
VMEM = pl.BlockSpec(memory_space=pltpu.VMEM)
SMEM = pl.BlockSpec(memory_space=pltpu.SMEM)


def beam_index():
    return (lax.axis_index("x") * 4 + lax.axis_index("y")) * 2 + lax.axis_index("core")


def transposed_dot(a, b):
    return lax.dot_general(a, b, (((0,), (0,)), ((), ())), preferred_element_type=F32)


def attend_kernel(len_ref, m0, m1, m2, m3, k_ref, v_ref, out_ref, q_ref, s_ref, o_ref):
    own = beam_index()
    member = own % 4
    rows = lax.broadcasted_iota(jnp.int32, (BEAMS, HEAD), 0)
    lanes = lax.broadcasted_iota(jnp.int32, (BEAMS, HEAD), 1)
    slot_ids = ((member ^ (rows // SLOTS)) * SLOTS + rows % SLOTS).astype(F32)
    everything = jnp.concatenate([m[...].astype(F32) for m in (m0, m1, m2, m3)], axis=0)
    parents = everything[:, IN_COLS - HEAD :].astype(jnp.int32)
    local = (parents // SLOTS) == own
    before = (
        lax.broadcasted_iota(jnp.int32, (BEAMS, BEAMS), 1)
        < lax.broadcasted_iota(jnp.int32, (BEAMS, BEAMS), 0)
    )
    rank = jnp.dot(
        before.astype(F32).astype(BF16), local.astype(F32).astype(BF16), preferred_element_type=F32
    ).astype(jnp.int32)
    pick = (local & (rank == lanes)).astype(F32).astype(BF16)
    wide = jnp.concatenate([everything, slot_ids], axis=1).astype(BF16)
    chosen = transposed_dot(pick, wide)[:SLOTS]
    fresh_keys = chosen[:, Q_COLS : Q_COLS + HEAD]
    fresh_values = chosen[:, Q_COLS + HEAD : Q_COLS + 2 * HEAD]
    cache_rows = chosen[:, Q_COLS + 2 * HEAD : IN_COLS].astype(jnp.int32) - own * SLOTS
    ids = chosen[:, IN_COLS:]
    for h in range(GROUPED):
        q_ref[h * SLOTS : (h + 1) * SLOTS, :] = chosen[:, h * HEAD : (h + 1) * HEAD]
    scale = HEAD ** (-0.5)
    positions = lax.broadcasted_iota(jnp.int32, (GROUPED, POSITIONS), 1)
    picked, new_scores = [], []
    for i in range(SLOTS):
        row = jnp.clip(cache_rows[i, 0], 0, SLOTS - 1)
        picked.append(row)
        q = q_ref[pl.ds(i, GROUPED, stride=SLOTS), :]
        scores = lax.dot_general(
            q.astype(BF16), k_ref[row], (((1,), (1,)), ((), ())), preferred_element_type=F32
        ) * scale
        s_ref[i] = jnp.where(positions < len_ref[row], scores, -1e30)
        new_scores.append(jnp.sum(q * fresh_keys[i : i + 1], axis=1, keepdims=True) * scale)
    for i in range(SLOTS):
        scores = s_ref[i]
        maximum = jnp.maximum(jnp.max(scores, axis=1, keepdims=True), new_scores[i])
        weights = jnp.exp(scores - maximum)
        new_weight = jnp.exp(new_scores[i] - maximum)
        denominator = jnp.sum(weights, axis=1, keepdims=True) + new_weight
        weighted = jnp.dot(weights.astype(BF16), v_ref[picked[i]], preferred_element_type=F32)
        weighted = weighted + new_weight.astype(BF16).astype(F32) * fresh_values[i : i + 1]
        o_ref[pl.ds(i, GROUPED, stride=SLOTS), :] = weighted / denominator
    block = jnp.concatenate(
        [o_ref[h * SLOTS : (h + 1) * SLOTS, :] for h in range(GROUPED)] + [ids], axis=1
    )
    pair = jnp.concatenate([block, block], axis=0).astype(BF16)
    for j in range(8):
        out_ref[j * 16 : (j + 1) * 16, :] = pair


def project_kernel(own_ref, other_ref, w_ref, out_ref, place_ref):
    weight = w_ref[...]
    for part, ref in enumerate((own_ref, other_ref)):
        terms = jnp.dot(ref[:, :Q_COLS], weight, preferred_element_type=F32).astype(BF16)
        for g in range(8):
            out_ref[g * 32 + part * 16 : g * 32 + part * 16 + 16, :] = terms[g * 16 : g * 16 + 16]
    first = pl.multiple_of(lax.axis_index("tensor") * 16, 16)
    lanes = lax.broadcasted_iota(jnp.int32, (16, HEAD), 1)
    for part, ref in enumerate((own_ref, other_ref)):
        ids = ref[pl.ds(first, 16), Q_COLS:].astype(F32).astype(jnp.int32)
        place_ref[part * 16 : part * 16 + 16, :] = (ids == lanes).astype(F32).astype(BF16)


def finish_kernel(terms_ref, place_ref, out_ref):
    total = terms_ref[0:32, :].astype(F32)
    for z in range(1, 8):
        total = total + terms_ref[z * 32 : z * 32 + 32, :].astype(F32)
    out_ref[...] = transposed_dot(place_ref[...], total.astype(BF16))[:BEAMS].astype(BF16)


def body(parents, lengths, queries, token_keys, token_values, key_cache, value_cache, weight):
    marks = jnp.broadcast_to(parents.astype(BF16)[:, None], (SLOTS, HEAD))
    message = jnp.concatenate([queries, token_keys, token_values, marks], axis=1)
    partners = [
        lax.ppermute(message, BEAM_AXES, [(i, i ^ d) for i in range(32)]) for d in (1, 2, 3)
    ]
    heads = pl.pallas_call(
        attend_kernel,
        out_shape=jax.ShapeDtypeStruct((16 * SLOTS, OUT_COLS), BF16),
        in_specs=[SMEM] + [VMEM] * 6,
        out_specs=VMEM,
        scratch_shapes=[
            pltpu.VMEM((GROUPED * SLOTS, HEAD), F32),
            pltpu.VMEM((SLOTS, GROUPED, POSITIONS), F32),
            pltpu.VMEM((GROUPED * SLOTS, HEAD), F32),
        ],
        compiler_params=pltpu.CompilerParams(vmem_limit_bytes=24 * 1024 * 1024),
        cost_estimate=pl.CostEstimate(
            flops=2 * 2 * 64 * 2048 * 128, bytes_accessed=9 * 2**20, transcendentals=64 * 2048
        ),
        name="attend",
    )(
        lengths,
        message,
        *partners,
        key_cache.reshape(SLOTS, POSITIONS, HEAD),
        value_cache.reshape(SLOTS, POSITIONS, HEAD),
    )
    gathered = lax.all_to_all(heads, ("x", "y"), 0, 0, tiled=True)
    other = lax.ppermute(gathered, BEAM_AXES, [(i, i ^ 1) for i in range(32)])
    terms, place = pl.pallas_call(
        project_kernel,
        out_shape=(
            jax.ShapeDtypeStruct((256, 256), BF16),
            jax.ShapeDtypeStruct((BEAMS, HEAD), BF16),
        ),
        in_specs=[VMEM] * 3,
        out_specs=(VMEM, VMEM),
        compiler_params=pltpu.CompilerParams(vmem_limit_bytes=16 * 1024 * 1024),
        name="project",
    )(gathered, other, weight)
    shares = lax.all_to_all(terms, "tensor", 0, 0, tiled=True)
    return pl.pallas_call(
        finish_kernel,
        out_shape=jax.ShapeDtypeStruct((BEAMS, 256), BF16),
        in_specs=[VMEM] * 2,
        out_specs=VMEM,
        compiler_params=pltpu.CompilerParams(vmem_limit_bytes=16 * 1024 * 1024),
        name="finish",
    )(shares, place)


def solution(mesh):
    fine = Mesh(mesh.devices.reshape(4, 4, 2, 8), ("x", "y", "core", "tensor"))
    in_specs = (
        P(BEAM_AXES),
        P(BEAM_AXES),
        P(BEAM_AXES, "tensor"),
        P(BEAM_AXES, "tensor"),
        P(BEAM_AXES, "tensor"),
        P(BEAM_AXES, "tensor", None, None),
        P(BEAM_AXES, "tensor", None, None),
        P("tensor", BEAM_AXES),
    )
    out_specs = P("tensor", BEAM_AXES)
    return jax.shard_map(body, mesh=fine, in_specs=in_specs, out_specs=out_specs, check_vma=False)
```

time: 367 us -> 49.3 us (0.13); the launches traced: 360 us -> 49 us
  starting transfers between devices: 105 us -> 6.89 us
  local copies, waits for them, and re-layouts: 92.7 us -> 5.11 us
  waiting for transfers between devices: 75.3 us -> 2.69 us
  other arithmetic: 21.4 us -> 1.41 us
  blocking collectives: 45 us -> 29 us
  between operations: 13.8 us -> 0.03 us
  matrix products: 7.63 us -> 0 us
  Pallas kernels: 0 us -> 3.86 us
    ppermute x24 -> x4, starting transfers between devices: 105 us -> 6.89 us  [the longest x3 4.59 us: body(): lax.ppermute(message, BEAM_AXES, [(i, i ^ d) for i in range(32)])]
    gather x14 -> x0, local copies, waits for them, and re-layouts: 58.6 us -> none  [the longest x6 22.2 us: body(): packed_values = jnp.take(cached_value_rows, picked_rows, axis=0)]
    all_gather x1 -> x0, blocking collectives: 45 us -> none  [body(): lax.all_gather(heads_out, 'beam', axis=0, tiled=True)]
    ppermute x24 -> x4, waiting for transfers between devices: 42.4 us -> 2.69 us  [the longest x3 1.48 us: body(): lax.ppermute(message, BEAM_AXES, [(i, i ^ d) for i in range(32)])]
    reduce_scatter x1 -> x0, waiting for transfers between devices: 32.9 us -> none  [body(): lax.psum_scatter(terms, 'tensor', scatter_dimension=0, tiled=True)]
    all_to_all x0 -> x2, blocking collectives: none -> 29 us  [the longest x1 15.9 us: body(): shares = lax.all_to_all(terms, 'tensor', 0, 0, tiled=True)]
    unnamed x33 -> x8, local copies, waits for them, and re-layouts: 32 us -> 5.03 us
    select_n x18 -> x0, other arithmetic: 13.7 us -> none  [the longest x6 13.6 us: body(): jnp.where(present_mask, packed_keys, jnp.zeros_like(packed_keys))]
  transfers between devices with their start and end apart: 25 -> 4, of which waited for: 4 -> 2; matrix products, arithmetic and copies ran while one was open for 30% -> 0% of each run, Pallas kernels for 0% -> 0%
where the time goes in v1:
time: 49.3 us; the launch traced here: 49 us
  blocking collectives  29 us (59%)
  starting transfers between devices  6.89 us (14%)
  local copies, waits for them, and re-layouts  5.11 us (10%)
  Pallas kernels  3.86 us (8%)
  waiting for transfers between devices  2.69 us (5%)
  other arithmetic  1.41 us (3%)
    all_to_all x1, blocking collectives, body(): shares = lax.all_to_all(terms, 'tensor', 0, 0, tiled=True)  15.9 us
    all_to_all x1, blocking collectives, body(): gathered = lax.all_to_all(heads, ('x', 'y'), 0, 0, tiled=True)  13.2 us
    unnamed x8, local copies, waits for them, and re-layouts  5.03 us
    ppermute x3, starting transfers between devices, body(): lax.ppermute(message, BEAM_AXES, [(i, i ^ d) for i in range(32)])  4.59 us
    pallas_call x1, Pallas kernels, body(): pl.pallas_call(attend_kernel, out_shape=jax.ShapeDtypeStruct((16 * SLOTS,...  2.76 us
    ppermute x1, starting transfers between devices, body(): other = lax.ppermute(gathered, BEAM_AXES, [(i, i ^ 1) for i in range(32)])  2.3 us
    ppermute x3, waiting for transfers between devices, body(): lax.ppermute(message, BEAM_AXES, [(i, i ^ d) for i in range(32)])  1.48 us
    ppermute x1, waiting for transfers between devices, body(): other = lax.ppermute(gathered, BEAM_AXES, [(i, i ^ 1) for i in range(32)])  1.21 us
  transfers between devices with their start and end apart: 4, of which 2 were waited for; matrix products, arithmetic and copies ran while one was open for 0% of the time, Pallas kernels for 0%

profile of v1, /device:TPU:1, one launch (start us, length us, event | category | flops | bytes accessed | tf_op | source)
XLA Modules:
  0.0 49.0 jit_solution(8279830719437271309)
XLA Ops:
  0.0 0.7 %convert_element_type.3 = bf16[8]{0:T(256)(128)(2,1)S(1)} convert(s32[8]{0:T(128)} %param.8) | non-fusion elementwise | flops 8 | bytes 48 | tf_op jit(solution)/shard_map/convert_element_type | solution.py:107
  0.7 0.1 broadcast_in_dim.2
  0.7 0.8 %pad_maximum_fusion.m0 = bf16[8,1408]{1,0:T(8,128)(2,1)S(1)} fusion(bf16[8,128]{1,0:T(8,128)(2,1)S(1)} %broadcast_in_dim.2, bf16[8,128]{1,0:T(8,128)(2,1)} %param.12, bf16[8,128]{1,0:T(8,128)(2,1)} %param.11, bf16[8,1024]{1,0:T(8,128)(2,1)} %param.10), kind=kLoop, calls=%fused_computation | loop fusion | flops 90112 | bytes 45056 | tf_op jit(solution)/shard_map/concatenate | solution.py:108
  1.5 2.7 %collective-permute-start.2 = (bf16[8,1408]{1,0:T(8,128)(2,1)S(1)}, bf16[8,1408]{1,0:T(8,128)(2,1)S(1)}, u32[]{:S(2)}, u32[]{:S(2)}) collective-permute-start(bf16[8,1408]{1,0:T(8,128)(2,1)S(1)} %pad_maximum_fusion.m0), channel_id=1, source_target_pairs={{0,24},{8,16},{16,8},{24,0},{32,56},{40,48},{48,40},{56,32},{64,88... | collective-permute-start | bytes 67592 | tf_op jit(solution)/shard_map/ppermute | solution.py:110
  4.2 1.9 %collective-permute-start.1 = (bf16[8,1408]{1,0:T(8,128)(2,1)S(1)}, bf16[8,1408]{1,0:T(8,128)(2,1)S(1)}, u32[]{:S(2)}, u32[]{:S(2)}) collective-permute-start(bf16[8,1408]{1,0:T(8,128)(2,1)S(1)} %pad_maximum_fusion.m0), channel_id=1, source_target_pairs={{0,16},{8,24},{16,0},{24,8},{32,48},{40,56},{48,32},{56,40},{64,80... | collective-permute-start | bytes 67592 | tf_op jit(solution)/shard_map/ppermute | solution.py:110
  6.1 0.0 collective-permute-start
  6.1 0.0 collective-permute-done.2.m3
  6.1 1.5 %collective-permute-done.1.m2 = bf16[8,1408]{1,0:T(8,128)(2,1)S(1)} collective-permute-done((bf16[8,1408]{1,0:T(8,128)(2,1)S(1)}, bf16[8,1408]{1,0:T(8,128)(2,1)S(1)}, u32[]{:S(2)}, u32[]{:S(2)}) %collective-permute-start.1) | collective-permute-done | bytes 22560 | tf_op jit(solution)/shard_map/ppermute | solution.py:110
  7.6 0.0 collective-permute-done.m1
  7.6 0.0 copy-start
  7.6 2.2 %copy-done = bf16[8,1,2048,128]{3,2,1,0:T(8,128)(2,1)S(1)} copy-done((bf16[8,1,2048,128]{3,2,1,0:T(8,128)(2,1)S(1)}, bf16[8,1,2048,128]{3,2,1,0:T(8,128)(2,1)}, u32[]{:S(2)}) %copy-start) | copy-done | bytes 4194328
  9.8 0.0 copy-start.1
  9.8 2.2 %copy-done.1 = bf16[8,1,2048,128]{3,2,1,0:T(8,128)(2,1)S(1)} copy-done((bf16[8,1,2048,128]{3,2,1,0:T(8,128)(2,1)S(1)}, bf16[8,1,2048,128]{3,2,1,0:T(8,128)(2,1)}, u32[]{:S(2)}) %copy-start.1) | copy-done | bytes 4194328
  11.9 0.0 copy-start.3
  11.9 0.7 %copy-done.3 = s32[8]{0:T(128)S(1)} copy-done((s32[8]{0:T(128)S(1)}, s32[8]{0:T(128)}, u32[]{:S(2)}) %copy-start.3) | copy-done | bytes 56
  12.6 0.0 copy-start.2
  12.6 2.8 %attend.1 = bf16[128,1152]{1,0:T(8,128)(2,1)S(1)} custom-call(s32[8]{0:T(128)S(1)} %copy-done.3, bf16[8,1408]{1,0:T(8,128)(2,1)S(1)} %pad_maximum_fusion.m0, bf16[8,1408]{1,0:T(8,128)(2,1)S(1)} %collective-permute-done.m1, bf16[8,1408]{1,0:T(8,128)(2,1)S(1)} %collective-permute-done.1.m2, bf16[8,1408]{1,0:T(8,128)(2,1)S(1)} %collective-permute-done.2.m3, ...), custom_call_target="tpu_custom_call" | custom-call | flops 67108864 | bytes 9437184 | tf_op jit(solution)/shard_map/attend/pallas_call | solution.py:112
  15.4 13.2 %all_to_all.22 = bf16[16,8,1152]{2,1,0:T(8,128)(2,1)S(1)} all-to-all(bf16[16,8,1152]{2,1,0:T(8,128)(2,1)S(1)} %bitcast.8), channel_id=1, replica_groups=mesh['x'=4,'y'=4,'core'=2,'tensor'=8] {'x','y'}, dimensions={0} | all-to-all | bytes 589824 | tf_op jit(solution)/shard_map/all_to_all | solution.py:134
  28.5 2.3 %collective-permute-start.3 = (bf16[128,1152]{1,0:T(8,128)(2,1)S(1)}, bf16[128,1152]{1,0:T(8,128)(2,1)S(1)}, u32[]{:S(2)}, u32[]{:S(2)}) collective-permute-start(bf16[128,1152]{1,0:T(8,128)(2,1)S(1)} %bitcast.9), channel_id=1, source_target_pairs={{0,8},{8,0},{16,24},{24,16},{32,40},{40,32},{48,56},{56,48},{64,72... | collective-permute-start | bytes 884744 | tf_op jit(solution)/shard_map/ppermute | solution.py:135
  30.8 1.2 %collective-permute-done.3.other_ref = bf16[128,1152]{1,0:T(8,128)(2,1)S(1)} collective-permute-done((bf16[128,1152]{1,0:T(8,128)(2,1)S(1)}, bf16[128,1152]{1,0:T(8,128)(2,1)S(1)}, u32[]{:S(2)}, u32[]{:S(2)}) %collective-permute-start.3) | collective-permute-done | bytes 294944 | tf_op jit(solution)/shard_map/ppermute | solution.py:135
  32.0 0.0 copy-done.2
  32.0 0.3 project.1
  32.4 15.9 %all_to_all.23 = bf16[8,32,256]{2,1,0:T(8,128)(2,1)S(1)} all-to-all(bf16[8,32,256]{2,1,0:T(8,128)(2,1)S(1)} %bitcast.12), channel_id=1, replica_groups=mesh['x'=4,'y'=4,'core'=2,'tensor'=8] {'tensor'}, dimensions={0} | all-to-all | bytes 262144 | tf_op jit(solution)/shard_map/all_to_all | solution.py:147
  48.2 0.8 %finish.1 = bf16[32,256]{1,0:T(8,128)(2,1)} custom-call(bf16[256,256]{1,0:T(8,128)(2,1)S(1)} %bitcast.11, bf16[32,128]{1,0:T(8,128)(2,1)S(1)} %get-tuple-element.8.place_ref), custom_call_target="tpu_custom_call" | custom-call | tf_op jit(solution)/shard_map/finish/pallas_call | solution.py:148
Async XLA Ops:
  1.5 4.6 %collective-permute-start.2 = (bf16[8,1408]{1,0:T(8,128)(2,1)S(1)}, bf16[8,1408]{1,0:T(8,128)(2,1)S(1)}, u32[]{:S(2)}, u32[]{:S(2)}) collective-permute-start(bf16[8,1408]{1,0:T(8,128)(2,1)S(1)} %pad_maximum_fusion.m0), channel_id=1, source_target_pairs={{0,24},{8,16},{16,8},{24,0},{32,56},{40,48},{48,40},{56,32},{64,88... | collective-permute-start | bytes 67592 | tf_op jit(solution)/shard_map/ppermute | solution.py:110
  4.2 3.4 %collective-permute-start.1 = (bf16[8,1408]{1,0:T(8,128)(2,1)S(1)}, bf16[8,1408]{1,0:T(8,128)(2,1)S(1)}, u32[]{:S(2)}, u32[]{:S(2)}) collective-permute-start(bf16[8,1408]{1,0:T(8,128)(2,1)S(1)} %pad_maximum_fusion.m0), channel_id=1, source_target_pairs={{0,16},{8,24},{16,0},{24,8},{32,48},{40,56},{48,32},{56,40},{64,80... | collective-permute-start | bytes 67592 | tf_op jit(solution)/shard_map/ppermute | solution.py:110
  6.1 1.5 %collective-permute-start = (bf16[8,1408]{1,0:T(8,128)(2,1)S(1)}, bf16[8,1408]{1,0:T(8,128)(2,1)S(1)}, u32[]{:S(2)}, u32[]{:S(2)}) collective-permute-start(bf16[8,1408]{1,0:T(8,128)(2,1)S(1)} %pad_maximum_fusion.m0), channel_id=1, source_target_pairs={{0,8},{8,0},{16,24},{24,16},{32,40},{40,32},{48,56},{56,48},{64,72... | collective-permute-start | bytes 67592 | tf_op jit(solution)/shard_map/ppermute | solution.py:110
  7.6 2.2 %copy-start = (bf16[8,1,2048,128]{3,2,1,0:T(8,128)(2,1)S(1)}, bf16[8,1,2048,128]{3,2,1,0:T(8,128)(2,1)}, u32[]{:S(2)}) copy-start(bf16[8,1,2048,128]{3,2,1,0:T(8,128)(2,1)} %param.13) | copy-start | bytes 12582916
  9.8 2.2 %copy-start.1 = (bf16[8,1,2048,128]{3,2,1,0:T(8,128)(2,1)S(1)}, bf16[8,1,2048,128]{3,2,1,0:T(8,128)(2,1)}, u32[]{:S(2)}) copy-start(bf16[8,1,2048,128]{3,2,1,0:T(8,128)(2,1)} %param.14) | copy-start | bytes 12582916
  11.9 0.7 %copy-start.3 = (s32[8]{0:T(128)S(1)}, s32[8]{0:T(128)}, u32[]{:S(2)}) copy-start(s32[8]{0:T(128)} %len_ref.1) | copy-start | bytes 100
  12.6 19.4 %copy-start.2 = (bf16[1024,256]{1,0:T(8,128)(2,1)S(1)}, bf16[1024,256]{1,0:T(8,128)(2,1)}, u32[]{:S(2)}) copy-start(bf16[1024,256]{1,0:T(8,128)(2,1)} %w_ref.1) | copy-start | bytes 1572868
  28.5 3.5 %collective-permute-start.3 = (bf16[128,1152]{1,0:T(8,128)(2,1)S(1)}, bf16[128,1152]{1,0:T(8,128)(2,1)S(1)}, u32[]{:S(2)}, u32[]{:S(2)}) collective-permute-start(bf16[128,1152]{1,0:T(8,128)(2,1)S(1)} %bitcast.9), channel_id=1, source_target_pairs={{0,8},{8,0},{16,24},{24,16},{32,40},{40,32},{48,56},{56,48},{64,72... | collective-permute-start | bytes 884744 | tf_op jit(solution)/shard_map/ppermute | solution.py:135

commit v2 on v1

--- a/solution.py
+++ b/solution.py
@@ -18,7 +18,11 @@
 F32 = jnp.float32
 BF16 = jnp.bfloat16
 VMEM = pl.BlockSpec(memory_space=pltpu.VMEM)
-SMEM = pl.BlockSpec(memory_space=pltpu.SMEM)
+HBM = pl.BlockSpec(memory_space=pltpu.HBM)
+
+
+def in_hbm(x):
+    return pltpu.with_memory_space_constraint(x, pltpu.HBM)
 
 
 def beam_index():
@@ -27,6 +31,43 @@
 
 def transposed_dot(a, b):
     return lax.dot_general(a, b, (((0,), (0,)), ((), ())), preferred_element_type=F32)
+
+
+def pack_kernel(parent_hbm, q_hbm, key_hbm, value_hbm, out_ref, parent_ref, sems):
+    copies = [pltpu.make_async_copy(parent_hbm, parent_ref, sems.at[0])]
+    start = 0
+    for n, ref in enumerate((q_hbm, key_hbm, value_hbm)):
+        columns = out_ref.at[:, start : start + ref.shape[1]]
+        copies.append(pltpu.make_async_copy(ref, columns, sems.at[n + 1]))
+        start += ref.shape[1]
+    for copy in copies:
+        copy.start()
+    rows = lax.broadcasted_iota(jnp.int32, (SLOTS, HEAD), 0)
+    marks = jnp.zeros((SLOTS, HEAD), jnp.int32)
+    copies[0].wait()
+    for i in range(SLOTS):
+        marks = jnp.where(rows == i, parent_ref[i], marks)
+    out_ref[:, start:] = marks.astype(F32).astype(BF16)
+    for copy in copies[1:]:
+        copy.wait()
+
+
+def load_kernel(after_ref, len_hbm, k_hbm, v_hbm, k_out, v_out, len_out, len_ref, sems):
+    copies = [
+        pltpu.make_async_copy(len_hbm, len_ref, sems.at[0]),
+        pltpu.make_async_copy(k_hbm, k_out, sems.at[1]),
+        pltpu.make_async_copy(v_hbm, v_out, sems.at[2]),
+    ]
+    for copy in copies:
+        copy.start()
+    rows = lax.broadcasted_iota(jnp.int32, (SLOTS, HEAD), 0)
+    spread = jnp.zeros((SLOTS, HEAD), jnp.int32)
+    copies[0].wait()
+    for i in range(SLOTS):
+        spread = jnp.where(rows == i, len_ref[i], spread)
+    len_out[...] = spread
+    for copy in copies[1:]:
+        copy.wait()
 
 
 def attend_kernel(len_ref, m0, m1, m2, m3, k_ref, v_ref, out_ref, q_ref, s_ref, o_ref):
@@ -52,6 +93,9 @@
     fresh_values = chosen[:, Q_COLS + HEAD : Q_COLS + 2 * HEAD]
     cache_rows = chosen[:, Q_COLS + 2 * HEAD : IN_COLS].astype(jnp.int32) - own * SLOTS
     ids = chosen[:, IN_COLS:]
+    limits = jnp.zeros((SLOTS, HEAD), jnp.int32)
+    for r in range(SLOTS):
+        limits = jnp.where(cache_rows == r, len_ref[r : r + 1, :], limits)
     for h in range(GROUPED):
         q_ref[h * SLOTS : (h + 1) * SLOTS, :] = chosen[:, h * HEAD : (h + 1) * HEAD]
     scale = HEAD ** (-0.5)
@@ -64,7 +108,7 @@
         scores = lax.dot_general(
             q.astype(BF16), k_ref[row], (((1,), (1,)), ((), ())), preferred_element_type=F32
         ) * scale
-        s_ref[i] = jnp.where(positions < len_ref[row], scores, -1e30)
+        s_ref[i] = jnp.where(positions < limits[i : i + 1, :1], scores, -1e30)
         new_scores.append(jnp.sum(q * fresh_keys[i : i + 1], axis=1, keepdims=True) * scale)
     for i in range(SLOTS):
         scores = s_ref[i]
@@ -104,15 +148,37 @@
 
 
 def body(parents, lengths, queries, token_keys, token_values, key_cache, value_cache, weight):
-    marks = jnp.broadcast_to(parents.astype(BF16)[:, None], (SLOTS, HEAD))
-    message = jnp.concatenate([queries, token_keys, token_values, marks], axis=1)
+    message = pl.pallas_call(
+        pack_kernel,
+        out_shape=pltpu.VMEM((SLOTS, IN_COLS), BF16),
+        in_specs=[HBM] * 4,
+        out_specs=VMEM,
+        scratch_shapes=[pltpu.SMEM((SLOTS,), jnp.int32), pltpu.SemaphoreType.DMA((4,))],
+        name="pack",
+    )(*[in_hbm(x) for x in (parents, queries, token_keys, token_values)])
     partners = [
         lax.ppermute(message, BEAM_AXES, [(i, i ^ d) for i in range(32)]) for d in (1, 2, 3)
     ]
+    cache = pltpu.VMEM((SLOTS, POSITIONS, HEAD), BF16)
+    keys, values, limits = pl.pallas_call(
+        load_kernel,
+        out_shape=(cache, cache, pltpu.VMEM((SLOTS, HEAD), jnp.int32)),
+        in_specs=[VMEM] + [HBM] * 3,
+        out_specs=(VMEM, VMEM, VMEM),
+        scratch_shapes=[pltpu.SMEM((SLOTS,), jnp.int32), pltpu.SemaphoreType.DMA((3,))],
+        compiler_params=pltpu.CompilerParams(vmem_limit_bytes=8 * 1024 * 1024),
+        cost_estimate=pl.CostEstimate(flops=0, bytes_accessed=16 * 2**20, transcendentals=0),
+        name="load",
+    )(
+        message,
+        in_hbm(lengths),
+        in_hbm(key_cache.reshape(SLOTS, POSITIONS, HEAD)),
+        in_hbm(value_cache.reshape(SLOTS, POSITIONS, HEAD)),
+    )
     heads = pl.pallas_call(
         attend_kernel,
         out_shape=jax.ShapeDtypeStruct((16 * SLOTS, OUT_COLS), BF16),
-        in_specs=[SMEM] + [VMEM] * 6,
+        in_specs=[VMEM] * 7,
         out_specs=VMEM,
         scratch_shapes=[
             pltpu.VMEM((GROUPED * SLOTS, HEAD), F32),
@@ -125,11 +191,11 @@
         ),
         name="attend",
     )(
-        lengths,
+        limits,
         message,
         *partners,
-        key_cache.reshape(SLOTS, POSITIONS, HEAD),
-        value_cache.reshape(SLOTS, POSITIONS, HEAD),
+        keys,
+        values,
     )
     gathered = lax.all_to_all(heads, ("x", "y"), 0, 0, tiled=True)
     other = lax.ppermute(gathered, BEAM_AXES, [(i, i ^ 1) for i in range(32)])

time: 49.3 us -> 44.3 us (0.90)
  local copies, waits for them, and re-layouts: 5.11 us -> 0.01 us
  Pallas kernels: 3.86 us -> 7.57 us
  waiting for transfers between devices: 2.69 us -> 1.22 us
  other arithmetic: 1.41 us -> 0 us
  blocking collectives: 29 us -> 28.5 us
    unnamed x8 -> x2, local copies, waits for them, and re-layouts: 5.03 us -> 0.01 us
    pallas_call x0 -> x2, Pallas kernels: none -> 4.25 us  [the longest x1 3.49 us: body(): pl.pallas_call(load_kernel, out_shape=(cache, cache, pltpu.VMEM((SLOTS, H...]
    ppermute x3, waiting for transfers between devices: 1.48 us -> 0.01 us  [body(): lax.ppermute(message, BEAM_AXES, [(i, i ^ d) for i in range(32)])]
    concatenate x1 -> x0, other arithmetic: 0.75 us -> none  [body(): jnp.concatenate([queries, token_keys, token_values, marks], axis=1)]
    convert_element_type x1 -> x0, other arithmetic: 0.66 us -> none  [body(): marks = jnp.broadcast_to(parents.astype(BF16)[:, None], (SLOTS, HEAD))]
    pallas_call x1, Pallas kernels: 2.76 us -> 2.22 us  [body(): pl.pallas_call(attend_kernel, out_shape=jax.ShapeDtypeStruct((16 * SLOTS,...]
  transfers between devices with their start and end apart: 4 -> 4, of which waited for: 2 -> 1; matrix products, arithmetic and copies ran while one was open for 0% -> 0% of each run, Pallas kernels for 0% -> 8%
where the time goes in v2:
time: 44.3 us; the launch traced here: 44.1 us
  blocking collectives  28.5 us (64%)
  Pallas kernels  7.57 us (17%)
  starting transfers between devices  6.73 us (15%)
  waiting for transfers between devices  1.22 us (3%)
    all_to_all x1, blocking collectives, body(): shares = lax.all_to_all(terms, 'tensor', 0, 0, tiled=True)  15.9 us
    all_to_all x1, blocking collectives, body(): gathered = lax.all_to_all(heads, ('x', 'y'), 0, 0, tiled=True)  12.7 us
    ppermute x3, starting transfers between devices, body(): lax.ppermute(message, BEAM_AXES, [(i, i ^ d) for i in range(32)])  4.68 us
    pallas_call x1, Pallas kernels, body(): pl.pallas_call(load_kernel, out_shape=(cache, cache, pltpu.VMEM((SLOTS, H...  3.49 us
    pallas_call x1, Pallas kernels, body(): pl.pallas_call(attend_kernel, out_shape=jax.ShapeDtypeStruct((16 * SLOTS,...  2.22 us
    ppermute x1, starting transfers between devices, body(): other = lax.ppermute(gathered, BEAM_AXES, [(i, i ^ 1) for i in range(32)])  2.05 us
    ppermute x1, waiting for transfers between devices, body(): other = lax.ppermute(gathered, BEAM_AXES, [(i, i ^ 1) for i in range(32)])  1.21 us
  transfers between devices with their start and end apart: 4, of which 1 were waited for; matrix products, arithmetic and copies ran while one was open for 0% of the time, Pallas kernels for 8%

profile of v2, /device:TPU:1, one launch (start us, length us, event | category | flops | bytes accessed | tf_op | source)
XLA Modules:
  0.0 44.1 jit_solution(3607445627900828814)
XLA Ops:
  0.0 0.8 %pack.1.after_ref.m0 = bf16[8,1408]{1,0:T(8,128)(2,1)S(1)} custom-call(s32[8]{0:T(128)} %parent_hbm.1, bf16[8,1024]{1,0:T(8,128)(2,1)} %q_hbm.1, bf16[8,128]{1,0:T(8,128)(2,1)} %key_hbm.1, bf16[8,128]{1,0:T(8,128)(2,1)} %value_hbm.1), custom_call_target="tpu_custom_call" | custom-call | tf_op jit(solution)/shard_map/pack/pallas_call | solution.py:151
  0.8 2.8 %collective-permute-start.2 = (bf16[8,1408]{1,0:T(8,128)(2,1)S(1)}, bf16[8,1408]{1,0:T(8,128)(2,1)S(1)}, u32[]{:S(2)}, u32[]{:S(2)}) collective-permute-start(bf16[8,1408]{1,0:T(8,128)(2,1)S(1)} %pack.1.after_ref.m0), channel_id=1, source_target_pairs={{0,24},{8,16},{16,8},{24,0},{32,56},{40,48},{48,40},{56,32},{64,88... | collective-permute-start | bytes 67592 | tf_op jit(solution)/shard_map/ppermute | solution.py:160
  3.5 1.9 %collective-permute-start.1 = (bf16[8,1408]{1,0:T(8,128)(2,1)S(1)}, bf16[8,1408]{1,0:T(8,128)(2,1)S(1)}, u32[]{:S(2)}, u32[]{:S(2)}) collective-permute-start(bf16[8,1408]{1,0:T(8,128)(2,1)S(1)} %pack.1.after_ref.m0), channel_id=1, source_target_pairs={{0,16},{8,24},{16,0},{24,8},{32,48},{40,56},{48,32},{56,40},{64,80... | collective-permute-start | bytes 67592 | tf_op jit(solution)/shard_map/ppermute | solution.py:160
  5.4 0.0 collective-permute-start
  5.4 3.5 %load.1 = (bf16[8,2048,128]{2,1,0:T(8,128)(2,1)S(1)}, bf16[8,2048,128]{2,1,0:T(8,128)(2,1)S(1)}, s32[8,128]{1,0:T(8,128)S(1)}) custom-call(bf16[8,1408]{1,0:T(8,128)(2,1)S(1)} %pack.1.after_ref.m0, s32[8]{0:T(128)} %len_hbm.1, bf16[8,2048,128]{2,1,0:T(8,128)(2,1)} %bitcast.11, bf16[8,2048,128]{2,1,0:T(8,128)(2,1)} %bitcast.12), custom_call_target="tpu_custom_call" | custom-call | bytes 16777216 | tf_op jit(solution)/shard_map/load/pallas_call | solution.py:163
  8.9 0.0 collective-permute-done.2.m3
  9.0 0.0 collective-permute-done.1.m2
  9.0 0.0 collective-permute-done.m1
  9.0 0.0 copy-start
  9.0 2.2 %attend.1 = bf16[128,1152]{1,0:T(8,128)(2,1)S(1)} custom-call(s32[8,128]{1,0:T(8,128)S(1)} %get-tuple-element.10.len_ref, bf16[8,1408]{1,0:T(8,128)(2,1)S(1)} %pack.1.after_ref.m0, bf16[8,1408]{1,0:T(8,128)(2,1)S(1)} %collective-permute-done.m1, bf16[8,1408]{1,0:T(8,128)(2,1)S(1)} %collective-permute-done.1.m2, ...), custom_call_target="tpu_custom_call" | custom-call | flops 67108864 | bytes 9437184 | tf_op jit(solution)/shard_map/attend/pallas_call | solution.py:178
  11.2 12.7 %all_to_all.22 = bf16[16,8,1152]{2,1,0:T(8,128)(2,1)S(1)} all-to-all(bf16[16,8,1152]{2,1,0:T(8,128)(2,1)S(1)} %bitcast.6), channel_id=1, replica_groups=mesh['x'=4,'y'=4,'core'=2,'tensor'=8] {'x','y'}, dimensions={0} | all-to-all | bytes 589824 | tf_op jit(solution)/shard_map/all_to_all | solution.py:200
  23.9 2.0 %collective-permute-start.3 = (bf16[128,1152]{1,0:T(8,128)(2,1)S(1)}, bf16[128,1152]{1,0:T(8,128)(2,1)S(1)}, u32[]{:S(2)}, u32[]{:S(2)}) collective-permute-start(bf16[128,1152]{1,0:T(8,128)(2,1)S(1)} %bitcast.7), channel_id=1, source_target_pairs={{0,8},{8,0},{16,24},{24,16},{32,40},{40,32},{48,56},{56,48},{64,72... | collective-permute-start | bytes 884744 | tf_op jit(solution)/shard_map/ppermute | solution.py:201
  25.9 1.2 %collective-permute-done.3.other_ref = bf16[128,1152]{1,0:T(8,128)(2,1)S(1)} collective-permute-done((bf16[128,1152]{1,0:T(8,128)(2,1)S(1)}, bf16[128,1152]{1,0:T(8,128)(2,1)S(1)}, u32[]{:S(2)}, u32[]{:S(2)}) %collective-permute-start.3) | collective-permute-done | bytes 294944 | tf_op jit(solution)/shard_map/ppermute | solution.py:201
  27.2 0.0 copy-done
  27.2 0.3 project.1
  27.5 15.9 %all_to_all.23 = bf16[8,32,256]{2,1,0:T(8,128)(2,1)S(1)} all-to-all(bf16[8,32,256]{2,1,0:T(8,128)(2,1)S(1)} %bitcast.10), channel_id=1, replica_groups=mesh['x'=4,'y'=4,'core'=2,'tensor'=8] {'tensor'}, dimensions={0} | all-to-all | bytes 262144 | tf_op jit(solution)/shard_map/all_to_all | solution.py:213
  43.3 0.8 %finish.1 = bf16[32,256]{1,0:T(8,128)(2,1)} custom-call(bf16[256,256]{1,0:T(8,128)(2,1)S(1)} %bitcast.9, bf16[32,128]{1,0:T(8,128)(2,1)S(1)} %get-tuple-element.14.place_ref), custom_call_target="tpu_custom_call" | custom-call | tf_op jit(solution)/shard_map/finish/pallas_call | solution.py:214
Async XLA Ops:
  0.8 8.2 %collective-permute-start.2 = (bf16[8,1408]{1,0:T(8,128)(2,1)S(1)}, bf16[8,1408]{1,0:T(8,128)(2,1)S(1)}, u32[]{:S(2)}, u32[]{:S(2)}) collective-permute-start(bf16[8,1408]{1,0:T(8,128)(2,1)S(1)} %pack.1.after_ref.m0), channel_id=1, source_target_pairs={{0,24},{8,16},{16,8},{24,0},{32,56},{40,48},{48,40},{56,32},{64,88... | collective-permute-start | bytes 67592 | tf_op jit(solution)/shard_map/ppermute | solution.py:160
  3.5 5.4 %collective-permute-start.1 = (bf16[8,1408]{1,0:T(8,128)(2,1)S(1)}, bf16[8,1408]{1,0:T(8,128)(2,1)S(1)}, u32[]{:S(2)}, u32[]{:S(2)}) collective-permute-start(bf16[8,1408]{1,0:T(8,128)(2,1)S(1)} %pack.1.after_ref.m0), channel_id=1, source_target_pairs={{0,16},{8,24},{16,0},{24,8},{32,48},{40,56},{48,32},{56,40},{64,80... | collective-permute-start | bytes 67592 | tf_op jit(solution)/shard_map/ppermute | solution.py:160
  5.4 3.5 %collective-permute-start = (bf16[8,1408]{1,0:T(8,128)(2,1)S(1)}, bf16[8,1408]{1,0:T(8,128)(2,1)S(1)}, u32[]{:S(2)}, u32[]{:S(2)}) collective-permute-start(bf16[8,1408]{1,0:T(8,128)(2,1)S(1)} %pack.1.after_ref.m0), channel_id=1, source_target_pairs={{0,8},{8,0},{16,24},{24,16},{32,40},{40,32},{48,56},{56,48},{64,72... | collective-permute-start | bytes 67592 | tf_op jit(solution)/shard_map/ppermute | solution.py:160
  9.0 18.2 %copy-start = (bf16[1024,256]{1,0:T(8,128)(2,1)S(1)}, bf16[1024,256]{1,0:T(8,128)(2,1)}, u32[]{:S(2)}) copy-start(bf16[1024,256]{1,0:T(8,128)(2,1)} %w_ref.1) | copy-start | bytes 1572868
  23.9 3.3 %collective-permute-start.3 = (bf16[128,1152]{1,0:T(8,128)(2,1)S(1)}, bf16[128,1152]{1,0:T(8,128)(2,1)S(1)}, u32[]{:S(2)}, u32[]{:S(2)}) collective-permute-start(bf16[128,1152]{1,0:T(8,128)(2,1)S(1)} %bitcast.7), channel_id=1, source_target_pairs={{0,8},{8,0},{16,24},{24,16},{32,40},{40,32},{48,56},{56,48},{64,72... | collective-permute-start | bytes 884744 | tf_op jit(solution)/shard_map/ppermute | solution.py:201

commit v3 on v1

v3 whole, which is shorter than its diff:
```python
import jax
import jax.numpy as jnp
from jax import lax
from jax.experimental import pallas as pl
from jax.experimental.pallas import tpu as pltpu
from jax.sharding import Mesh
from jax.sharding import PartitionSpec as P

HEAD = 128
GROUPED = 8
SLOTS = 8
BEAMS = 32
POSITIONS = 2048
Q_COLS = GROUPED * HEAD
OUT_COLS = Q_COLS + HEAD
PACKED = 32
BEAM_AXES = ("x", "y", "core")
F32 = jnp.float32
BF16 = jnp.bfloat16
I32 = jnp.int32
MIB = 1024 * 1024
VMEM = pl.BlockSpec(memory_space=pltpu.VMEM)
HBM = pl.BlockSpec(memory_space=pltpu.HBM)


def in_hbm(x):
    return pltpu.with_memory_space_constraint(x, pltpu.HBM)


def beam_index():
    return (lax.axis_index("x") * 4 + lax.axis_index("y")) * 2 + lax.axis_index("core")


def transposed_dot(a, b):
    return lax.dot_general(a, b, (((0,), (0,)), ((), ())), preferred_element_type=F32)


def pack_kernel(
    parent_hbm, len_hbm, q_hbm, key_hbm, value_hbm,
    m0, m1, m2, m3, limit_ref,
    parent_ref, len_ref, q_ref, key_ref, value_ref, head_ref, place_ref, info_ref, sems,
):
    pairs = (
        (parent_hbm, parent_ref),
        (q_hbm, q_ref),
        (key_hbm, key_ref),
        (value_hbm, value_ref),
        (len_hbm, len_ref),
    )
    copies = [pltpu.make_async_copy(a, b, sems.at[n]) for n, (a, b) in enumerate(pairs)]
    for copy in copies:
        copy.start()
    info_ref[...] = jnp.zeros_like(info_ref)
    member = beam_index() % 4
    copies[0].wait()
    partner, order = [], []
    for s in range(SLOTS):
        partner.append((parent_ref[s] // SLOTS) % 4 ^ member)
        earlier = sum([(partner[e] == partner[s]).astype(I32) for e in range(s)], jnp.int32(0))
        order.append(jnp.minimum(earlier, 1))
    for copy in copies[1:4]:
        copy.wait()
    queries = q_ref[...].astype(F32)
    for h in range(GROUPED):
        head_ref[h * SLOTS : (h + 1) * SLOTS, :] = queries[:, h * HEAD : (h + 1) * HEAD]
    fresh_keys = key_ref[...].astype(F32)
    fresh_values = value_ref[...].astype(F32)
    for s in range(SLOTS):
        block = pl.multiple_of(partner[s] * 16 + order[s] * 8, 8)
        place_ref[pl.ds(block, GROUPED), :] = head_ref[pl.ds(s, GROUPED, stride=SLOTS), :]
        row = partner[s] * 16 + order[s]
        cache_row = (parent_ref[s] % SLOTS).astype(F32)
        slot = (member * SLOTS + s).astype(F32)
        info_ref[pl.ds(row, 1), :] = fresh_keys[s : s + 1]
        info_ref[pl.ds(row + 2, 1), :] = fresh_values[s : s + 1]
        info_ref[pl.ds(row + 4, 1), :] = jnp.full((1, HEAD), cache_row, F32)
        info_ref[pl.ds(row + 6, 1), :] = jnp.full((1, HEAD), slot, F32)
    for j, out_ref in enumerate((m0, m1, m2, m3)):
        out_ref[:16, :] = place_ref[j * 16 : j * 16 + 16, :].astype(BF16)
        out_ref[16:, :] = info_ref[j * 16 : j * 16 + 16, :].astype(BF16)
    copies[4].wait()
    rows = lax.broadcasted_iota(I32, (SLOTS, HEAD), 0)
    spread = jnp.zeros((SLOTS, HEAD), I32)
    for r in range(SLOTS):
        spread = jnp.where(rows == r, len_ref[r], spread)
    limit_ref[...] = spread


def load_kernel(after_ref, k_hbm, k_out, sems):
    copies = [
        pltpu.make_async_copy(k_hbm.at[r], k_out.at[r], sems.at[r]) for r in range(SLOTS)
    ]
    for copy in copies:
        copy.start()
    for copy in copies:
        copy.wait()


def attend_kernel(limit_ref, m0, m1, m2, m3, k_ref, v_hbm, out_ref, v_ref, s_ref, o_ref, sems):
    infos = [m[16:, :].astype(F32) for m in (m0, m1, m2, m3)]
    heads = [m[:16, :].astype(F32) for m in (m0, m1, m2, m3)]
    info_ints = [info.astype(I32) for info in infos]
    cache_rows, fetches = [], []
    for i in range(SLOTS):
        row = jnp.clip(info_ints[i // 2][4 + i % 2, 0], 0, SLOTS - 1)
        cache_rows.append(row)
        fetches.append(pltpu.make_async_copy(v_hbm.at[row], v_ref.at[i], sems.at[i]))
        fetches[i].start()
    scale = HEAD ** (-0.5)
    positions = lax.broadcasted_iota(I32, (GROUPED, POSITIONS), 1)
    new_scores = []
    for i in range(SLOTS):
        q = heads[i // 2][i % 2 * 8 : i % 2 * 8 + 8]
        fresh_key = infos[i // 2][i % 2 : i % 2 + 1]
        scores = lax.dot_general(
            q.astype(BF16), k_ref[cache_rows[i]], (((1,), (1,)), ((), ())), preferred_element_type=F32
        ) * scale
        limit = limit_ref[pl.ds(cache_rows[i], 1), :][:, :1]
        s_ref[i] = jnp.where(positions < limit, scores, -1e30)
        new_scores.append(jnp.sum(q * fresh_key, axis=1, keepdims=True) * scale)
    for i in range(SLOTS):
        scores = s_ref[i]
        maximum = jnp.maximum(jnp.max(scores, axis=1, keepdims=True), new_scores[i])
        weights = jnp.exp(scores - maximum)
        new_weight = jnp.exp(new_scores[i] - maximum)
        denominator = jnp.sum(weights, axis=1, keepdims=True) + new_weight
        fetches[i].wait()
        weighted = jnp.dot(weights.astype(BF16), v_ref[i], preferred_element_type=F32)
        fresh_value = infos[i // 2][2 + i % 2 : 3 + i % 2]
        weighted = weighted + new_weight.astype(BF16).astype(F32) * fresh_value
        o_ref[pl.ds(i, GROUPED, stride=SLOTS), :] = weighted / denominator
    ids = jnp.concatenate([info[6:8] for info in infos], axis=0)
    block = jnp.concatenate(
        [o_ref[h * SLOTS : (h + 1) * SLOTS, :] for h in range(GROUPED)] + [ids], axis=1
    )
    pair = jnp.concatenate([block, block], axis=0).astype(BF16)
    for j in range(8):
        out_ref[j * 16 : (j + 1) * 16, :] = pair


def project_kernel(own_ref, other_ref, w_ref, out_ref, place_ref):
    weight = w_ref[...]
    for part, ref in enumerate((own_ref, other_ref)):
        terms = jnp.dot(ref[:, :Q_COLS], weight, preferred_element_type=F32).astype(BF16)
        for g in range(8):
            out_ref[g * 32 + part * 16 : g * 32 + part * 16 + 16, :] = terms[g * 16 : g * 16 + 16]
    first = pl.multiple_of(lax.axis_index("tensor") * 16, 16)
    lanes = lax.broadcasted_iota(I32, (16, HEAD), 1)
    for part, ref in enumerate((own_ref, other_ref)):
        ids = ref[pl.ds(first, 16), Q_COLS:].astype(F32).astype(I32)
        place_ref[part * 16 : part * 16 + 16, :] = (ids == lanes).astype(F32).astype(BF16)


def finish_kernel(terms_ref, place_ref, out_ref):
    total = terms_ref[0:32, :].astype(F32)
    for z in range(1, 8):
        total = total + terms_ref[z * 32 : z * 32 + 32, :].astype(F32)
    out_ref[...] = transposed_dot(place_ref[...], total.astype(BF16))[:BEAMS].astype(BF16)


def pack(parents, lengths, queries, token_keys, token_values):
    message = pltpu.VMEM((PACKED, HEAD), BF16)
    operands = (parents, lengths, queries, token_keys, token_values)
    return pl.pallas_call(
        pack_kernel,
        out_shape=(message,) * 4 + (pltpu.VMEM((SLOTS, HEAD), I32),),
        in_specs=[HBM] * 5,
        out_specs=(VMEM,) * 5,
        scratch_shapes=[
            pltpu.SMEM((SLOTS,), I32),
            pltpu.SMEM((SLOTS,), I32),
            pltpu.VMEM((SLOTS, Q_COLS), BF16),
            pltpu.VMEM((SLOTS, HEAD), BF16),
            pltpu.VMEM((SLOTS, HEAD), BF16),
            pltpu.VMEM((GROUPED * SLOTS, HEAD), F32),
            pltpu.VMEM((GROUPED * SLOTS, HEAD), F32),
            pltpu.VMEM((64, HEAD), F32),
            pltpu.SemaphoreType.DMA((5,)),
        ],
        name="pack",
    )(*[in_hbm(x) for x in operands])


def load(message, key_cache):
    return pl.pallas_call(
        load_kernel,
        out_shape=pltpu.VMEM((SLOTS, POSITIONS, HEAD), BF16),
        in_specs=[VMEM, HBM],
        out_specs=VMEM,
        scratch_shapes=[pltpu.SemaphoreType.DMA((SLOTS,))],
        compiler_params=pltpu.CompilerParams(vmem_limit_bytes=8 * MIB),
        cost_estimate=pl.CostEstimate(flops=0, bytes_accessed=8 * MIB, transcendentals=0),
        name="load",
    )(message, in_hbm(key_cache.reshape(SLOTS, POSITIONS, HEAD)))


def attend(limits, messages, keys, value_cache):
    return pl.pallas_call(
        attend_kernel,
        out_shape=jax.ShapeDtypeStruct((16 * SLOTS, OUT_COLS), BF16),
        in_specs=[VMEM] * 6 + [HBM],
        out_specs=VMEM,
        scratch_shapes=[
            pltpu.VMEM((SLOTS, POSITIONS, HEAD), BF16),
            pltpu.VMEM((SLOTS, GROUPED, POSITIONS), F32),
            pltpu.VMEM((GROUPED * SLOTS, HEAD), F32),
            pltpu.SemaphoreType.DMA((SLOTS,)),
        ],
        compiler_params=pltpu.CompilerParams(vmem_limit_bytes=24 * MIB),
        name="attend",
    )(limits, *messages, keys, in_hbm(value_cache.reshape(SLOTS, POSITIONS, HEAD)))


def body(parents, lengths, queries, token_keys, token_values, key_cache, value_cache, weight):
    *messages, limits = pack(parents, lengths, queries, token_keys, token_values)
    arrived = [
        lax.ppermute(messages[d], BEAM_AXES, [(i, i ^ d) for i in range(32)]) for d in (1, 2, 3)
    ]
    keys = load(messages[0], key_cache)
    heads = attend(limits, [messages[0]] + arrived, keys, value_cache)
    gathered = lax.all_to_all(heads, ("x", "y"), 0, 0, tiled=True)
    other = lax.ppermute(gathered, BEAM_AXES, [(i, i ^ 1) for i in range(32)])
    terms, place = pl.pallas_call(
        project_kernel,
        out_shape=(
            jax.ShapeDtypeStruct((256, 256), BF16),
            jax.ShapeDtypeStruct((BEAMS, HEAD), BF16),
        ),
        in_specs=[VMEM] * 3,
        out_specs=(VMEM, VMEM),
        compiler_params=pltpu.CompilerParams(vmem_limit_bytes=16 * MIB),
        name="project",
    )(gathered, other, weight)
    shares = lax.all_to_all(terms, "tensor", 0, 0, tiled=True)
    return pl.pallas_call(
        finish_kernel,
        out_shape=jax.ShapeDtypeStruct((BEAMS, 256), BF16),
        in_specs=[VMEM] * 2,
        out_specs=VMEM,
        compiler_params=pltpu.CompilerParams(vmem_limit_bytes=16 * MIB),
        name="finish",
    )(shares, place)


def solution(mesh):
    fine = Mesh(mesh.devices.reshape(4, 4, 2, 8), ("x", "y", "core", "tensor"))
    in_specs = (
        P(BEAM_AXES),
        P(BEAM_AXES),
        P(BEAM_AXES, "tensor"),
        P(BEAM_AXES, "tensor"),
        P(BEAM_AXES, "tensor"),
        P(BEAM_AXES, "tensor", None, None),
        P(BEAM_AXES, "tensor", None, None),
        P("tensor", BEAM_AXES),
    )
    out_specs = P("tensor", BEAM_AXES)
    return jax.shard_map(body, mesh=fine, in_specs=in_specs, out_specs=out_specs, check_vma=False)
```

time: 49.3 us -> 44.3 us (0.90)
  local copies, waits for them, and re-layouts: 5.11 us -> 0.01 us
  Pallas kernels: 3.86 us -> 7.18 us
  waiting for transfers between devices: 2.69 us -> 1.22 us
  other arithmetic: 1.41 us -> 0 us
  blocking collectives: 29 us -> 28.3 us
    unnamed x8 -> x2, local copies, waits for them, and re-layouts: 5.03 us -> 0.01 us
    pallas_call x1 -> x3, Pallas kernels: 2.76 us -> 6.08 us  [the longest x1 2.99 us: attend(): pl.pallas_call(attend_kernel, out_shape=jax.ShapeDtypeStruct((16 * SLOTS,...]
    ppermute x3, waiting for transfers between devices: 1.48 us -> 0.01 us  [body(): lax.ppermute(messages[d], BEAM_AXES, [(i, i ^ d) for i in range(32)])]
    concatenate x1 -> x0, other arithmetic: 0.75 us -> none  [body(): jnp.concatenate([queries, token_keys, token_values, marks], axis=1)]
    all_to_all x1, blocking collectives: 13.2 us -> 12.4 us  [body(): gathered = lax.all_to_all(heads, ('x', 'y'), 0, 0, tiled=True)]
    convert_element_type x1 -> x0, other arithmetic: 0.66 us -> none  [body(): marks = jnp.broadcast_to(parents.astype(BF16)[:, None], (SLOTS, HEAD))]
  transfers between devices with their start and end apart: 4 -> 4, of which waited for: 2 -> 1; matrix products, arithmetic and copies ran while one was open for 0% -> 0% of each run, Pallas kernels for 0% -> 5%
where the time goes in v3:
time: 44.3 us; the launch traced here: 44 us
  blocking collectives  28.3 us (64%)
  starting transfers between devices  7.23 us (16%)
  Pallas kernels  7.18 us (16%)
  waiting for transfers between devices  1.22 us (3%)
    all_to_all x1, blocking collectives, body(): shares = lax.all_to_all(terms, 'tensor', 0, 0, tiled=True)  15.9 us
    all_to_all x1, blocking collectives, body(): gathered = lax.all_to_all(heads, ('x', 'y'), 0, 0, tiled=True)  12.4 us
    ppermute x3, starting transfers between devices, body(): lax.ppermute(messages[d], BEAM_AXES, [(i, i ^ d) for i in range(32)])  5.06 us
    pallas_call x1, Pallas kernels, attend(): pl.pallas_call(attend_kernel, out_shape=jax.ShapeDtypeStruct((16 * SLOTS,...  2.99 us
    pallas_call x1, Pallas kernels, load(): pl.pallas_call(load_kernel, out_shape=pltpu.VMEM((SLOTS, POSITIONS, HEAD)...  2.21 us
    ppermute x1, starting transfers between devices, body(): other = lax.ppermute(gathered, BEAM_AXES, [(i, i ^ 1) for i in range(32)])  2.17 us
    ppermute x1, waiting for transfers between devices, body(): other = lax.ppermute(gathered, BEAM_AXES, [(i, i ^ 1) for i in range(32)])  1.21 us
  transfers between devices with their start and end apart: 4, of which 1 were waited for; matrix products, arithmetic and copies ran while one was open for 0% of the time, Pallas kernels for 5%

profile of v3, /device:TPU:1, one launch (start us, length us, event | category | flops | bytes accessed | tf_op | source)
XLA Modules:
  0.0 44.0 jit_solution(7027058433973448003)
XLA Ops:
  0.0 0.9 %pack.1 = (bf16[32,128]{1,0:T(8,128)(2,1)S(1)}, bf16[32,128]{1,0:T(8,128)(2,1)S(1)}, bf16[32,128]{1,0:T(8,128)(2,1)S(1)}, bf16[32,128]{1,0:T(8,128)(2,1)S(1)}, s32[8,128]{1,0:T(8,128)S(1)}) custom-call(s32[8]{0:T(128)} %parent_hbm.1, s32[8]{0:T(128)} %len_hbm.1, bf16[8,1024]{1,0:T(8,128)(2,1)} %q_hbm.1, bf16[8,128]{1,0:T(8,128)(2,1)} %key_hbm.1, ...), custom_call_target="tpu_custom_call" | custom-call | tf_op jit(solution)/shard_map/pack/pallas_call | solution.py:164
  0.9 3.3 %collective-permute-start = (bf16[32,128]{1,0:T(8,128)(2,1)S(1)}, bf16[32,128]{1,0:T(8,128)(2,1)S(1)}, u32[]{:S(2)}, u32[]{:S(2)}) collective-permute-start(bf16[32,128]{1,0:T(8,128)(2,1)S(1)} %get-tuple-element.14), channel_id=1, source_target_pairs={{0,8},{8,0},{16,24},{24,16},{32,40},{40,32},{48,56},{56,48},{64,72... | collective-permute-start | bytes 24584 | tf_op jit(solution)/shard_map/ppermute | solution.py:217
  4.2 0.0 collective-permute-start.1
  4.2 1.7 %collective-permute-start.2 = (bf16[32,128]{1,0:T(8,128)(2,1)S(1)}, bf16[32,128]{1,0:T(8,128)(2,1)S(1)}, u32[]{:S(2)}, u32[]{:S(2)}) collective-permute-start(bf16[32,128]{1,0:T(8,128)(2,1)S(1)} %get-tuple-element.16), channel_id=1, source_target_pairs={{0,24},{8,16},{16,8},{24,0},{32,56},{40,48},{48,40},{56,32},{64,88... | collective-permute-start | bytes 24584 | tf_op jit(solution)/shard_map/ppermute | solution.py:217
  5.9 2.2 %load.1.k_ref = bf16[8,2048,128]{2,1,0:T(8,128)(2,1)S(1)} custom-call(bf16[32,128]{1,0:T(8,128)(2,1)S(1)} %get-tuple-element.13.after_ref.m0, bf16[8,2048,128]{2,1,0:T(8,128)(2,1)} %bitcast.11), custom_call_target="tpu_custom_call" | custom-call | bytes 8388608 | tf_op jit(solution)/shard_map/load/pallas_call | solution.py:185
  8.2 0.0 collective-permute-done.m1
  8.2 0.0 collective-permute-done.1.m2
  8.2 0.0 collective-permute-done.2.m3
  8.2 0.0 copy-start
  8.2 3.0 %attend.1 = bf16[128,1152]{1,0:T(8,128)(2,1)S(1)} custom-call(s32[8,128]{1,0:T(8,128)S(1)} %get-tuple-element.12.limit_ref, bf16[32,128]{1,0:T(8,128)(2,1)S(1)} %get-tuple-element.13.after_ref.m0, bf16[32,128]{1,0:T(8,128)(2,1)S(1)} %collective-permute-done.m1, bf16[32,128]{1,0:T(8,128)(2,1)S(1)} %collective-permute-done.1.m2, ...), custom_call_target="tpu_custom_call" | custom-call | tf_op jit(solution)/shard_map/attend/pallas_call | solution.py:198
  11.2 12.4 %all_to_all.22 = bf16[16,8,1152]{2,1,0:T(8,128)(2,1)S(1)} all-to-all(bf16[16,8,1152]{2,1,0:T(8,128)(2,1)S(1)} %bitcast.6), channel_id=1, replica_groups=mesh['x'=4,'y'=4,'core'=2,'tensor'=8] {'x','y'}, dimensions={0} | all-to-all | bytes 589824 | tf_op jit(solution)/shard_map/all_to_all | solution.py:221
  23.6 2.2 %collective-permute-start.3 = (bf16[128,1152]{1,0:T(8,128)(2,1)S(1)}, bf16[128,1152]{1,0:T(8,128)(2,1)S(1)}, u32[]{:S(2)}, u32[]{:S(2)}) collective-permute-start(bf16[128,1152]{1,0:T(8,128)(2,1)S(1)} %bitcast.7), channel_id=1, source_target_pairs={{0,8},{8,0},{16,24},{24,16},{32,40},{40,32},{48,56},{56,48},{64,72... | collective-permute-start | bytes 884744 | tf_op jit(solution)/shard_map/ppermute | solution.py:222
  25.8 1.2 %collective-permute-done.3.other_ref = bf16[128,1152]{1,0:T(8,128)(2,1)S(1)} collective-permute-done((bf16[128,1152]{1,0:T(8,128)(2,1)S(1)}, bf16[128,1152]{1,0:T(8,128)(2,1)S(1)}, u32[]{:S(2)}, u32[]{:S(2)}) %collective-permute-start.3) | collective-permute-done | bytes 294944 | tf_op jit(solution)/shard_map/ppermute | solution.py:222
  27.0 0.0 copy-done
  27.0 0.3 project.1
  27.3 15.9 %all_to_all.23 = bf16[8,32,256]{2,1,0:T(8,128)(2,1)S(1)} all-to-all(bf16[8,32,256]{2,1,0:T(8,128)(2,1)S(1)} %bitcast.10), channel_id=1, replica_groups=mesh['x'=4,'y'=4,'core'=2,'tensor'=8] {'tensor'}, dimensions={0} | all-to-all | bytes 262144 | tf_op jit(solution)/shard_map/all_to_all | solution.py:234
  43.2 0.8 %finish.1 = bf16[32,256]{1,0:T(8,128)(2,1)} custom-call(bf16[256,256]{1,0:T(8,128)(2,1)S(1)} %bitcast.9, bf16[32,128]{1,0:T(8,128)(2,1)S(1)} %get-tuple-element.18.place_ref), custom_call_target="tpu_custom_call" | custom-call | tf_op jit(solution)/shard_map/finish/pallas_call | solution.py:235
Async XLA Ops:
  0.9 7.3 %collective-permute-start = (bf16[32,128]{1,0:T(8,128)(2,1)S(1)}, bf16[32,128]{1,0:T(8,128)(2,1)S(1)}, u32[]{:S(2)}, u32[]{:S(2)}) collective-permute-start(bf16[32,128]{1,0:T(8,128)(2,1)S(1)} %get-tuple-element.14), channel_id=1, source_target_pairs={{0,8},{8,0},{16,24},{24,16},{32,40},{40,32},{48,56},{56,48},{64,72... | collective-permute-start | bytes 24584 | tf_op jit(solution)/shard_map/ppermute | solution.py:217
  4.2 4.0 %collective-permute-start.1 = (bf16[32,128]{1,0:T(8,128)(2,1)S(1)}, bf16[32,128]{1,0:T(8,128)(2,1)S(1)}, u32[]{:S(2)}, u32[]{:S(2)}) collective-permute-start(bf16[32,128]{1,0:T(8,128)(2,1)S(1)} %get-tuple-element.15), channel_id=1, source_target_pairs={{0,16},{8,24},{16,0},{24,8},{32,48},{40,56},{48,32},{56,40},{64,80... | collective-permute-start | bytes 24584 | tf_op jit(solution)/shard_map/ppermute | solution.py:217
  4.2 4.0 %collective-permute-start.2 = (bf16[32,128]{1,0:T(8,128)(2,1)S(1)}, bf16[32,128]{1,0:T(8,128)(2,1)S(1)}, u32[]{:S(2)}, u32[]{:S(2)}) collective-permute-start(bf16[32,128]{1,0:T(8,128)(2,1)S(1)} %get-tuple-element.16), channel_id=1, source_target_pairs={{0,24},{8,16},{16,8},{24,0},{32,56},{40,48},{48,40},{56,32},{64,88... | collective-permute-start | bytes 24584 | tf_op jit(solution)/shard_map/ppermute | solution.py:217
  8.2 18.8 %copy-start = (bf16[1024,256]{1,0:T(8,128)(2,1)S(1)}, bf16[1024,256]{1,0:T(8,128)(2,1)}, u32[]{:S(2)}) copy-start(bf16[1024,256]{1,0:T(8,128)(2,1)} %w_ref.1) | copy-start | bytes 1572868
  23.6 3.4 %collective-permute-start.3 = (bf16[128,1152]{1,0:T(8,128)(2,1)S(1)}, bf16[128,1152]{1,0:T(8,128)(2,1)S(1)}, u32[]{:S(2)}, u32[]{:S(2)}) collective-permute-start(bf16[128,1152]{1,0:T(8,128)(2,1)S(1)} %bitcast.7), channel_id=1, source_target_pairs={{0,8},{8,0},{16,24},{24,16},{32,40},{40,32},{48,56},{56,48},{64,72... | collective-permute-start | bytes 884744 | tf_op jit(solution)/shard_map/ppermute | solution.py:222

commit v4 on v3

--- a/solution.py
+++ b/solution.py
@@ -86,26 +86,13 @@
     limit_ref[...] = spread
 
 
-def load_kernel(after_ref, k_hbm, k_out, sems):
-    copies = [
-        pltpu.make_async_copy(k_hbm.at[r], k_out.at[r], sems.at[r]) for r in range(SLOTS)
-    ]
-    for copy in copies:
-        copy.start()
-    for copy in copies:
-        copy.wait()
-
-
-def attend_kernel(limit_ref, m0, m1, m2, m3, k_ref, v_hbm, out_ref, v_ref, s_ref, o_ref, sems):
+def attend_kernel(limit_ref, m0, m1, m2, m3, k_ref, v_ref, out_ref, s_ref, o_ref):
     infos = [m[16:, :].astype(F32) for m in (m0, m1, m2, m3)]
     heads = [m[:16, :].astype(F32) for m in (m0, m1, m2, m3)]
     info_ints = [info.astype(I32) for info in infos]
-    cache_rows, fetches = [], []
-    for i in range(SLOTS):
-        row = jnp.clip(info_ints[i // 2][4 + i % 2, 0], 0, SLOTS - 1)
-        cache_rows.append(row)
-        fetches.append(pltpu.make_async_copy(v_hbm.at[row], v_ref.at[i], sems.at[i]))
-        fetches[i].start()
+    cache_rows = [
+        jnp.clip(info_ints[i // 2][4 + i % 2, 0], 0, SLOTS - 1) for i in range(SLOTS)
+    ]
     scale = HEAD ** (-0.5)
     positions = lax.broadcasted_iota(I32, (GROUPED, POSITIONS), 1)
     new_scores = []
@@ -124,8 +111,9 @@
         weights = jnp.exp(scores - maximum)
         new_weight = jnp.exp(new_scores[i] - maximum)
         denominator = jnp.sum(weights, axis=1, keepdims=True) + new_weight
-        fetches[i].wait()
-        weighted = jnp.dot(weights.astype(BF16), v_ref[i], preferred_element_type=F32)
+        weighted = jnp.dot(
+            weights.astype(BF16), v_ref[cache_rows[i]], preferred_element_type=F32
+        )
         fresh_value = infos[i // 2][2 + i % 2 : 3 + i % 2]
         weighted = weighted + new_weight.astype(BF16).astype(F32) * fresh_value
         o_ref[pl.ds(i, GROUPED, stride=SLOTS), :] = weighted / denominator
@@ -177,38 +165,24 @@
             pltpu.VMEM((64, HEAD), F32),
             pltpu.SemaphoreType.DMA((5,)),
         ],
+        cost_estimate=pl.CostEstimate(flops=2 * 10**10, bytes_accessed=0, transcendentals=0),
         name="pack",
     )(*[in_hbm(x) for x in operands])
 
 
-def load(message, key_cache):
-    return pl.pallas_call(
-        load_kernel,
-        out_shape=pltpu.VMEM((SLOTS, POSITIONS, HEAD), BF16),
-        in_specs=[VMEM, HBM],
-        out_specs=VMEM,
-        scratch_shapes=[pltpu.SemaphoreType.DMA((SLOTS,))],
-        compiler_params=pltpu.CompilerParams(vmem_limit_bytes=8 * MIB),
-        cost_estimate=pl.CostEstimate(flops=0, bytes_accessed=8 * MIB, transcendentals=0),
-        name="load",
-    )(message, in_hbm(key_cache.reshape(SLOTS, POSITIONS, HEAD)))
-
-
-def attend(limits, messages, keys, value_cache):
+def attend(limits, messages, key_cache, value_cache):
     return pl.pallas_call(
         attend_kernel,
         out_shape=jax.ShapeDtypeStruct((16 * SLOTS, OUT_COLS), BF16),
-        in_specs=[VMEM] * 6 + [HBM],
+        in_specs=[VMEM] * 7,
         out_specs=VMEM,
         scratch_shapes=[
-            pltpu.VMEM((SLOTS, POSITIONS, HEAD), BF16),
             pltpu.VMEM((SLOTS, GROUPED, POSITIONS), F32),
             pltpu.VMEM((GROUPED * SLOTS, HEAD), F32),
-            pltpu.SemaphoreType.DMA((SLOTS,)),
         ],
         compiler_params=pltpu.CompilerParams(vmem_limit_bytes=24 * MIB),
         name="attend",
-    )(limits, *messages, keys, in_hbm(value_cache.reshape(SLOTS, POSITIONS, HEAD)))
+    )(limits, *messages, *[x.reshape(SLOTS, POSITIONS, HEAD) for x in (key_cache, value_cache)])
 
 
 def body(parents, lengths, queries, token_keys, token_values, key_cache, value_cache, weight):
@@ -216,8 +190,7 @@
     arrived = [
         lax.ppermute(messages[d], BEAM_AXES, [(i, i ^ d) for i in range(32)]) for d in (1, 2, 3)
     ]
-    keys = load(messages[0], key_cache)
-    heads = attend(limits, [messages[0]] + arrived, keys, value_cache)
+    heads = attend(limits, [messages[0]] + arrived, key_cache, value_cache)
     gathered = lax.all_to_all(heads, ("x", "y"), 0, 0, tiled=True)
     other = lax.ppermute(gathered, BEAM_AXES, [(i, i ^ 1) for i in range(32)])
     terms, place = pl.pallas_call(

time: 44.3 us -> 47.6 us (1.074)
  local copies, waits for them, and re-layouts: 0.01 us -> 4.38 us
  Pallas kernels: 7.18 us -> 3.81 us
  waiting for transfers between devices: 1.22 us -> 2.83 us
  blocking collectives: 28.3 us -> 29.2 us
    unnamed x2 -> x6, local copies, waits for them, and re-layouts: 0.01 us -> 4.38 us
    pallas_call x1 -> x0, Pallas kernels: 2.21 us -> none  [load(): pl.pallas_call(load_kernel, out_shape=pltpu.VMEM((SLOTS, POSITIONS, HEAD)...]
    ppermute x3, waiting for transfers between devices: 0.01 us -> 1.62 us  [body(): lax.ppermute(messages[d], BEAM_AXES, [(i, i ^ d) for i in range(32)])]
    pallas_call x1, Pallas kernels: 2.99 us -> 1.83 us  [attend(): pl.pallas_call(attend_kernel, out_shape=jax.ShapeDtypeStruct((16 * SLOTS,...]
    all_to_all x1, blocking collectives: 12.4 us -> 13.3 us  [body(): gathered = lax.all_to_all(heads, ('x', 'y'), 0, 0, tiled=True)]
  transfers between devices with their start and end apart: 4 -> 4, of which waited for: 1 -> 3; matrix products, arithmetic and copies ran while one was open for 0% -> 0% of each run, Pallas kernels for 5% -> 0%
where the time goes in v4:
time: 47.6 us; the launch traced here: 47.3 us
  blocking collectives  29.2 us (61%)
  starting transfers between devices  7.1 us (15%)
  local copies, waits for them, and re-layouts  4.38 us (9%)
  Pallas kernels  3.81 us (8%)
  waiting for transfers between devices  2.83 us (6%)
    all_to_all x1, blocking collectives, body(): shares = lax.all_to_all(terms, 'tensor', 0, 0, tiled=True)  15.9 us
    all_to_all x1, blocking collectives, body(): gathered = lax.all_to_all(heads, ('x', 'y'), 0, 0, tiled=True)  13.3 us
    ppermute x3, starting transfers between devices, body(): lax.ppermute(messages[d], BEAM_AXES, [(i, i ^ d) for i in range(32)])  5.06 us
    unnamed x6, local copies, waits for them, and re-layouts  4.38 us
    ppermute x1, starting transfers between devices, body(): other = lax.ppermute(gathered, BEAM_AXES, [(i, i ^ 1) for i in range(32)])  2.05 us
    pallas_call x1, Pallas kernels, attend(): pl.pallas_call(attend_kernel, out_shape=jax.ShapeDtypeStruct((16 * SLOTS,...  1.83 us
    ppermute x3, waiting for transfers between devices, body(): lax.ppermute(messages[d], BEAM_AXES, [(i, i ^ d) for i in range(32)])  1.62 us
    ppermute x1, waiting for transfers between devices, body(): other = lax.ppermute(gathered, BEAM_AXES, [(i, i ^ 1) for i in range(32)])  1.21 us
  transfers between devices with their start and end apart: 4, of which 3 were waited for; matrix products, arithmetic and copies ran while one was open for 0% of the time, Pallas kernels for 0%

profile of v4, /device:TPU:1, one launch (start us, length us, event | category | flops | bytes accessed | tf_op | source)
XLA Modules:
  0.0 47.3 jit_solution(14631471439815679949)
XLA Ops:
  0.0 0.9 %pack.1 = (bf16[32,128]{1,0:T(8,128)(2,1)S(1)}, bf16[32,128]{1,0:T(8,128)(2,1)S(1)}, bf16[32,128]{1,0:T(8,128)(2,1)S(1)}, bf16[32,128]{1,0:T(8,128)(2,1)S(1)}, s32[8,128]{1,0:T(8,128)S(1)}) custom-call(s32[8]{0:T(128)} %parent_hbm.1, s32[8]{0:T(128)} %len_hbm.1, bf16[8,1024]{1,0:T(8,128)(2,1)} %q_hbm.1, bf16[8,128]{1,0:T(8,128)(2,1)} %key_hbm.1, ...), custom_call_target="tpu_custom_call" | custom-call | flops 20000000000 | tf_op jit(solution)/shard_map/pack/pallas_call | solution.py:152
  0.9 3.3 %collective-permute-start = (bf16[32,128]{1,0:T(8,128)(2,1)S(1)}, bf16[32,128]{1,0:T(8,128)(2,1)S(1)}, u32[]{:S(2)}, u32[]{:S(2)}) collective-permute-start(bf16[32,128]{1,0:T(8,128)(2,1)S(1)} %get-tuple-element.14), channel_id=1, source_target_pairs={{0,8},{8,0},{16,24},{24,16},{32,40},{40,32},{48,56},{56,48},{64,72... | collective-permute-start | bytes 24584 | tf_op jit(solution)/shard_map/ppermute | solution.py:191
  4.2 0.0 collective-permute-start.1
  4.2 1.7 %collective-permute-start.2 = (bf16[32,128]{1,0:T(8,128)(2,1)S(1)}, bf16[32,128]{1,0:T(8,128)(2,1)S(1)}, u32[]{:S(2)}, u32[]{:S(2)}) collective-permute-start(bf16[32,128]{1,0:T(8,128)(2,1)S(1)} %get-tuple-element.16), channel_id=1, source_target_pairs={{0,24},{8,16},{16,8},{24,0},{32,56},{40,48},{48,40},{56,32},{64,88... | collective-permute-start | bytes 24584 | tf_op jit(solution)/shard_map/ppermute | solution.py:191
  5.9 0.0 collective-permute-done.m1
  5.9 0.8 %collective-permute-done.1.m2 = bf16[32,128]{1,0:T(8,128)(2,1)S(1)} collective-permute-done((bf16[32,128]{1,0:T(8,128)(2,1)S(1)}, bf16[32,128]{1,0:T(8,128)(2,1)S(1)}, u32[]{:S(2)}, u32[]{:S(2)}) %collective-permute-start.1) | collective-permute-done | bytes 8224 | tf_op jit(solution)/shard_map/ppermute | solution.py:191
  6.7 0.8 %collective-permute-done.2.m3 = bf16[32,128]{1,0:T(8,128)(2,1)S(1)} collective-permute-done((bf16[32,128]{1,0:T(8,128)(2,1)S(1)}, bf16[32,128]{1,0:T(8,128)(2,1)S(1)}, u32[]{:S(2)}, u32[]{:S(2)}) %collective-permute-start.2) | collective-permute-done | bytes 8224 | tf_op jit(solution)/shard_map/ppermute | solution.py:191
  7.6 0.0 copy-start
  7.6 2.2 %copy-done = bf16[8,1,2048,128]{3,2,1,0:T(8,128)(2,1)S(1)} copy-done((bf16[8,1,2048,128]{3,2,1,0:T(8,128)(2,1)S(1)}, bf16[8,1,2048,128]{3,2,1,0:T(8,128)(2,1)}, u32[]{:S(2)}) %copy-start) | copy-done | bytes 4194328
  9.8 0.0 copy-start.1
  9.8 2.2 %copy-done.1 = bf16[8,1,2048,128]{3,2,1,0:T(8,128)(2,1)S(1)} copy-done((bf16[8,1,2048,128]{3,2,1,0:T(8,128)(2,1)S(1)}, bf16[8,1,2048,128]{3,2,1,0:T(8,128)(2,1)}, u32[]{:S(2)}) %copy-start.1) | copy-done | bytes 4194328
  11.9 0.0 copy-start.2
  11.9 1.8 %attend.1 = bf16[128,1152]{1,0:T(8,128)(2,1)S(1)} custom-call(s32[8,128]{1,0:T(8,128)S(1)} %get-tuple-element.12.limit_ref, bf16[32,128]{1,0:T(8,128)(2,1)S(1)} %get-tuple-element.13.m0, bf16[32,128]{1,0:T(8,128)(2,1)S(1)} %collective-permute-done.m1, bf16[32,128]{1,0:T(8,128)(2,1)S(1)} %collective-permute-done.1.m2, ...), custom_call_target="tpu_custom_call" | custom-call | tf_op jit(solution)/shard_map/attend/pallas_call | solution.py:174
  13.8 13.3 %all_to_all.22 = bf16[16,8,1152]{2,1,0:T(8,128)(2,1)S(1)} all-to-all(bf16[16,8,1152]{2,1,0:T(8,128)(2,1)S(1)} %bitcast.8), channel_id=1, replica_groups=mesh['x'=4,'y'=4,'core'=2,'tensor'=8] {'x','y'}, dimensions={0} | all-to-all | bytes 589824 | tf_op jit(solution)/shard_map/all_to_all | solution.py:194
  27.1 2.0 %collective-permute-start.3 = (bf16[128,1152]{1,0:T(8,128)(2,1)S(1)}, bf16[128,1152]{1,0:T(8,128)(2,1)S(1)}, u32[]{:S(2)}, u32[]{:S(2)}) collective-permute-start(bf16[128,1152]{1,0:T(8,128)(2,1)S(1)} %bitcast.9), channel_id=1, source_target_pairs={{0,8},{8,0},{16,24},{24,16},{32,40},{40,32},{48,56},{56,48},{64,72... | collective-permute-start | bytes 884744 | tf_op jit(solution)/shard_map/ppermute | solution.py:195
  29.1 1.2 %collective-permute-done.3.other_ref = bf16[128,1152]{1,0:T(8,128)(2,1)S(1)} collective-permute-done((bf16[128,1152]{1,0:T(8,128)(2,1)S(1)}, bf16[128,1152]{1,0:T(8,128)(2,1)S(1)}, u32[]{:S(2)}, u32[]{:S(2)}) %collective-permute-start.3) | collective-permute-done | bytes 294944 | tf_op jit(solution)/shard_map/ppermute | solution.py:195
  30.3 0.0 copy-done.2
  30.4 0.3 project.1
  30.7 15.9 %all_to_all.23 = bf16[8,32,256]{2,1,0:T(8,128)(2,1)S(1)} all-to-all(bf16[8,32,256]{2,1,0:T(8,128)(2,1)S(1)} %bitcast.12), channel_id=1, replica_groups=mesh['x'=4,'y'=4,'core'=2,'tensor'=8] {'tensor'}, dimensions={0} | all-to-all | bytes 262144 | tf_op jit(solution)/shard_map/all_to_all | solution.py:207
  46.5 0.8 %finish.1 = bf16[32,256]{1,0:T(8,128)(2,1)} custom-call(bf16[256,256]{1,0:T(8,128)(2,1)S(1)} %bitcast.11, bf16[32,128]{1,0:T(8,128)(2,1)S(1)} %get-tuple-element.18.place_ref), custom_call_target="tpu_custom_call" | custom-call | tf_op jit(solution)/shard_map/finish/pallas_call | solution.py:208
Async XLA Ops:
  0.9 5.1 %collective-permute-start = (bf16[32,128]{1,0:T(8,128)(2,1)S(1)}, bf16[32,128]{1,0:T(8,128)(2,1)S(1)}, u32[]{:S(2)}, u32[]{:S(2)}) collective-permute-start(bf16[32,128]{1,0:T(8,128)(2,1)S(1)} %get-tuple-element.14), channel_id=1, source_target_pairs={{0,8},{8,0},{16,24},{24,16},{32,40},{40,32},{48,56},{56,48},{64,72... | collective-permute-start | bytes 24584 | tf_op jit(solution)/shard_map/ppermute | solution.py:191
  4.2 2.5 %collective-permute-start.1 = (bf16[32,128]{1,0:T(8,128)(2,1)S(1)}, bf16[32,128]{1,0:T(8,128)(2,1)S(1)}, u32[]{:S(2)}, u32[]{:S(2)}) collective-permute-start(bf16[32,128]{1,0:T(8,128)(2,1)S(1)} %get-tuple-element.15), channel_id=1, source_target_pairs={{0,16},{8,24},{16,0},{24,8},{32,48},{40,56},{48,32},{56,40},{64,80... | collective-permute-start | bytes 24584 | tf_op jit(solution)/shard_map/ppermute | solution.py:191
  4.2 3.4 %collective-permute-start.2 = (bf16[32,128]{1,0:T(8,128)(2,1)S(1)}, bf16[32,128]{1,0:T(8,128)(2,1)S(1)}, u32[]{:S(2)}, u32[]{:S(2)}) collective-permute-start(bf16[32,128]{1,0:T(8,128)(2,1)S(1)} %get-tuple-element.16), channel_id=1, source_target_pairs={{0,24},{8,16},{16,8},{24,0},{32,56},{40,48},{48,40},{56,32},{64,88... | collective-permute-start | bytes 24584 | tf_op jit(solution)/shard_map/ppermute | solution.py:191
  7.6 2.2 %copy-start = (bf16[8,1,2048,128]{3,2,1,0:T(8,128)(2,1)S(1)}, bf16[8,1,2048,128]{3,2,1,0:T(8,128)(2,1)}, u32[]{:S(2)}) copy-start(bf16[8,1,2048,128]{3,2,1,0:T(8,128)(2,1)} %param.13) | copy-start | bytes 12582916
  9.8 2.2 %copy-start.1 = (bf16[8,1,2048,128]{3,2,1,0:T(8,128)(2,1)S(1)}, bf16[8,1,2048,128]{3,2,1,0:T(8,128)(2,1)}, u32[]{:S(2)}) copy-start(bf16[8,1,2048,128]{3,2,1,0:T(8,128)(2,1)} %param.14) | copy-start | bytes 12582916
  11.9 18.4 %copy-start.2 = (bf16[1024,256]{1,0:T(8,128)(2,1)S(1)}, bf16[1024,256]{1,0:T(8,128)(2,1)}, u32[]{:S(2)}) copy-start(bf16[1024,256]{1,0:T(8,128)(2,1)} %w_ref.1) | copy-start | bytes 1572868
  27.1 3.3 %collective-permute-start.3 = (bf16[128,1152]{1,0:T(8,128)(2,1)S(1)}, bf16[128,1152]{1,0:T(8,128)(2,1)S(1)}, u32[]{:S(2)}, u32[]{:S(2)}) collective-permute-start(bf16[128,1152]{1,0:T(8,128)(2,1)S(1)} %bitcast.9), channel_id=1, source_target_pairs={{0,8},{8,0},{16,24},{24,16},{32,40},{40,32},{48,56},{56,48},{64,72... | collective-permute-start | bytes 884744 | tf_op jit(solution)/shard_map/ppermute | solution.py:195

commit v5 on v4

--- a/solution.py
+++ b/solution.py
@@ -51,11 +51,11 @@
     for copy in copies:
         copy.start()
     info_ref[...] = jnp.zeros_like(info_ref)
-    member = beam_index() % 4
+    member = beam_index() & 3
     copies[0].wait()
     partner, order = [], []
     for s in range(SLOTS):
-        partner.append((parent_ref[s] // SLOTS) % 4 ^ member)
+        partner.append((parent_ref[s] >> 3) & 3 ^ member)
         earlier = sum([(partner[e] == partner[s]).astype(I32) for e in range(s)], jnp.int32(0))
         order.append(jnp.minimum(earlier, 1))
     for copy in copies[1:4]:
@@ -69,7 +69,7 @@
         block = pl.multiple_of(partner[s] * 16 + order[s] * 8, 8)
         place_ref[pl.ds(block, GROUPED), :] = head_ref[pl.ds(s, GROUPED, stride=SLOTS), :]
         row = partner[s] * 16 + order[s]
-        cache_row = (parent_ref[s] % SLOTS).astype(F32)
+        cache_row = (parent_ref[s] & 7).astype(F32)
         slot = (member * SLOTS + s).astype(F32)
         info_ref[pl.ds(row, 1), :] = fresh_keys[s : s + 1]
         info_ref[pl.ds(row + 2, 1), :] = fresh_values[s : s + 1]
@@ -86,17 +86,17 @@
     limit_ref[...] = spread
 
 
-def attend_kernel(limit_ref, m0, m1, m2, m3, k_ref, v_ref, out_ref, s_ref, o_ref):
-    infos = [m[16:, :].astype(F32) for m in (m0, m1, m2, m3)]
-    heads = [m[:16, :].astype(F32) for m in (m0, m1, m2, m3)]
-    info_ints = [info.astype(I32) for info in infos]
+def attend_pairs(first, messages, limit_ref, k_ref, v_ref, s_ref, o_ref):
+    infos = [m[16:, :].astype(F32) for m in messages]
+    heads = [m[:16, :].astype(F32) for m in messages]
+    slots = range(2 * len(messages))
     cache_rows = [
-        jnp.clip(info_ints[i // 2][4 + i % 2, 0], 0, SLOTS - 1) for i in range(SLOTS)
+        jnp.clip(infos[i // 2].astype(I32)[4 + i % 2, 0], 0, SLOTS - 1) for i in slots
     ]
     scale = HEAD ** (-0.5)
     positions = lax.broadcasted_iota(I32, (GROUPED, POSITIONS), 1)
     new_scores = []
-    for i in range(SLOTS):
+    for i in slots:
         q = heads[i // 2][i % 2 * 8 : i % 2 * 8 + 8]
         fresh_key = infos[i // 2][i % 2 : i % 2 + 1]
         scores = lax.dot_general(
@@ -105,7 +105,7 @@
         limit = limit_ref[pl.ds(cache_rows[i], 1), :][:, :1]
         s_ref[i] = jnp.where(positions < limit, scores, -1e30)
         new_scores.append(jnp.sum(q * fresh_key, axis=1, keepdims=True) * scale)
-    for i in range(SLOTS):
+    for i in slots:
         scores = s_ref[i]
         maximum = jnp.maximum(jnp.max(scores, axis=1, keepdims=True), new_scores[i])
         weights = jnp.exp(scores - maximum)
@@ -116,8 +116,23 @@
         )
         fresh_value = infos[i // 2][2 + i % 2 : 3 + i % 2]
         weighted = weighted + new_weight.astype(BF16).astype(F32) * fresh_value
-        o_ref[pl.ds(i, GROUPED, stride=SLOTS), :] = weighted / denominator
-    ids = jnp.concatenate([info[6:8] for info in infos], axis=0)
+        o_ref[pl.ds(first + i, GROUPED, stride=SLOTS), :] = weighted / denominator
+
+
+def attend_near_kernel(limit_ref, m0, m1, k_ref, v_ref, o_ref, s_ref):
+    o_ref[...] = jnp.zeros_like(o_ref)
+    attend_pairs(0, (m0, m1), limit_ref, k_ref, v_ref, s_ref, o_ref)
+
+
+def attend_next_kernel(limit_ref, before_ref, m2, k_ref, v_ref, o_ref, s_ref):
+    o_ref[...] = before_ref[...]
+    attend_pairs(4, (m2,), limit_ref, k_ref, v_ref, s_ref, o_ref)
+
+
+def attend_far_kernel(limit_ref, before_ref, m0, m1, m2, m3, k_ref, v_ref, out_ref, s_ref, o_ref):
+    o_ref[...] = before_ref[...]
+    attend_pairs(6, (m3,), limit_ref, k_ref, v_ref, s_ref, o_ref)
+    ids = jnp.concatenate([m[16:, :].astype(F32)[6:8] for m in (m0, m1, m2, m3)], axis=0)
     block = jnp.concatenate(
         [o_ref[h * SLOTS : (h + 1) * SLOTS, :] for h in range(GROUPED)] + [ids], axis=1
     )
@@ -165,24 +180,38 @@
             pltpu.VMEM((64, HEAD), F32),
             pltpu.SemaphoreType.DMA((5,)),
         ],
+        compiler_params=pltpu.CompilerParams(vmem_limit_bytes=4 * MIB),
         cost_estimate=pl.CostEstimate(flops=2 * 10**10, bytes_accessed=0, transcendentals=0),
         name="pack",
     )(*[in_hbm(x) for x in operands])
 
 
-def attend(limits, messages, key_cache, value_cache):
-    return pl.pallas_call(
-        attend_kernel,
+def attend_early(kernel, slots, name, *operands):
+    return pl.pallas_call(
+        kernel,
+        out_shape=jax.ShapeDtypeStruct((GROUPED * SLOTS, HEAD), F32),
+        in_specs=[VMEM] * len(operands),
+        out_specs=VMEM,
+        scratch_shapes=[pltpu.VMEM((slots, GROUPED, POSITIONS), F32)],
+        compiler_params=pltpu.CompilerParams(vmem_limit_bytes=16 * MIB),
+        cost_estimate=pl.CostEstimate(flops=2 * 10**9, bytes_accessed=0, transcendentals=0),
+        name=name,
+    )(*operands)
+
+
+def attend_far(*operands):
+    return pl.pallas_call(
+        attend_far_kernel,
         out_shape=jax.ShapeDtypeStruct((16 * SLOTS, OUT_COLS), BF16),
-        in_specs=[VMEM] * 7,
+        in_specs=[VMEM] * len(operands),
         out_specs=VMEM,
         scratch_shapes=[
-            pltpu.VMEM((SLOTS, GROUPED, POSITIONS), F32),
+            pltpu.VMEM((2, GROUPED, POSITIONS), F32),
             pltpu.VMEM((GROUPED * SLOTS, HEAD), F32),
         ],
-        compiler_params=pltpu.CompilerParams(vmem_limit_bytes=24 * MIB),
-        name="attend",
-    )(limits, *messages, *[x.reshape(SLOTS, POSITIONS, HEAD) for x in (key_cache, value_cache)])
+        compiler_params=pltpu.CompilerParams(vmem_limit_bytes=16 * MIB),
+        name="attend_far",
+    )(*operands)
 
 
 def body(parents, lengths, queries, token_keys, token_values, key_cache, value_cache, weight):
@@ -190,7 +219,11 @@
     arrived = [
         lax.ppermute(messages[d], BEAM_AXES, [(i, i ^ d) for i in range(32)]) for d in (1, 2, 3)
     ]
-    heads = attend(limits, [messages[0]] + arrived, key_cache, value_cache)
+    caches = [x.reshape(SLOTS, POSITIONS, HEAD) for x in (key_cache, value_cache)]
+    m0, m1, m2, m3 = [messages[0]] + arrived
+    part = attend_early(attend_near_kernel, 4, "attend_near", limits, m0, m1, *caches)
+    part = attend_early(attend_next_kernel, 2, "attend_next", limits, part, m2, *caches)
+    heads = attend_far(limits, part, m0, m1, m2, m3, *caches)
     gathered = lax.all_to_all(heads, ("x", "y"), 0, 0, tiled=True)
     other = lax.ppermute(gathered, BEAM_AXES, [(i, i ^ 1) for i in range(32)])
     terms, place = pl.pallas_call(

time: 47.6 us -> 42.1 us (0.88)
  local copies, waits for them, and re-layouts: 4.38 us -> 0.01 us
  waiting for transfers between devices: 2.83 us -> 1.22 us
  Pallas kernels: 3.81 us -> 4.43 us
    unnamed x6, local copies, waits for them, and re-layouts: 4.38 us -> 0.01 us
    ppermute x3, waiting for transfers between devices: 1.62 us -> 0.01 us  [body(): lax.ppermute(messages[d], BEAM_AXES, [(i, i ^ d) for i in range(32)])]
    pallas_call x1 -> x3, Pallas kernels: 1.83 us -> 2.38 us  [the longest x2 1.65 us: attend_early(): pl.pallas_call(kernel, out_shape=jax.ShapeDtypeStruct((GROUPED * SLOTS, H...]
  transfers between devices with their start and end apart: 4 -> 4, of which waited for: 3 -> 1; matrix products, arithmetic and copies ran while one was open for 0% -> 0% of each run, Pallas kernels for 0% -> 4%
where the time goes in v5:
time: 42.1 us; the launch traced here: 41.9 us
  blocking collectives  29.1 us (69%)
  starting transfers between devices  7.1 us (17%)
  Pallas kernels  4.43 us (11%)
  waiting for transfers between devices  1.22 us (3%)
    all_to_all x1, blocking collectives, body(): shares = lax.all_to_all(terms, 'tensor', 0, 0, tiled=True)  15.9 us
    all_to_all x1, blocking collectives, body(): gathered = lax.all_to_all(heads, ('x', 'y'), 0, 0, tiled=True)  13.2 us
    ppermute x3, starting transfers between devices, body(): lax.ppermute(messages[d], BEAM_AXES, [(i, i ^ d) for i in range(32)])  5.06 us
    ppermute x1, starting transfers between devices, body(): other = lax.ppermute(gathered, BEAM_AXES, [(i, i ^ 1) for i in range(32)])  2.05 us
    pallas_call x2, Pallas kernels, attend_early(): pl.pallas_call(kernel, out_shape=jax.ShapeDtypeStruct((GROUPED * SLOTS, H...  1.65 us
    ppermute x1, waiting for transfers between devices, body(): other = lax.ppermute(gathered, BEAM_AXES, [(i, i ^ 1) for i in range(32)])  1.21 us
    pallas_call x1, Pallas kernels, pack(): pl.pallas_call(pack_kernel, out_shape=(message,) * 4 + (pltpu.VMEM((SLOTS...  0.97 us
  transfers between devices with their start and end apart: 4, of which 1 were waited for; matrix products, arithmetic and copies ran while one was open for 0% of the time, Pallas kernels for 4%

profile of v5, /device:TPU:1, one launch (start us, length us, event | category | flops | bytes accessed | tf_op | source)
XLA Modules:
  0.0 41.9 jit_solution(8601310389169594604)
XLA Ops:
  0.0 0.0 copy-start.1
  0.0 0.0 copy-start
  0.0 1.0 %pack.1 = (bf16[32,128]{1,0:T(8,128)(2,1)S(1)}, bf16[32,128]{1,0:T(8,128)(2,1)S(1)}, bf16[32,128]{1,0:T(8,128)(2,1)S(1)}, bf16[32,128]{1,0:T(8,128)(2,1)S(1)}, s32[8,128]{1,0:T(8,128)S(1)}) custom-call(s32[8]{0:T(128)} %parent_hbm.1, s32[8]{0:T(128)} %len_hbm.1, bf16[8,1024]{1,0:T(8,128)(2,1)} %q_hbm.1, bf16[8,128]{1,0:T(8,128)(2,1)} %key_hbm.1, ...), custom_call_target="tpu_custom_call" | custom-call | flops 20000000000 | tf_op jit(solution)/shard_map/pack/pallas_call | solution.py:167
  1.0 3.3 %collective-permute-start = (bf16[32,128]{1,0:T(8,128)(2,1)S(1)}, bf16[32,128]{1,0:T(8,128)(2,1)S(1)}, u32[]{:S(2)}, u32[]{:S(2)}) collective-permute-start(bf16[32,128]{1,0:T(8,128)(2,1)S(1)} %get-tuple-element.14), channel_id=1, source_target_pairs={{0,8},{8,0},{16,24},{24,16},{32,40},{40,32},{48,56},{56,48},{64,72... | collective-permute-start | bytes 24584 | tf_op jit(solution)/shard_map/ppermute | solution.py:220
  4.3 0.0 collective-permute-start.1
  4.3 1.7 %collective-permute-start.2 = (bf16[32,128]{1,0:T(8,128)(2,1)S(1)}, bf16[32,128]{1,0:T(8,128)(2,1)S(1)}, u32[]{:S(2)}, u32[]{:S(2)}) collective-permute-start(bf16[32,128]{1,0:T(8,128)(2,1)S(1)} %get-tuple-element.16), channel_id=1, source_target_pairs={{0,24},{8,16},{16,8},{24,0},{32,56},{40,48},{48,40},{56,32},{64,88... | collective-permute-start | bytes 24584 | tf_op jit(solution)/shard_map/ppermute | solution.py:220
  6.0 0.0 collective-permute-done.m1
  6.0 0.0 copy-done.1
  6.0 0.0 copy-done
  6.1 1.0 %attend_near.1.before_ref = f32[64,128]{1,0:T(8,128)S(1)} custom-call(s32[8,128]{1,0:T(8,128)S(1)} %get-tuple-element.12.limit_ref, bf16[32,128]{1,0:T(8,128)(2,1)S(1)} %get-tuple-element.13.m0, bf16[32,128]{1,0:T(8,128)(2,1)S(1)} %collective-permute-done.m1, bf16[8,2048,128]{2,1,0:T(8,128)(2,1)S(1)} %bitcast.6, bf16[8,2048,128]{2,1,0:T(8,128)(2,1)S(1)} %bitcast.9), custom_call_target="tpu_custom_call" | custom-call | flops 2000000000 | tf_op jit(solution)/shard_map/attend_near/pallas_call | solution.py:190
  7.0 0.0 collective-permute-done.1.m2
  7.0 0.7 %attend_next.1.before_ref = f32[64,128]{1,0:T(8,128)S(1)} custom-call(s32[8,128]{1,0:T(8,128)S(1)} %get-tuple-element.12.limit_ref, f32[64,128]{1,0:T(8,128)S(1)} %attend_near.1.before_ref, bf16[32,128]{1,0:T(8,128)(2,1)S(1)} %collective-permute-done.1.m2, bf16[8,2048,128]{2,1,0:T(8,128)(2,1)S(1)} %bitcast.7, bf16[8,2048,128]{2,1,0:T(8,128)(2,1)S(1)} %bitcast.10), custom_call_target="tpu_custom_call" | custom-call | flops 2000000000 | tf_op jit(solution)/shard_map/attend_next/pallas_call | solution.py:190
  7.7 0.0 copy-start.2
  7.7 0.0 collective-permute-done.2.m3
  7.7 0.7 %attend_far.1 = bf16[128,1152]{1,0:T(8,128)(2,1)S(1)} custom-call(s32[8,128]{1,0:T(8,128)S(1)} %get-tuple-element.12.limit_ref, f32[64,128]{1,0:T(8,128)S(1)} %attend_next.1.before_ref, bf16[32,128]{1,0:T(8,128)(2,1)S(1)} %get-tuple-element.13.m0, bf16[32,128]{1,0:T(8,128)(2,1)S(1)} %collective-permute-done.m1, ...), custom_call_target="tpu_custom_call" | custom-call | tf_op jit(solution)/shard_map/attend_far/pallas_call | solution.py:203
  8.5 13.2 %all_to_all.22 = bf16[16,8,1152]{2,1,0:T(8,128)(2,1)S(1)} all-to-all(bf16[16,8,1152]{2,1,0:T(8,128)(2,1)S(1)} %bitcast.12), channel_id=1, replica_groups=mesh['x'=4,'y'=4,'core'=2,'tensor'=8] {'x','y'}, dimensions={0} | all-to-all | bytes 589824 | tf_op jit(solution)/shard_map/all_to_all | solution.py:227
  21.7 2.0 %collective-permute-start.3 = (bf16[128,1152]{1,0:T(8,128)(2,1)S(1)}, bf16[128,1152]{1,0:T(8,128)(2,1)S(1)}, u32[]{:S(2)}, u32[]{:S(2)}) collective-permute-start(bf16[128,1152]{1,0:T(8,128)(2,1)S(1)} %bitcast.13), channel_id=1, source_target_pairs={{0,8},{8,0},{16,24},{24,16},{32,40},{40,32},{48,56},{56,48},{64,72... | collective-permute-start | bytes 884744 | tf_op jit(solution)/shard_map/ppermute | solution.py:228
  23.7 1.2 %collective-permute-done.3.other_ref = bf16[128,1152]{1,0:T(8,128)(2,1)S(1)} collective-permute-done((bf16[128,1152]{1,0:T(8,128)(2,1)S(1)}, bf16[128,1152]{1,0:T(8,128)(2,1)S(1)}, u32[]{:S(2)}, u32[]{:S(2)}) %collective-permute-start.3) | collective-permute-done | bytes 294944 | tf_op jit(solution)/shard_map/ppermute | solution.py:228
  24.9 0.0 copy-done.2
  25.0 0.3 project.1
  25.3 15.9 %all_to_all.23 = bf16[8,32,256]{2,1,0:T(8,128)(2,1)S(1)} all-to-all(bf16[8,32,256]{2,1,0:T(8,128)(2,1)S(1)} %bitcast.16), channel_id=1, replica_groups=mesh['x'=4,'y'=4,'core'=2,'tensor'=8] {'tensor'}, dimensions={0} | all-to-all | bytes 262144 | tf_op jit(solution)/shard_map/all_to_all | solution.py:240
  41.2 0.8 %finish.1 = bf16[32,256]{1,0:T(8,128)(2,1)} custom-call(bf16[256,256]{1,0:T(8,128)(2,1)S(1)} %bitcast.15, bf16[32,128]{1,0:T(8,128)(2,1)S(1)} %get-tuple-element.18.place_ref), custom_call_target="tpu_custom_call" | custom-call | tf_op jit(solution)/shard_map/finish/pallas_call | solution.py:241
Async XLA Ops:
  0.0 6.0 %copy-start.1 = (bf16[8,1,2048,128]{3,2,1,0:T(8,128)(2,1)S(1)}, bf16[8,1,2048,128]{3,2,1,0:T(8,128)(2,1)}, u32[]{:S(2)}) copy-start(bf16[8,1,2048,128]{3,2,1,0:T(8,128)(2,1)} %param.14) | copy-start | bytes 12582916
  0.0 6.0 %copy-start = (bf16[8,1,2048,128]{3,2,1,0:T(8,128)(2,1)S(1)}, bf16[8,1,2048,128]{3,2,1,0:T(8,128)(2,1)}, u32[]{:S(2)}) copy-start(bf16[8,1,2048,128]{3,2,1,0:T(8,128)(2,1)} %param.13) | copy-start | bytes 12582916
  1.0 5.1 %collective-permute-start = (bf16[32,128]{1,0:T(8,128)(2,1)S(1)}, bf16[32,128]{1,0:T(8,128)(2,1)S(1)}, u32[]{:S(2)}, u32[]{:S(2)}) collective-permute-start(bf16[32,128]{1,0:T(8,128)(2,1)S(1)} %get-tuple-element.14), channel_id=1, source_target_pairs={{0,8},{8,0},{16,24},{24,16},{32,40},{40,32},{48,56},{56,48},{64,72... | collective-permute-start | bytes 24584 | tf_op jit(solution)/shard_map/ppermute | solution.py:220
  4.3 2.7 %collective-permute-start.1 = (bf16[32,128]{1,0:T(8,128)(2,1)S(1)}, bf16[32,128]{1,0:T(8,128)(2,1)S(1)}, u32[]{:S(2)}, u32[]{:S(2)}) collective-permute-start(bf16[32,128]{1,0:T(8,128)(2,1)S(1)} %get-tuple-element.15), channel_id=1, source_target_pairs={{0,16},{8,24},{16,0},{24,8},{32,48},{40,56},{48,32},{56,40},{64,80... | collective-permute-start | bytes 24584 | tf_op jit(solution)/shard_map/ppermute | solution.py:220
  4.3 3.4 %collective-permute-start.2 = (bf16[32,128]{1,0:T(8,128)(2,1)S(1)}, bf16[32,128]{1,0:T(8,128)(2,1)S(1)}, u32[]{:S(2)}, u32[]{:S(2)}) collective-permute-start(bf16[32,128]{1,0:T(8,128)(2,1)S(1)} %get-tuple-element.16), channel_id=1, source_target_pairs={{0,24},{8,16},{16,8},{24,0},{32,56},{40,48},{48,40},{56,32},{64,88... | collective-permute-start | bytes 24584 | tf_op jit(solution)/shard_map/ppermute | solution.py:220
  7.7 17.2 %copy-start.2 = (bf16[1024,256]{1,0:T(8,128)(2,1)S(1)}, bf16[1024,256]{1,0:T(8,128)(2,1)}, u32[]{:S(2)}) copy-start(bf16[1024,256]{1,0:T(8,128)(2,1)} %w_ref.1) | copy-start | bytes 1572868
  21.7 3.3 %collective-permute-start.3 = (bf16[128,1152]{1,0:T(8,128)(2,1)S(1)}, bf16[128,1152]{1,0:T(8,128)(2,1)S(1)}, u32[]{:S(2)}, u32[]{:S(2)}) collective-permute-start(bf16[128,1152]{1,0:T(8,128)(2,1)S(1)} %bitcast.13), channel_id=1, source_target_pairs={{0,8},{8,0},{16,24},{24,16},{32,40},{40,32},{48,56},{56,48},{64,72... | collective-permute-start | bytes 884744 | tf_op jit(solution)/shard_map/ppermute | solution.py:228

commit v6 on v5

--- a/solution.py
+++ b/solution.py
@@ -3,7 +3,6 @@
 from jax import lax
 from jax.experimental import pallas as pl
 from jax.experimental.pallas import tpu as pltpu
-from jax.sharding import Mesh
 from jax.sharding import PartitionSpec as P
 
 HEAD = 128
@@ -14,7 +13,10 @@
 Q_COLS = GROUPED * HEAD
 OUT_COLS = Q_COLS + HEAD
 PACKED = 32
-BEAM_AXES = ("x", "y", "core")
+BEAM_AXES = "beam"
+QUERY_ORDER = (7, 6, 5, 4, 3, 2, 1, 0)
+PLANE_ORDER = (4, 5, 6, 7, 0, 1, 2, 3)
+CHIP_GROUPS = [[4 * q + 2 * p + c for q in QUERY_ORDER for p in (1, 0)] for c in range(2)]
 F32 = jnp.float32
 BF16 = jnp.bfloat16
 I32 = jnp.int32
@@ -28,7 +30,7 @@
 
 
 def beam_index():
-    return (lax.axis_index("x") * 4 + lax.axis_index("y")) * 2 + lax.axis_index("core")
+    return lax.axis_index("beam")
 
 
 def transposed_dot(a, b):
@@ -52,12 +54,6 @@
         copy.start()
     info_ref[...] = jnp.zeros_like(info_ref)
     member = beam_index() & 3
-    copies[0].wait()
-    partner, order = [], []
-    for s in range(SLOTS):
-        partner.append((parent_ref[s] >> 3) & 3 ^ member)
-        earlier = sum([(partner[e] == partner[s]).astype(I32) for e in range(s)], jnp.int32(0))
-        order.append(jnp.minimum(earlier, 1))
     for copy in copies[1:4]:
         copy.wait()
     queries = q_ref[...].astype(F32)
@@ -65,6 +61,17 @@
         head_ref[h * SLOTS : (h + 1) * SLOTS, :] = queries[:, h * HEAD : (h + 1) * HEAD]
     fresh_keys = key_ref[...].astype(F32)
     fresh_values = value_ref[...].astype(F32)
+    copies[0].wait()
+    copies[4].wait()
+    partner, order = [], []
+    for s in range(SLOTS):
+        partner.append((parent_ref[s] >> 3) & 3 ^ member)
+        earlier = jnp.int32(0)
+        for e in range(s):
+            earlier = jnp.where(partner[e] == partner[s], 1, earlier)
+        order.append(earlier)
+    rows = lax.broadcasted_iota(I32, (SLOTS, HEAD), 0)
+    spread = jnp.zeros((SLOTS, HEAD), I32)
     for s in range(SLOTS):
         block = pl.multiple_of(partner[s] * 16 + order[s] * 8, 8)
         place_ref[pl.ds(block, GROUPED), :] = head_ref[pl.ds(s, GROUPED, stride=SLOTS), :]
@@ -75,15 +82,11 @@
         info_ref[pl.ds(row + 2, 1), :] = fresh_values[s : s + 1]
         info_ref[pl.ds(row + 4, 1), :] = jnp.full((1, HEAD), cache_row, F32)
         info_ref[pl.ds(row + 6, 1), :] = jnp.full((1, HEAD), slot, F32)
+        spread = jnp.where(rows == s, len_ref[s], spread)
+    limit_ref[...] = spread
     for j, out_ref in enumerate((m0, m1, m2, m3)):
         out_ref[:16, :] = place_ref[j * 16 : j * 16 + 16, :].astype(BF16)
         out_ref[16:, :] = info_ref[j * 16 : j * 16 + 16, :].astype(BF16)
-    copies[4].wait()
-    rows = lax.broadcasted_iota(I32, (SLOTS, HEAD), 0)
-    spread = jnp.zeros((SLOTS, HEAD), I32)
-    for r in range(SLOTS):
-        spread = jnp.where(rows == r, len_ref[r], spread)
-    limit_ref[...] = spread
 
 
 def attend_pairs(first, messages, limit_ref, k_ref, v_ref, s_ref, o_ref):
@@ -141,17 +144,34 @@
         out_ref[j * 16 : (j + 1) * 16, :] = pair
 
 
-def project_kernel(own_ref, other_ref, w_ref, out_ref, place_ref):
-    weight = w_ref[...]
-    for part, ref in enumerate((own_ref, other_ref)):
-        terms = jnp.dot(ref[:, :Q_COLS], weight, preferred_element_type=F32).astype(BF16)
-        for g in range(8):
-            out_ref[g * 32 + part * 16 : g * 32 + part * 16 + 16, :] = terms[g * 16 : g * 16 + 16]
-    first = pl.multiple_of(lax.axis_index("tensor") * 16, 16)
+def project_half(part, rows_ref, w_ref, out_ref):
+    terms = jnp.dot(rows_ref[:, :Q_COLS], w_ref[...], preferred_element_type=F32).astype(BF16)
+    for q in range(8):
+        source = QUERY_ORDER.index(q) * 16
+        target = PLANE_ORDER.index(q) * 32 + part * 16
+        out_ref[target : target + 16, :] = terms[source : source + 16]
+
+
+def place_half(rows_ref):
+    query = lax.axis_index("tensor")
+    place = jnp.int32(0)
+    for q in range(8):
+        place = jnp.where(query == q, QUERY_ORDER.index(q), place)
+    first = pl.multiple_of(place * 16, 16)
     lanes = lax.broadcasted_iota(I32, (16, HEAD), 1)
-    for part, ref in enumerate((own_ref, other_ref)):
-        ids = ref[pl.ds(first, 16), Q_COLS:].astype(F32).astype(I32)
-        place_ref[part * 16 : part * 16 + 16, :] = (ids == lanes).astype(F32).astype(BF16)
+    ids = rows_ref[pl.ds(first, 16), Q_COLS:].astype(F32).astype(I32)
+    return (ids == lanes).astype(F32).astype(BF16)
+
+
+def project_own_kernel(rows_ref, w_ref, out_ref, place_ref):
+    project_half(0, rows_ref, w_ref, out_ref)
+    place_ref[:16, :] = place_half(rows_ref)
+    place_ref[16:, :] = jnp.zeros((16, HEAD), BF16)
+
+
+def project_other_kernel(rows_ref, w_ref, own_ref, own_place_ref, out_ref, place_ref):
+    project_half(1, rows_ref, w_ref, out_ref)
+    place_ref[16:, :] = place_half(rows_ref)
 
 
 def finish_kernel(terms_ref, place_ref, out_ref):
@@ -224,20 +244,31 @@
     part = attend_early(attend_near_kernel, 4, "attend_near", limits, m0, m1, *caches)
     part = attend_early(attend_next_kernel, 2, "attend_next", limits, part, m2, *caches)
     heads = attend_far(limits, part, m0, m1, m2, m3, *caches)
-    gathered = lax.all_to_all(heads, ("x", "y"), 0, 0, tiled=True)
+    gathered = lax.all_to_all(heads, "beam", 0, 0, axis_index_groups=CHIP_GROUPS, tiled=True)
     other = lax.ppermute(gathered, BEAM_AXES, [(i, i ^ 1) for i in range(32)])
+    shapes = (pltpu.VMEM((256, 256), BF16), pltpu.VMEM((BEAMS, HEAD), BF16))
+    params = pltpu.CompilerParams(vmem_limit_bytes=16 * MIB)
+    own = pl.pallas_call(
+        project_own_kernel,
+        out_shape=shapes,
+        in_specs=[VMEM] * 2,
+        out_specs=(VMEM, VMEM),
+        compiler_params=params,
+        cost_estimate=pl.CostEstimate(flops=2 * 10**9, bytes_accessed=0, transcendentals=0),
+        name="project_own",
+    )(gathered, weight)
     terms, place = pl.pallas_call(
-        project_kernel,
-        out_shape=(
-            jax.ShapeDtypeStruct((256, 256), BF16),
-            jax.ShapeDtypeStruct((BEAMS, HEAD), BF16),
-        ),
-        in_specs=[VMEM] * 3,
+        project_other_kernel,
+        out_shape=shapes,
+        in_specs=[VMEM] * 4,
         out_specs=(VMEM, VMEM),
-        compiler_params=pltpu.CompilerParams(vmem_limit_bytes=16 * MIB),
-        name="project",
-    )(gathered, other, weight)
-    shares = lax.all_to_all(terms, "tensor", 0, 0, tiled=True)
+        input_output_aliases={2: 0, 3: 1},
+        compiler_params=params,
+        name="project_other",
+    )(other, weight, *own)
+    shares = lax.all_to_all(
+        terms, "tensor", 0, 0, axis_index_groups=[list(PLANE_ORDER)], tiled=True
+    )
     return pl.pallas_call(
         finish_kernel,
         out_shape=jax.ShapeDtypeStruct((BEAMS, 256), BF16),
@@ -249,7 +280,6 @@
 
 
 def solution(mesh):
-    fine = Mesh(mesh.devices.reshape(4, 4, 2, 8), ("x", "y", "core", "tensor"))
     in_specs = (
         P(BEAM_AXES),
         P(BEAM_AXES),
@@ -261,4 +291,4 @@
         P("tensor", BEAM_AXES),
     )
     out_specs = P("tensor", BEAM_AXES)
-    return jax.shard_map(body, mesh=fine, in_specs=in_specs, out_specs=out_specs, check_vma=False)
+    return jax.shard_map(body, mesh=mesh, in_specs=in_specs, out_specs=out_specs, check_vma=False)

time: 42.1 us -> 36.2 us (0.86)
  blocking collectives: 29.1 us -> 23.4 us
    all_to_all x2, blocking collectives: 29.1 us -> 23.4 us  [the longest x1 12.5 us: body(): lax.all_to_all(terms, 'tensor', 0, 0, axis_index_groups=[list(PLANE_ORDER...]
  transfers between devices with their start and end apart: 4 -> 4, of which waited for: 1 -> 1; matrix products, arithmetic and copies ran while one was open for 0% -> 0% of each run, Pallas kernels for 4% -> 5%
where the time goes in v6:
time: 36.2 us; the launch traced here: 36 us
  blocking collectives  23.4 us (65%)
  starting transfers between devices  6.99 us (19%)
  Pallas kernels  4.63 us (13%)
  waiting for transfers between devices  0.97 us (3%)
    all_to_all x1, blocking collectives, body(): lax.all_to_all(terms, 'tensor', 0, 0, axis_index_groups=[list(PLANE_ORDER...  12.5 us
    all_to_all x1, blocking collectives, body(): lax.all_to_all(heads, 'beam', 0, 0, axis_index_groups=CHIP_GROUPS, tiled=...  10.9 us
    ppermute x3, starting transfers between devices, body(): lax.ppermute(messages[d], BEAM_AXES, [(i, i ^ d) for i in range(32)])  5.06 us
    ppermute x1, starting transfers between devices, body(): other = lax.ppermute(gathered, BEAM_AXES, [(i, i ^ 1) for i in range(32)])  1.93 us
    pallas_call x2, Pallas kernels, attend_early(): pl.pallas_call(kernel, out_shape=jax.ShapeDtypeStruct((GROUPED * SLOTS, H...  1.65 us
    pallas_call x1, Pallas kernels, pack(): pl.pallas_call(pack_kernel, out_shape=(message,) * 4 + (pltpu.VMEM((SLOTS...  1 us
    ppermute x1, waiting for transfers between devices, body(): other = lax.ppermute(gathered, BEAM_AXES, [(i, i ^ 1) for i in range(32)])  0.96 us
    pallas_call x1, Pallas kernels, body(): pl.pallas_call(finish_kernel, out_shape=jax.ShapeDtypeStruct((BEAMS, 256)...  0.78 us
  transfers between devices with their start and end apart: 4, of which 1 were waited for; matrix products, arithmetic and copies ran while one was open for 0% of the time, Pallas kernels for 5%

profile of v6, /device:TPU:1, one launch (start us, length us, event | category | flops | bytes accessed | tf_op | source)
XLA Modules:
  0.0 36.0 jit_solution(8872063728209864031)
XLA Ops:
  0.0 0.0 copy-start
  0.0 0.0 copy-start.1
  0.0 1.0 %pack.1 = (bf16[32,128]{1,0:T(8,128)(2,1)S(1)}, bf16[32,128]{1,0:T(8,128)(2,1)S(1)}, bf16[32,128]{1,0:T(8,128)(2,1)S(1)}, bf16[32,128]{1,0:T(8,128)(2,1)S(1)}, s32[8,128]{1,0:T(8,128)S(1)}) custom-call(s32[8]{0:T(128)} %parent_hbm.1, s32[8]{0:T(128)} %len_hbm.1, bf16[8,1024]{1,0:T(8,128)(2,1)} %q_hbm.1, bf16[8,128]{1,0:T(8,128)(2,1)} %key_hbm.1, ...), custom_call_target="tpu_custom_call" | custom-call | flops 20000000000 | tf_op jit(solution)/shard_map/pack/pallas_call | solution.py:187
  1.0 3.3 %collective-permute-start = (bf16[32,128]{1,0:T(8,128)(2,1)S(1)}, bf16[32,128]{1,0:T(8,128)(2,1)S(1)}, u32[]{:S(2)}, u32[]{:S(2)}) collective-permute-start(bf16[32,128]{1,0:T(8,128)(2,1)S(1)} %get-tuple-element.16), channel_id=1, source_target_pairs={{0,8},{8,0},{16,24},{24,16},{32,40},{40,32},{48,56},{56,48},{64,72... | collective-permute-start | bytes 24584 | tf_op jit(solution)/shard_map/ppermute | solution.py:240
  4.3 0.0 collective-permute-start.1
  4.3 1.7 %collective-permute-start.2 = (bf16[32,128]{1,0:T(8,128)(2,1)S(1)}, bf16[32,128]{1,0:T(8,128)(2,1)S(1)}, u32[]{:S(2)}, u32[]{:S(2)}) collective-permute-start(bf16[32,128]{1,0:T(8,128)(2,1)S(1)} %get-tuple-element.18), channel_id=1, source_target_pairs={{0,24},{8,16},{16,8},{24,0},{32,56},{40,48},{48,40},{56,32},{64,88... | collective-permute-start | bytes 24584 | tf_op jit(solution)/shard_map/ppermute | solution.py:240
  6.1 0.0 collective-permute-done.m1
  6.1 0.0 copy-done
  6.1 0.0 copy-done.1
  6.1 1.0 %attend_near.1.before_ref = f32[64,128]{1,0:T(8,128)S(1)} custom-call(s32[8,128]{1,0:T(8,128)S(1)} %get-tuple-element.14.limit_ref, bf16[32,128]{1,0:T(8,128)(2,1)S(1)} %get-tuple-element.15.m0, bf16[32,128]{1,0:T(8,128)(2,1)S(1)} %collective-permute-done.m1, bf16[8,2048,128]{2,1,0:T(8,128)(2,1)S(1)} %bitcast.6, bf16[8,2048,128]{2,1,0:T(8,128)(2,1)S(1)} %bitcast.9), custom_call_target="tpu_custom_call" | custom-call | flops 2000000000 | tf_op jit(solution)/shard_map/attend_near/pallas_call | solution.py:210
  7.0 0.0 collective-permute-done.1.m2
  7.1 0.7 %attend_next.1.before_ref = f32[64,128]{1,0:T(8,128)S(1)} custom-call(s32[8,128]{1,0:T(8,128)S(1)} %get-tuple-element.14.limit_ref, f32[64,128]{1,0:T(8,128)S(1)} %attend_near.1.before_ref, bf16[32,128]{1,0:T(8,128)(2,1)S(1)} %collective-permute-done.1.m2, bf16[8,2048,128]{2,1,0:T(8,128)(2,1)S(1)} %bitcast.7, bf16[8,2048,128]{2,1,0:T(8,128)(2,1)S(1)} %bitcast.10), custom_call_target="tpu_custom_call" | custom-call | flops 2000000000 | tf_op jit(solution)/shard_map/attend_next/pallas_call | solution.py:210
  7.7 0.0 copy-start.2
  7.7 0.0 collective-permute-done.2.m3
  7.8 0.7 %attend_far.1 = bf16[128,1152]{1,0:T(8,128)(2,1)S(1)} custom-call(s32[8,128]{1,0:T(8,128)S(1)} %get-tuple-element.14.limit_ref, f32[64,128]{1,0:T(8,128)S(1)} %attend_next.1.before_ref, bf16[32,128]{1,0:T(8,128)(2,1)S(1)} %get-tuple-element.15.m0, bf16[32,128]{1,0:T(8,128)(2,1)S(1)} %collective-permute-done.m1, ...), custom_call_target="tpu_custom_call" | custom-call | tf_op jit(solution)/shard_map/attend_far/pallas_call | solution.py:223
  8.5 10.9 %all_to_all.22 = bf16[16,8,1152]{2,1,0:T(8,128)(2,1)S(1)} all-to-all(bf16[16,8,1152]{2,1,0:T(8,128)(2,1)S(1)} %bitcast.12), channel_id=1, replica_groups={{240,224,208,192,176,160,144,128,112,96,80,64,48,32,16,0},{248,232,216,..., dimensions={0} | all-to-all | bytes 589824 | tf_op jit(solution)/shard_map/all_to_all | solution.py:247
  19.4 1.9 %collective-permute-start.3 = (bf16[128,1152]{1,0:T(8,128)(2,1)S(1)}, bf16[128,1152]{1,0:T(8,128)(2,1)S(1)}, u32[]{:S(2)}, u32[]{:S(2)}) collective-permute-start(bf16[128,1152]{1,0:T(8,128)(2,1)S(1)} %bitcast.15), channel_id=1, source_target_pairs={{0,8},{8,0},{16,24},{24,16},{32,40},{40,32},{48,56},{56,48},{64,72... | collective-permute-start | bytes 884744 | tf_op jit(solution)/shard_map/ppermute | solution.py:248
  21.3 0.0 copy-done.2
  21.3 0.2 project_own.1
  21.5 1.0 %collective-permute-done.3.rows_ref = bf16[128,1152]{1,0:T(8,128)(2,1)S(1)} collective-permute-done((bf16[128,1152]{1,0:T(8,128)(2,1)S(1)}, bf16[128,1152]{1,0:T(8,128)(2,1)S(1)}, u32[]{:S(2)}, u32[]{:S(2)}) %collective-permute-start.3) | collective-permute-done | bytes 294944 | tf_op jit(solution)/shard_map/ppermute | solution.py:248
  22.5 0.2 project_other.1
  22.7 12.5 %all_to_all.23 = bf16[8,32,256]{2,1,0:T(8,128)(2,1)S(1)} all-to-all(bf16[8,32,256]{2,1,0:T(8,128)(2,1)S(1)} %bitcast.14), channel_id=1, replica_groups={{4,5,6,7,0,1,2,3},{12,13,14,15,8,9,10,11},{20,21,22,23,16,17,18,19},{28..., dimensions={0} | all-to-all | bytes 262144 | tf_op jit(solution)/shard_map/all_to_all | solution.py:269
  35.3 0.8 %finish.1 = bf16[32,256]{1,0:T(8,128)(2,1)} custom-call(bf16[256,256]{1,0:T(8,128)(2,1)S(1)} %bitcast.13, bf16[32,128]{1,0:T(8,128)(2,1)S(1)} %get-tuple-element.22.place_ref), custom_call_target="tpu_custom_call" | custom-call | tf_op jit(solution)/shard_map/finish/pallas_call | solution.py:272
Async XLA Ops:
  0.0 6.1 %copy-start = (bf16[8,1,2048,128]{3,2,1,0:T(8,128)(2,1)S(1)}, bf16[8,1,2048,128]{3,2,1,0:T(8,128)(2,1)}, u32[]{:S(2)}) copy-start(bf16[8,1,2048,128]{3,2,1,0:T(8,128)(2,1)} %param.13) | copy-start | bytes 12582916
  0.0 6.1 %copy-start.1 = (bf16[8,1,2048,128]{3,2,1,0:T(8,128)(2,1)S(1)}, bf16[8,1,2048,128]{3,2,1,0:T(8,128)(2,1)}, u32[]{:S(2)}) copy-start(bf16[8,1,2048,128]{3,2,1,0:T(8,128)(2,1)} %param.14) | copy-start | bytes 12582916
  1.0 5.1 %collective-permute-start = (bf16[32,128]{1,0:T(8,128)(2,1)S(1)}, bf16[32,128]{1,0:T(8,128)(2,1)S(1)}, u32[]{:S(2)}, u32[]{:S(2)}) collective-permute-start(bf16[32,128]{1,0:T(8,128)(2,1)S(1)} %get-tuple-element.16), channel_id=1, source_target_pairs={{0,8},{8,0},{16,24},{24,16},{32,40},{40,32},{48,56},{56,48},{64,72... | collective-permute-start | bytes 24584 | tf_op jit(solution)/shard_map/ppermute | solution.py:240
  4.3 2.7 %collective-permute-start.1 = (bf16[32,128]{1,0:T(8,128)(2,1)S(1)}, bf16[32,128]{1,0:T(8,128)(2,1)S(1)}, u32[]{:S(2)}, u32[]{:S(2)}) collective-permute-start(bf16[32,128]{1,0:T(8,128)(2,1)S(1)} %get-tuple-element.17), channel_id=1, source_target_pairs={{0,16},{8,24},{16,0},{24,8},{32,48},{40,56},{48,32},{56,40},{64,80... | collective-permute-start | bytes 24584 | tf_op jit(solution)/shard_map/ppermute | solution.py:240
  4.3 3.4 %collective-permute-start.2 = (bf16[32,128]{1,0:T(8,128)(2,1)S(1)}, bf16[32,128]{1,0:T(8,128)(2,1)S(1)}, u32[]{:S(2)}, u32[]{:S(2)}) collective-permute-start(bf16[32,128]{1,0:T(8,128)(2,1)S(1)} %get-tuple-element.18), channel_id=1, source_target_pairs={{0,24},{8,16},{16,8},{24,0},{32,56},{40,48},{48,40},{56,32},{64,88... | collective-permute-start | bytes 24584 | tf_op jit(solution)/shard_map/ppermute | solution.py:240
  7.7 13.6 %copy-start.2 = (bf16[1024,256]{1,0:T(8,128)(2,1)S(1)}, bf16[1024,256]{1,0:T(8,128)(2,1)}, u32[]{:S(2)}) copy-start(bf16[1024,256]{1,0:T(8,128)(2,1)} %w_ref.3) | copy-start | bytes 1572868
  19.4 3.1 %collective-permute-start.3 = (bf16[128,1152]{1,0:T(8,128)(2,1)S(1)}, bf16[128,1152]{1,0:T(8,128)(2,1)S(1)}, u32[]{:S(2)}, u32[]{:S(2)}) collective-permute-start(bf16[128,1152]{1,0:T(8,128)(2,1)S(1)} %bitcast.15), channel_id=1, source_target_pairs={{0,8},{8,0},{16,24},{24,16},{32,40},{40,32},{48,56},{56,48},{64,72... | collective-permute-start | bytes 884744 | tf_op jit(solution)/shard_map/ppermute | solution.py:248

commit v7 on v6

--- a/solution.py
+++ b/solution.py
@@ -14,8 +14,9 @@
 OUT_COLS = Q_COLS + HEAD
 PACKED = 32
 BEAM_AXES = "beam"
-QUERY_ORDER = (7, 6, 5, 4, 3, 2, 1, 0)
-PLANE_ORDER = (4, 5, 6, 7, 0, 1, 2, 3)
+QUERY_ORDER = (5, 7, 6, 4, 3, 2, 0, 1)
+LINE_ORDER = ((4, 0), (4, 1), (5, 0), (5, 1), (6, 0), (0, 1), (6, 1), (7, 0), (7, 1), (1, 1), (0, 0), (1, 0), (3, 0), (2, 0), (2, 1), (3, 1))
+LINE_GROUPS = [[(2 * k + c) * 8 + z for z, c in LINE_ORDER] for k in range(16)]
 CHIP_GROUPS = [[4 * q + 2 * p + c for q in QUERY_ORDER for p in (1, 0)] for c in range(2)]
 F32 = jnp.float32
 BF16 = jnp.bfloat16
@@ -82,6 +83,8 @@
         info_ref[pl.ds(row + 2, 1), :] = fresh_values[s : s + 1]
         info_ref[pl.ds(row + 4, 1), :] = jnp.full((1, HEAD), cache_row, F32)
         info_ref[pl.ds(row + 6, 1), :] = jnp.full((1, HEAD), slot, F32)
+        beside = (partner[s] ^ 1) * 16 + order[s]
+        info_ref[pl.ds(beside + 8, 1), :] = jnp.full((1, HEAD), slot, F32)
         spread = jnp.where(rows == s, len_ref[s], spread)
     limit_ref[...] = spread
     for j, out_ref in enumerate((m0, m1, m2, m3)):
@@ -135,7 +138,11 @@
 def attend_far_kernel(limit_ref, before_ref, m0, m1, m2, m3, k_ref, v_ref, out_ref, s_ref, o_ref):
     o_ref[...] = before_ref[...]
     attend_pairs(6, (m3,), limit_ref, k_ref, v_ref, s_ref, o_ref)
-    ids = jnp.concatenate([m[16:, :].astype(F32)[6:8] for m in (m0, m1, m2, m3)], axis=0)
+    infos = [m[16:, :].astype(F32) for m in (m0, m1, m2, m3)]
+    own_ids = jnp.concatenate([info[6:8] for info in infos], axis=0)
+    core_ids = jnp.concatenate([infos[d ^ 1][8:10] for d in range(4)], axis=0)
+    lanes = lax.broadcasted_iota(I32, (SLOTS, HEAD), 1)
+    ids = jnp.where(lanes < HEAD // 2, own_ids, core_ids)
     block = jnp.concatenate(
         [o_ref[h * SLOTS : (h + 1) * SLOTS, :] for h in range(GROUPED)] + [ids], axis=1
     )
@@ -144,15 +151,16 @@
         out_ref[j * 16 : (j + 1) * 16, :] = pair
 
 
-def project_half(part, rows_ref, w_ref, out_ref):
-    terms = jnp.dot(rows_ref[:, :Q_COLS], w_ref[...], preferred_element_type=F32).astype(BF16)
-    for q in range(8):
-        source = QUERY_ORDER.index(q) * 16
-        target = PLANE_ORDER.index(q) * 32 + part * 16
-        out_ref[target : target + 16, :] = terms[source : source + 16]
-
-
-def place_half(rows_ref):
+def project_kernel(rows_ref, w_ref, w_core_ref, out_ref, place_ref):
+    core = beam_index() & 1
+    rows = rows_ref[:, :Q_COLS]
+    sides = (core, 1 - core)
+    for side, ref in zip(sides, (w_ref, w_core_ref)):
+        terms = jnp.dot(rows, ref[...], preferred_element_type=F32).astype(BF16)
+        for q in range(8):
+            source = QUERY_ORDER.index(q) * 16
+            at = jnp.where(side == 0, LINE_ORDER.index((q, 0)), LINE_ORDER.index((q, 1)))
+            out_ref[pl.ds(pl.multiple_of(at * 16, 16), 16), :] = terms[source : source + 16]
     query = lax.axis_index("tensor")
     place = jnp.int32(0)
     for q in range(8):
@@ -160,25 +168,21 @@
     first = pl.multiple_of(place * 16, 16)
     lanes = lax.broadcasted_iota(I32, (16, HEAD), 1)
     ids = rows_ref[pl.ds(first, 16), Q_COLS:].astype(F32).astype(I32)
-    return (ids == lanes).astype(F32).astype(BF16)
-
-
-def project_own_kernel(rows_ref, w_ref, out_ref, place_ref):
-    project_half(0, rows_ref, w_ref, out_ref)
-    place_ref[:16, :] = place_half(rows_ref)
-    place_ref[16:, :] = jnp.zeros((16, HEAD), BF16)
-
-
-def project_other_kernel(rows_ref, w_ref, own_ref, own_place_ref, out_ref, place_ref):
-    project_half(1, rows_ref, w_ref, out_ref)
-    place_ref[16:, :] = place_half(rows_ref)
+    for side, lane in zip(sides, (0, HEAD // 2)):
+        place = (ids[:, lane : lane + 1] == lanes).astype(F32).astype(BF16)
+        place_ref[pl.ds(pl.multiple_of(side * 16, 16), 16), :] = place
 
 
 def finish_kernel(terms_ref, place_ref, out_ref):
-    total = terms_ref[0:32, :].astype(F32)
-    for z in range(1, 8):
-        total = total + terms_ref[z * 32 : z * 32 + 32, :].astype(F32)
-    out_ref[...] = transposed_dot(place_ref[...], total.astype(BF16))[:BEAMS].astype(BF16)
+    halves = []
+    for core in range(2):
+        total = jnp.zeros((16, 256), F32)
+        for at, (_, source_core) in enumerate(LINE_ORDER):
+            if source_core == core:
+                total = total + terms_ref[at * 16 : at * 16 + 16, :].astype(F32)
+        halves.append(total.astype(BF16))
+    rows = jnp.concatenate(halves, axis=0)
+    out_ref[...] = transposed_dot(place_ref[...], rows)[:BEAMS].astype(BF16)
 
 
 def pack(parents, lengths, queries, token_keys, token_values):
@@ -241,33 +245,22 @@
     ]
     caches = [x.reshape(SLOTS, POSITIONS, HEAD) for x in (key_cache, value_cache)]
     m0, m1, m2, m3 = [messages[0]] + arrived
+    late_weight, m1 = lax.optimization_barrier((weight, m1))
+    core_weight = lax.ppermute(late_weight, BEAM_AXES, [(i, i ^ 1) for i in range(32)])
     part = attend_early(attend_near_kernel, 4, "attend_near", limits, m0, m1, *caches)
     part = attend_early(attend_next_kernel, 2, "attend_next", limits, part, m2, *caches)
     heads = attend_far(limits, part, m0, m1, m2, m3, *caches)
     gathered = lax.all_to_all(heads, "beam", 0, 0, axis_index_groups=CHIP_GROUPS, tiled=True)
-    other = lax.ppermute(gathered, BEAM_AXES, [(i, i ^ 1) for i in range(32)])
-    shapes = (pltpu.VMEM((256, 256), BF16), pltpu.VMEM((BEAMS, HEAD), BF16))
-    params = pltpu.CompilerParams(vmem_limit_bytes=16 * MIB)
-    own = pl.pallas_call(
-        project_own_kernel,
-        out_shape=shapes,
-        in_specs=[VMEM] * 2,
+    terms, place = pl.pallas_call(
+        project_kernel,
+        out_shape=(pltpu.VMEM((256, 256), BF16), pltpu.VMEM((BEAMS, HEAD), BF16)),
+        in_specs=[VMEM] * 3,
         out_specs=(VMEM, VMEM),
-        compiler_params=params,
-        cost_estimate=pl.CostEstimate(flops=2 * 10**9, bytes_accessed=0, transcendentals=0),
-        name="project_own",
-    )(gathered, weight)
-    terms, place = pl.pallas_call(
-        project_other_kernel,
-        out_shape=shapes,
-        in_specs=[VMEM] * 4,
-        out_specs=(VMEM, VMEM),
-        input_output_aliases={2: 0, 3: 1},
-        compiler_params=params,
-        name="project_other",
-    )(other, weight, *own)
+        compiler_params=pltpu.CompilerParams(vmem_limit_bytes=16 * MIB),
+        name="project",
+    )(gathered, weight, core_weight)
     shares = lax.all_to_all(
-        terms, "tensor", 0, 0, axis_index_groups=[list(PLANE_ORDER)], tiled=True
+        terms, ("beam", "tensor"), 0, 0, axis_index_groups=LINE_GROUPS, tiled=True
     )
     return pl.pallas_call(
         finish_kernel,

time: 36.2 us -> 35 us (0.967)
  starting transfers between devices: 6.99 us -> 5.2 us
  blocking collectives: 23.4 us -> 25.1 us
  waiting for transfers between devices: 0.97 us -> 0.01 us
    ppermute x1, starting transfers between devices: 1.93 us -> 0.15 us  [body(): lax.ppermute(late_weight, BEAM_AXES, [(i, i ^ 1) for i in range(32)])]
    all_to_all x1, blocking collectives: 12.5 us -> 14.3 us  [body(): lax.all_to_all(terms, ('beam', 'tensor'), 0, 0, axis_index_groups=LINE_GR...]
    ppermute x1, waiting for transfers between devices: 0.96 us -> 0.01 us  [body(): lax.ppermute(late_weight, BEAM_AXES, [(i, i ^ 1) for i in range(32)])]
  transfers between devices with their start and end apart: 4 -> 4, of which waited for: 1 -> 0; matrix products, arithmetic and copies ran while one was open for 0% -> 0% of each run, Pallas kernels for 5% -> 7%
where the time goes in v7:
time: 35 us; the launch traced here: 34.9 us
  blocking collectives  25.1 us (72%)
  starting transfers between devices  5.2 us (15%)
  Pallas kernels  4.49 us (13%)
    all_to_all x1, blocking collectives, body(): lax.all_to_all(terms, ('beam', 'tensor'), 0, 0, axis_index_groups=LINE_GR...  14.3 us
    all_to_all x1, blocking collectives, body(): lax.all_to_all(heads, 'beam', 0, 0, axis_index_groups=CHIP_GROUPS, tiled=...  10.8 us
    ppermute x3, starting transfers between devices, body(): lax.ppermute(messages[d], BEAM_AXES, [(i, i ^ d) for i in range(32)])  5.05 us
    pallas_call x2, Pallas kernels, attend_early(): pl.pallas_call(kernel, out_shape=jax.ShapeDtypeStruct((GROUPED * SLOTS, H...  1.65 us
    pallas_call x1, Pallas kernels, pack(): pl.pallas_call(pack_kernel, out_shape=(message,) * 4 + (pltpu.VMEM((SLOTS...  1.01 us
    pallas_call x1, Pallas kernels, body(): pl.pallas_call(finish_kernel, out_shape=jax.ShapeDtypeStruct((BEAMS, 256)...  0.78 us
    pallas_call x1, Pallas kernels, attend_far(): pl.pallas_call(attend_far_kernel, out_shape=jax.ShapeDtypeStruct((16 * SL...  0.73 us
  transfers between devices with their start and end apart: 4, of which 0 were waited for; matrix products, arithmetic and copies ran while one was open for 0% of the time, Pallas kernels for 7%

profile of v7, /device:TPU:1, one launch (start us, length us, event | category | flops | bytes accessed | tf_op | source)
XLA Modules:
  0.0 34.9 jit_solution(12060437204710273266)
XLA Ops:
  0.0 0.0 copy-start.2
  0.0 0.0 copy-start.1
  0.0 0.0 copy-start
  0.0 1.0 %pack.1 = (bf16[32,128]{1,0:T(8,128)(2,1)S(1)}, bf16[32,128]{1,0:T(8,128)(2,1)S(1)}, bf16[32,128]{1,0:T(8,128)(2,1)S(1)}, bf16[32,128]{1,0:T(8,128)(2,1)S(1)}, s32[8,128]{1,0:T(8,128)S(1)}) custom-call(s32[8]{0:T(128)} %parent_hbm.1, s32[8]{0:T(128)} %len_hbm.1, bf16[8,1024]{1,0:T(8,128)(2,1)} %q_hbm.1, bf16[8,128]{1,0:T(8,128)(2,1)} %key_hbm.1, ...), custom_call_target="tpu_custom_call" | custom-call | flops 20000000000 | tf_op jit(solution)/shard_map/pack/pallas_call | solution.py:191
  1.0 3.3 %collective-permute-start = (bf16[32,128]{1,0:T(8,128)(2,1)S(1)}, bf16[32,128]{1,0:T(8,128)(2,1)S(1)}, u32[]{:S(2)}, u32[]{:S(2)}) collective-permute-start(bf16[32,128]{1,0:T(8,128)(2,1)S(1)} %get-tuple-element.16), channel_id=1, source_target_pairs={{0,8},{8,0},{16,24},{24,16},{32,40},{40,32},{48,56},{56,48},{64,72... | collective-permute-start | bytes 24584 | tf_op jit(solution)/shard_map/ppermute | solution.py:244
  4.3 0.0 collective-permute-start.1
  4.4 1.7 %collective-permute-start.2 = (bf16[32,128]{1,0:T(8,128)(2,1)S(1)}, bf16[32,128]{1,0:T(8,128)(2,1)S(1)}, u32[]{:S(2)}, u32[]{:S(2)}) collective-permute-start(bf16[32,128]{1,0:T(8,128)(2,1)S(1)} %get-tuple-element.19), channel_id=1, source_target_pairs={{0,24},{8,16},{16,8},{24,0},{32,56},{40,48},{48,40},{56,32},{64,88... | collective-permute-start | bytes 24584 | tf_op jit(solution)/shard_map/ppermute | solution.py:244
  6.1 0.0 collective-permute-done.m1
  6.1 0.0 copy-done.2
  6.1 0.1 collective-permute-start.3
  6.2 0.0 copy-done.1
  6.2 0.0 copy-done
  6.2 1.0 %attend_near.1.before_ref = f32[64,128]{1,0:T(8,128)S(1)} custom-call(s32[8,128]{1,0:T(8,128)S(1)} %get-tuple-element.14.limit_ref, bf16[32,128]{1,0:T(8,128)(2,1)S(1)} %get-tuple-element.15.m0, bf16[32,128]{1,0:T(8,128)(2,1)S(1)} %collective-permute-done.m1, bf16[8,2048,128]{2,1,0:T(8,128)(2,1)S(1)} %bitcast.6, bf16[8,2048,128]{2,1,0:T(8,128)(2,1)S(1)} %bitcast.9), custom_call_target="tpu_custom_call" | custom-call | flops 2000000000 | tf_op jit(solution)/shard_map/attend_near/pallas_call | solution.py:214
  7.2 0.0 collective-permute-done.1.m2
  7.2 0.7 %attend_next.1.before_ref = f32[64,128]{1,0:T(8,128)S(1)} custom-call(s32[8,128]{1,0:T(8,128)S(1)} %get-tuple-element.14.limit_ref, f32[64,128]{1,0:T(8,128)S(1)} %attend_near.1.before_ref, bf16[32,128]{1,0:T(8,128)(2,1)S(1)} %collective-permute-done.1.m2, bf16[8,2048,128]{2,1,0:T(8,128)(2,1)S(1)} %bitcast.7, bf16[8,2048,128]{2,1,0:T(8,128)(2,1)S(1)} %bitcast.10), custom_call_target="tpu_custom_call" | custom-call | flops 2000000000 | tf_op jit(solution)/shard_map/attend_next/pallas_call | solution.py:214
  7.9 0.0 collective-permute-done.2.m3
  7.9 0.7 %attend_far.1 = bf16[128,1152]{1,0:T(8,128)(2,1)S(1)} custom-call(s32[8,128]{1,0:T(8,128)S(1)} %get-tuple-element.14.limit_ref, f32[64,128]{1,0:T(8,128)S(1)} %attend_next.1.before_ref, bf16[32,128]{1,0:T(8,128)(2,1)S(1)} %get-tuple-element.15.m0, bf16[32,128]{1,0:T(8,128)(2,1)S(1)} %collective-permute-done.m1, ...), custom_call_target="tpu_custom_call" | custom-call | tf_op jit(solution)/shard_map/attend_far/pallas_call | solution.py:227
  8.6 10.8 %all_to_all.22 = bf16[16,8,1152]{2,1,0:T(8,128)(2,1)S(1)} all-to-all(bf16[16,8,1152]{2,1,0:T(8,128)(2,1)S(1)} %bitcast.12), channel_id=1, replica_groups={{176,160,240,224,208,192,144,128,112,96,80,64,16,0,48,32},{184,168,248,..., dimensions={0} | all-to-all | bytes 589824 | tf_op jit(solution)/shard_map/all_to_all | solution.py:253
  19.5 0.0 collective-permute-done.3.w_core_ref
  19.5 0.3 project.1
  19.8 14.3 %all_to_all.23 = bf16[16,16,256]{2,1,0:T(8,128)(2,1)S(1)} all-to-all(bf16[16,16,256]{2,1,0:T(8,128)(2,1)S(1)} %bitcast.15), channel_id=1, replica_groups={{4,12,5,13,6,8,14,7,15,9,0,1,3,2,10,11},{20,28,21,29,22,24,30,23,31,25,..., dimensions={0} | all-to-all | bytes 262144 | tf_op jit(solution)/shard_map/all_to_all | solution.py:262
  34.1 0.8 %finish.1 = bf16[32,256]{1,0:T(8,128)(2,1)} custom-call(bf16[256,256]{1,0:T(8,128)(2,1)S(1)} %bitcast.14, bf16[32,128]{1,0:T(8,128)(2,1)S(1)} %get-tuple-element.22.place_ref), custom_call_target="tpu_custom_call" | custom-call | tf_op jit(solution)/shard_map/finish/pallas_call | solution.py:265
Async XLA Ops:
  0.0 6.1 %copy-start.2 = (bf16[1024,256]{1,0:T(8,128)(2,1)S(1)}, bf16[1024,256]{1,0:T(8,128)(2,1)}, u32[]{:S(2)}) copy-start(bf16[1024,256]{1,0:T(8,128)(2,1)} %w_ref.1) | copy-start | bytes 1572868
  0.0 6.2 %copy-start.1 = (bf16[8,1,2048,128]{3,2,1,0:T(8,128)(2,1)S(1)}, bf16[8,1,2048,128]{3,2,1,0:T(8,128)(2,1)}, u32[]{:S(2)}) copy-start(bf16[8,1,2048,128]{3,2,1,0:T(8,128)(2,1)} %param.14) | copy-start | bytes 12582916
  0.0 6.2 %copy-start = (bf16[8,1,2048,128]{3,2,1,0:T(8,128)(2,1)S(1)}, bf16[8,1,2048,128]{3,2,1,0:T(8,128)(2,1)}, u32[]{:S(2)}) copy-start(bf16[8,1,2048,128]{3,2,1,0:T(8,128)(2,1)} %param.13) | copy-start | bytes 12582916
  1.0 5.1 %collective-permute-start = (bf16[32,128]{1,0:T(8,128)(2,1)S(1)}, bf16[32,128]{1,0:T(8,128)(2,1)S(1)}, u32[]{:S(2)}, u32[]{:S(2)}) collective-permute-start(bf16[32,128]{1,0:T(8,128)(2,1)S(1)} %get-tuple-element.16), channel_id=1, source_target_pairs={{0,8},{8,0},{16,24},{24,16},{32,40},{40,32},{48,56},{56,48},{64,72... | collective-permute-start | bytes 24584 | tf_op jit(solution)/shard_map/ppermute | solution.py:244
  4.3 2.9 %collective-permute-start.1 = (bf16[32,128]{1,0:T(8,128)(2,1)S(1)}, bf16[32,128]{1,0:T(8,128)(2,1)S(1)}, u32[]{:S(2)}, u32[]{:S(2)}) collective-permute-start(bf16[32,128]{1,0:T(8,128)(2,1)S(1)} %get-tuple-element.18), channel_id=1, source_target_pairs={{0,16},{8,24},{16,0},{24,8},{32,48},{40,56},{48,32},{56,40},{64,80... | collective-permute-start | bytes 24584 | tf_op jit(solution)/shard_map/ppermute | solution.py:244
  4.4 3.6 %collective-permute-start.2 = (bf16[32,128]{1,0:T(8,128)(2,1)S(1)}, bf16[32,128]{1,0:T(8,128)(2,1)S(1)}, u32[]{:S(2)}, u32[]{:S(2)}) collective-permute-start(bf16[32,128]{1,0:T(8,128)(2,1)S(1)} %get-tuple-element.19), channel_id=1, source_target_pairs={{0,24},{8,16},{16,8},{24,0},{32,56},{40,48},{48,40},{56,32},{64,88... | collective-permute-start | bytes 24584 | tf_op jit(solution)/shard_map/ppermute | solution.py:244
  6.1 13.4 %collective-permute-start.3 = (bf16[1024,256]{1,0:T(8,128)(2,1)S(1)}, bf16[1024,256]{1,0:T(8,128)(2,1)S(1)}, u32[]{:S(2)}, u32[]{:S(2)}) collective-permute-start(bf16[1024,256]{1,0:T(8,128)(2,1)S(1)} %copy-done.2), channel_id=1, source_target_pairs={{0,8},{8,0},{16,24},{24,16},{32,40},{40,32},{48,56},{56,48},{64,72... | collective-permute-start | bytes 1572872 | tf_op jit(solution)/shard_map/ppermute | solution.py:249

commit v8 on v7

--- a/solution.py
+++ b/solution.py
@@ -10,12 +10,13 @@
 SLOTS = 8
 BEAMS = 32
 POSITIONS = 2048
+CHUNK = 1024
 Q_COLS = GROUPED * HEAD
 OUT_COLS = Q_COLS + HEAD
 PACKED = 32
 BEAM_AXES = "beam"
 QUERY_ORDER = (5, 7, 6, 4, 3, 2, 0, 1)
-LINE_ORDER = ((4, 0), (4, 1), (5, 0), (5, 1), (6, 0), (0, 1), (6, 1), (7, 0), (7, 1), (1, 1), (0, 0), (1, 0), (3, 0), (2, 0), (2, 1), (3, 1))
+LINE_ORDER = ((4, 1), (4, 0), (5, 0), (5, 1), (6, 0), (0, 1), (6, 1), (7, 0), (7, 1), (1, 1), (0, 0), (1, 0), (3, 0), (2, 0), (2, 1), (3, 1))
 LINE_GROUPS = [[(2 * k + c) * 8 + z for z, c in LINE_ORDER] for k in range(16)]
 CHIP_GROUPS = [[4 * q + 2 * p + c for q in QUERY_ORDER for p in (1, 0)] for c in range(2)]
 F32 = jnp.float32
@@ -100,28 +101,36 @@
         jnp.clip(infos[i // 2].astype(I32)[4 + i % 2, 0], 0, SLOTS - 1) for i in slots
     ]
     scale = HEAD ** (-0.5)
-    positions = lax.broadcasted_iota(I32, (GROUPED, POSITIONS), 1)
-    new_scores = []
+    positions = lax.broadcasted_iota(I32, (GROUPED, CHUNK), 1)
+    for c in range(POSITIONS // CHUNK):
+        for i in slots:
+            q = heads[i // 2][i % 2 * 8 : i % 2 * 8 + 8]
+            keys = k_ref[cache_rows[i], pl.ds(c * CHUNK, CHUNK), :]
+            scores = lax.dot_general(
+                q.astype(BF16), keys, (((1,), (1,)), ((), ())), preferred_element_type=F32
+            ) * scale
+            limit = limit_ref[pl.ds(cache_rows[i], 1), :][:, :1]
+            s_ref[i, :, pl.ds(c * CHUNK, CHUNK)] = jnp.where(
+                positions + c * CHUNK < limit, scores, -1e30
+            )
     for i in slots:
         q = heads[i // 2][i % 2 * 8 : i % 2 * 8 + 8]
         fresh_key = infos[i // 2][i % 2 : i % 2 + 1]
-        scores = lax.dot_general(
-            q.astype(BF16), k_ref[cache_rows[i]], (((1,), (1,)), ((), ())), preferred_element_type=F32
-        ) * scale
-        limit = limit_ref[pl.ds(cache_rows[i], 1), :][:, :1]
-        s_ref[i] = jnp.where(positions < limit, scores, -1e30)
-        new_scores.append(jnp.sum(q * fresh_key, axis=1, keepdims=True) * scale)
-    for i in slots:
+        new_score = jnp.sum(q * fresh_key, axis=1, keepdims=True) * scale
         scores = s_ref[i]
-        maximum = jnp.maximum(jnp.max(scores, axis=1, keepdims=True), new_scores[i])
-        weights = jnp.exp(scores - maximum)
-        new_weight = jnp.exp(new_scores[i] - maximum)
-        denominator = jnp.sum(weights, axis=1, keepdims=True) + new_weight
-        weighted = jnp.dot(
-            weights.astype(BF16), v_ref[cache_rows[i]], preferred_element_type=F32
-        )
+        maximum = jnp.maximum(jnp.max(scores, axis=1, keepdims=True), new_score)
+        new_weight = jnp.exp(new_score - maximum)
+        denominator = new_weight
         fresh_value = infos[i // 2][2 + i % 2 : 3 + i % 2]
-        weighted = weighted + new_weight.astype(BF16).astype(F32) * fresh_value
+        weighted = new_weight.astype(BF16).astype(F32) * fresh_value
+        for c in range(POSITIONS // CHUNK):
+            weights = jnp.exp(s_ref[i, :, pl.ds(c * CHUNK, CHUNK)] - maximum)
+            denominator = denominator + jnp.sum(weights, axis=1, keepdims=True)
+            weighted = weighted + jnp.dot(
+                weights.astype(BF16),
+                v_ref[cache_rows[i], pl.ds(c * CHUNK, CHUNK), :],
+                preferred_element_type=F32,
+            )
         o_ref[pl.ds(first + i, GROUPED, stride=SLOTS), :] = weighted / denominator
 
 

time: 35 us -> 34.9 us (level)
  no operation moved by 1% of the time
where the time goes in v8:
time: 34.9 us; the launch traced here: 34.7 us
  blocking collectives  24.9 us (71%)
  starting transfers between devices  5.2 us (15%)
  Pallas kernels  4.49 us (13%)
    all_to_all x1, blocking collectives, body(): lax.all_to_all(terms, ('beam', 'tensor'), 0, 0, axis_index_groups=LINE_GR...  14.1 us
    all_to_all x1, blocking collectives, body(): lax.all_to_all(heads, 'beam', 0, 0, axis_index_groups=CHIP_GROUPS, tiled=...  10.8 us
    ppermute x3, starting transfers between devices, body(): lax.ppermute(messages[d], BEAM_AXES, [(i, i ^ d) for i in range(32)])  5.05 us
    pallas_call x2, Pallas kernels, attend_early(): pl.pallas_call(kernel, out_shape=jax.ShapeDtypeStruct((GROUPED * SLOTS, H...  1.66 us
    pallas_call x1, Pallas kernels, pack(): pl.pallas_call(pack_kernel, out_shape=(message,) * 4 + (pltpu.VMEM((SLOTS...  1.01 us
    pallas_call x1, Pallas kernels, body(): pl.pallas_call(finish_kernel, out_shape=jax.ShapeDtypeStruct((BEAMS, 256)...  0.78 us
    pallas_call x1, Pallas kernels, attend_far(): pl.pallas_call(attend_far_kernel, out_shape=jax.ShapeDtypeStruct((16 * SL...  0.73 us
  transfers between devices with their start and end apart: 4, of which 0 were waited for; matrix products, arithmetic and copies ran while one was open for 0% of the time, Pallas kernels for 7%

profile of v8, /device:TPU:1, one launch (start us, length us, event | category | flops | bytes accessed | tf_op | source)
XLA Modules:
  0.0 34.7 jit_solution(4099985184222636476)
XLA Ops:
  0.0 0.0 copy-start.2
  0.0 0.0 copy-start.1
  0.0 0.0 copy-start
  0.0 1.0 %pack.1 = (bf16[32,128]{1,0:T(8,128)(2,1)S(1)}, bf16[32,128]{1,0:T(8,128)(2,1)S(1)}, bf16[32,128]{1,0:T(8,128)(2,1)S(1)}, bf16[32,128]{1,0:T(8,128)(2,1)S(1)}, s32[8,128]{1,0:T(8,128)S(1)}) custom-call(s32[8]{0:T(128)} %parent_hbm.1, s32[8]{0:T(128)} %len_hbm.1, bf16[8,1024]{1,0:T(8,128)(2,1)} %q_hbm.1, bf16[8,128]{1,0:T(8,128)(2,1)} %key_hbm.1, ...), custom_call_target="tpu_custom_call" | custom-call | flops 20000000000 | tf_op jit(solution)/shard_map/pack/pallas_call | solution.py:200
  1.0 3.3 %collective-permute-start = (bf16[32,128]{1,0:T(8,128)(2,1)S(1)}, bf16[32,128]{1,0:T(8,128)(2,1)S(1)}, u32[]{:S(2)}, u32[]{:S(2)}) collective-permute-start(bf16[32,128]{1,0:T(8,128)(2,1)S(1)} %get-tuple-element.16), channel_id=1, source_target_pairs={{0,8},{8,0},{16,24},{24,16},{32,40},{40,32},{48,56},{56,48},{64,72... | collective-permute-start | bytes 24584 | tf_op jit(solution)/shard_map/ppermute | solution.py:253
  4.3 0.0 collective-permute-start.1
  4.4 1.7 %collective-permute-start.2 = (bf16[32,128]{1,0:T(8,128)(2,1)S(1)}, bf16[32,128]{1,0:T(8,128)(2,1)S(1)}, u32[]{:S(2)}, u32[]{:S(2)}) collective-permute-start(bf16[32,128]{1,0:T(8,128)(2,1)S(1)} %get-tuple-element.19), channel_id=1, source_target_pairs={{0,24},{8,16},{16,8},{24,0},{32,56},{40,48},{48,40},{56,32},{64,88... | collective-permute-start | bytes 24584 | tf_op jit(solution)/shard_map/ppermute | solution.py:253
  6.1 0.0 collective-permute-done.m1
  6.1 0.0 copy-done.2
  6.1 0.1 collective-permute-start.3
  6.2 0.0 copy-done.1
  6.2 0.0 copy-done
  6.2 1.0 %attend_near.1.before_ref = f32[64,128]{1,0:T(8,128)S(1)} custom-call(s32[8,128]{1,0:T(8,128)S(1)} %get-tuple-element.14.limit_ref, bf16[32,128]{1,0:T(8,128)(2,1)S(1)} %get-tuple-element.15.m0, bf16[32,128]{1,0:T(8,128)(2,1)S(1)} %collective-permute-done.m1, bf16[8,2048,128]{2,1,0:T(8,128)(2,1)S(1)} %bitcast.6, bf16[8,2048,128]{2,1,0:T(8,128)(2,1)S(1)} %bitcast.9), custom_call_target="tpu_custom_call" | custom-call | flops 2000000000 | tf_op jit(solution)/shard_map/attend_near/pallas_call | solution.py:223
  7.2 0.0 collective-permute-done.1.m2
  7.2 0.7 %attend_next.1.before_ref = f32[64,128]{1,0:T(8,128)S(1)} custom-call(s32[8,128]{1,0:T(8,128)S(1)} %get-tuple-element.14.limit_ref, f32[64,128]{1,0:T(8,128)S(1)} %attend_near.1.before_ref, bf16[32,128]{1,0:T(8,128)(2,1)S(1)} %collective-permute-done.1.m2, bf16[8,2048,128]{2,1,0:T(8,128)(2,1)S(1)} %bitcast.7, bf16[8,2048,128]{2,1,0:T(8,128)(2,1)S(1)} %bitcast.10), custom_call_target="tpu_custom_call" | custom-call | flops 2000000000 | tf_op jit(solution)/shard_map/attend_next/pallas_call | solution.py:223
  7.9 0.0 collective-permute-done.2.m3
  7.9 0.7 %attend_far.1 = bf16[128,1152]{1,0:T(8,128)(2,1)S(1)} custom-call(s32[8,128]{1,0:T(8,128)S(1)} %get-tuple-element.14.limit_ref, f32[64,128]{1,0:T(8,128)S(1)} %attend_next.1.before_ref, bf16[32,128]{1,0:T(8,128)(2,1)S(1)} %get-tuple-element.15.m0, bf16[32,128]{1,0:T(8,128)(2,1)S(1)} %collective-permute-done.m1, ...), custom_call_target="tpu_custom_call" | custom-call | tf_op jit(solution)/shard_map/attend_far/pallas_call | solution.py:236
  8.7 10.8 %all_to_all.22 = bf16[16,8,1152]{2,1,0:T(8,128)(2,1)S(1)} all-to-all(bf16[16,8,1152]{2,1,0:T(8,128)(2,1)S(1)} %bitcast.12), channel_id=1, replica_groups={{176,160,240,224,208,192,144,128,112,96,80,64,16,0,48,32},{184,168,248,..., dimensions={0} | all-to-all | bytes 589824 | tf_op jit(solution)/shard_map/all_to_all | solution.py:262
  19.5 0.0 collective-permute-done.3.w_core_ref
  19.5 0.3 project.1
  19.8 14.1 %all_to_all.23 = bf16[16,16,256]{2,1,0:T(8,128)(2,1)S(1)} all-to-all(bf16[16,16,256]{2,1,0:T(8,128)(2,1)S(1)} %bitcast.15), channel_id=1, replica_groups={{12,4,5,13,6,8,14,7,15,9,0,1,3,2,10,11},{28,20,21,29,22,24,30,23,31,25,..., dimensions={0} | all-to-all | bytes 262144 | tf_op jit(solution)/shard_map/all_to_all | solution.py:271
  33.9 0.8 %finish.1 = bf16[32,256]{1,0:T(8,128)(2,1)} custom-call(bf16[256,256]{1,0:T(8,128)(2,1)S(1)} %bitcast.14, bf16[32,128]{1,0:T(8,128)(2,1)S(1)} %get-tuple-element.22.place_ref), custom_call_target="tpu_custom_call" | custom-call | tf_op jit(solution)/shard_map/finish/pallas_call | solution.py:274
Async XLA Ops:
  0.0 6.1 %copy-start.2 = (bf16[1024,256]{1,0:T(8,128)(2,1)S(1)}, bf16[1024,256]{1,0:T(8,128)(2,1)}, u32[]{:S(2)}) copy-start(bf16[1024,256]{1,0:T(8,128)(2,1)} %w_ref.1) | copy-start | bytes 1572868
  0.0 6.2 %copy-start.1 = (bf16[8,1,2048,128]{3,2,1,0:T(8,128)(2,1)S(1)}, bf16[8,1,2048,128]{3,2,1,0:T(8,128)(2,1)}, u32[]{:S(2)}) copy-start(bf16[8,1,2048,128]{3,2,1,0:T(8,128)(2,1)} %param.14) | copy-start | bytes 12582916
  0.0 6.2 %copy-start = (bf16[8,1,2048,128]{3,2,1,0:T(8,128)(2,1)S(1)}, bf16[8,1,2048,128]{3,2,1,0:T(8,128)(2,1)}, u32[]{:S(2)}) copy-start(bf16[8,1,2048,128]{3,2,1,0:T(8,128)(2,1)} %param.13) | copy-start | bytes 12582916
  1.0 5.1 %collective-permute-start = (bf16[32,128]{1,0:T(8,128)(2,1)S(1)}, bf16[32,128]{1,0:T(8,128)(2,1)S(1)}, u32[]{:S(2)}, u32[]{:S(2)}) collective-permute-start(bf16[32,128]{1,0:T(8,128)(2,1)S(1)} %get-tuple-element.16), channel_id=1, source_target_pairs={{0,8},{8,0},{16,24},{24,16},{32,40},{40,32},{48,56},{56,48},{64,72... | collective-permute-start | bytes 24584 | tf_op jit(solution)/shard_map/ppermute | solution.py:253
  4.3 2.9 %collective-permute-start.1 = (bf16[32,128]{1,0:T(8,128)(2,1)S(1)}, bf16[32,128]{1,0:T(8,128)(2,1)S(1)}, u32[]{:S(2)}, u32[]{:S(2)}) collective-permute-start(bf16[32,128]{1,0:T(8,128)(2,1)S(1)} %get-tuple-element.18), channel_id=1, source_target_pairs={{0,16},{8,24},{16,0},{24,8},{32,48},{40,56},{48,32},{56,40},{64,80... | collective-permute-start | bytes 24584 | tf_op jit(solution)/shard_map/ppermute | solution.py:253
  4.4 3.6 %collective-permute-start.2 = (bf16[32,128]{1,0:T(8,128)(2,1)S(1)}, bf16[32,128]{1,0:T(8,128)(2,1)S(1)}, u32[]{:S(2)}, u32[]{:S(2)}) collective-permute-start(bf16[32,128]{1,0:T(8,128)(2,1)S(1)} %get-tuple-element.19), channel_id=1, source_target_pairs={{0,24},{8,16},{16,8},{24,0},{32,56},{40,48},{48,40},{56,32},{64,88... | collective-permute-start | bytes 24584 | tf_op jit(solution)/shard_map/ppermute | solution.py:253
  6.1 13.4 %collective-permute-start.3 = (bf16[1024,256]{1,0:T(8,128)(2,1)S(1)}, bf16[1024,256]{1,0:T(8,128)(2,1)S(1)}, u32[]{:S(2)}, u32[]{:S(2)}) collective-permute-start(bf16[1024,256]{1,0:T(8,128)(2,1)S(1)} %copy-done.2), channel_id=1, source_target_pairs={{0,8},{8,0},{16,24},{24,16},{32,40},{40,32},{48,56},{56,48},{64,72... | collective-permute-start | bytes 1572872 | tf_op jit(solution)/shard_map/ppermute | solution.py:258

commit v9 on v8

--- a/solution.py
+++ b/solution.py
@@ -16,7 +16,7 @@
 PACKED = 32
 BEAM_AXES = "beam"
 QUERY_ORDER = (5, 7, 6, 4, 3, 2, 0, 1)
-LINE_ORDER = ((4, 1), (4, 0), (5, 0), (5, 1), (6, 0), (0, 1), (6, 1), (7, 0), (7, 1), (1, 1), (0, 0), (1, 0), (3, 0), (2, 0), (2, 1), (3, 1))
+LINE_ORDER = ((5, 1), (4, 0), (5, 0), (4, 1), (6, 0), (0, 1), (6, 1), (7, 0), (7, 1), (1, 1), (0, 0), (1, 0), (3, 0), (2, 0), (2, 1), (3, 1))
 LINE_GROUPS = [[(2 * k + c) * 8 + z for z, c in LINE_ORDER] for k in range(16)]
 CHIP_GROUPS = [[4 * q + 2 * p + c for q in QUERY_ORDER for p in (1, 0)] for c in range(2)]
 F32 = jnp.float32

time: 34.9 us -> 34.6 us (level)
  blocking collectives: 24.9 us -> 24.5 us
    all_to_all x1, blocking collectives: 14.1 us -> 13.7 us  [body(): lax.all_to_all(terms, ('beam', 'tensor'), 0, 0, axis_index_groups=LINE_GR...]
where the time goes in v9:
time: 34.6 us; the launch traced here: 34.3 us
  blocking collectives  24.5 us (71%)
  starting transfers between devices  5.2 us (15%)
  Pallas kernels  4.5 us (13%)
    all_to_all x1, blocking collectives, body(): lax.all_to_all(terms, ('beam', 'tensor'), 0, 0, axis_index_groups=LINE_GR...  13.7 us
    all_to_all x1, blocking collectives, body(): lax.all_to_all(heads, 'beam', 0, 0, axis_index_groups=CHIP_GROUPS, tiled=...  10.8 us
    ppermute x3, starting transfers between devices, body(): lax.ppermute(messages[d], BEAM_AXES, [(i, i ^ d) for i in range(32)])  5.05 us
    pallas_call x2, Pallas kernels, attend_early(): pl.pallas_call(kernel, out_shape=jax.ShapeDtypeStruct((GROUPED * SLOTS, H...  1.66 us
    pallas_call x1, Pallas kernels, pack(): pl.pallas_call(pack_kernel, out_shape=(message,) * 4 + (pltpu.VMEM((SLOTS...  1.01 us
    pallas_call x1, Pallas kernels, body(): pl.pallas_call(finish_kernel, out_shape=jax.ShapeDtypeStruct((BEAMS, 256)...  0.78 us
    pallas_call x1, Pallas kernels, attend_far(): pl.pallas_call(attend_far_kernel, out_shape=jax.ShapeDtypeStruct((16 * SL...  0.73 us
  transfers between devices with their start and end apart: 4, of which 0 were waited for; matrix products, arithmetic and copies ran while one was open for 0% of the time, Pallas kernels for 7%

profile of v9, /device:TPU:1, one launch (start us, length us, event | category | flops | bytes accessed | tf_op | source)
XLA Modules:
  0.0 34.3 jit_solution(15046859926089902430)
XLA Ops:
  0.0 0.0 copy-start.2
  0.0 0.0 copy-start.1
  0.0 0.0 copy-start
  0.0 1.0 %pack.1 = (bf16[32,128]{1,0:T(8,128)(2,1)S(1)}, bf16[32,128]{1,0:T(8,128)(2,1)S(1)}, bf16[32,128]{1,0:T(8,128)(2,1)S(1)}, bf16[32,128]{1,0:T(8,128)(2,1)S(1)}, s32[8,128]{1,0:T(8,128)S(1)}) custom-call(s32[8]{0:T(128)} %parent_hbm.1, s32[8]{0:T(128)} %len_hbm.1, bf16[8,1024]{1,0:T(8,128)(2,1)} %q_hbm.1, bf16[8,128]{1,0:T(8,128)(2,1)} %key_hbm.1, ...), custom_call_target="tpu_custom_call" | custom-call | flops 20000000000 | tf_op jit(solution)/shard_map/pack/pallas_call | solution.py:200
  1.0 3.3 %collective-permute-start = (bf16[32,128]{1,0:T(8,128)(2,1)S(1)}, bf16[32,128]{1,0:T(8,128)(2,1)S(1)}, u32[]{:S(2)}, u32[]{:S(2)}) collective-permute-start(bf16[32,128]{1,0:T(8,128)(2,1)S(1)} %get-tuple-element.16), channel_id=1, source_target_pairs={{0,8},{8,0},{16,24},{24,16},{32,40},{40,32},{48,56},{56,48},{64,72... | collective-permute-start | bytes 24584 | tf_op jit(solution)/shard_map/ppermute | solution.py:253
  4.3 0.0 collective-permute-start.1
  4.4 1.7 %collective-permute-start.2 = (bf16[32,128]{1,0:T(8,128)(2,1)S(1)}, bf16[32,128]{1,0:T(8,128)(2,1)S(1)}, u32[]{:S(2)}, u32[]{:S(2)}) collective-permute-start(bf16[32,128]{1,0:T(8,128)(2,1)S(1)} %get-tuple-element.19), channel_id=1, source_target_pairs={{0,24},{8,16},{16,8},{24,0},{32,56},{40,48},{48,40},{56,32},{64,88... | collective-permute-start | bytes 24584 | tf_op jit(solution)/shard_map/ppermute | solution.py:253
  6.1 0.0 collective-permute-done.m1
  6.1 0.0 copy-done.2
  6.1 0.1 collective-permute-start.3
  6.2 0.0 copy-done.1
  6.2 0.0 copy-done
  6.2 1.0 %attend_near.1.before_ref = f32[64,128]{1,0:T(8,128)S(1)} custom-call(s32[8,128]{1,0:T(8,128)S(1)} %get-tuple-element.14.limit_ref, bf16[32,128]{1,0:T(8,128)(2,1)S(1)} %get-tuple-element.15.m0, bf16[32,128]{1,0:T(8,128)(2,1)S(1)} %collective-permute-done.m1, bf16[8,2048,128]{2,1,0:T(8,128)(2,1)S(1)} %bitcast.6, bf16[8,2048,128]{2,1,0:T(8,128)(2,1)S(1)} %bitcast.9), custom_call_target="tpu_custom_call" | custom-call | flops 2000000000 | tf_op jit(solution)/shard_map/attend_near/pallas_call | solution.py:223
  7.2 0.0 collective-permute-done.1.m2
  7.2 0.7 %attend_next.1.before_ref = f32[64,128]{1,0:T(8,128)S(1)} custom-call(s32[8,128]{1,0:T(8,128)S(1)} %get-tuple-element.14.limit_ref, f32[64,128]{1,0:T(8,128)S(1)} %attend_near.1.before_ref, bf16[32,128]{1,0:T(8,128)(2,1)S(1)} %collective-permute-done.1.m2, bf16[8,2048,128]{2,1,0:T(8,128)(2,1)S(1)} %bitcast.7, bf16[8,2048,128]{2,1,0:T(8,128)(2,1)S(1)} %bitcast.10), custom_call_target="tpu_custom_call" | custom-call | flops 2000000000 | tf_op jit(solution)/shard_map/attend_next/pallas_call | solution.py:223
  7.9 0.0 collective-permute-done.2.m3
  7.9 0.7 %attend_far.1 = bf16[128,1152]{1,0:T(8,128)(2,1)S(1)} custom-call(s32[8,128]{1,0:T(8,128)S(1)} %get-tuple-element.14.limit_ref, f32[64,128]{1,0:T(8,128)S(1)} %attend_next.1.before_ref, bf16[32,128]{1,0:T(8,128)(2,1)S(1)} %get-tuple-element.15.m0, bf16[32,128]{1,0:T(8,128)(2,1)S(1)} %collective-permute-done.m1, ...), custom_call_target="tpu_custom_call" | custom-call | tf_op jit(solution)/shard_map/attend_far/pallas_call | solution.py:236
  8.7 10.8 %all_to_all.22 = bf16[16,8,1152]{2,1,0:T(8,128)(2,1)S(1)} all-to-all(bf16[16,8,1152]{2,1,0:T(8,128)(2,1)S(1)} %bitcast.12), channel_id=1, replica_groups={{176,160,240,224,208,192,144,128,112,96,80,64,16,0,48,32},{184,168,248,..., dimensions={0} | all-to-all | bytes 589824 | tf_op jit(solution)/shard_map/all_to_all | solution.py:262
  19.5 0.0 collective-permute-done.3.w_core_ref
  19.5 0.3 project.1
  19.8 13.7 %all_to_all.23 = bf16[16,16,256]{2,1,0:T(8,128)(2,1)S(1)} all-to-all(bf16[16,16,256]{2,1,0:T(8,128)(2,1)S(1)} %bitcast.15), channel_id=1, replica_groups={{13,4,5,12,6,8,14,7,15,9,0,1,3,2,10,11},{29,20,21,28,22,24,30,23,31,25,..., dimensions={0} | all-to-all | bytes 262144 | tf_op jit(solution)/shard_map/all_to_all | solution.py:271
  33.5 0.8 %finish.1 = bf16[32,256]{1,0:T(8,128)(2,1)} custom-call(bf16[256,256]{1,0:T(8,128)(2,1)S(1)} %bitcast.14, bf16[32,128]{1,0:T(8,128)(2,1)S(1)} %get-tuple-element.22.place_ref), custom_call_target="tpu_custom_call" | custom-call | tf_op jit(solution)/shard_map/finish/pallas_call | solution.py:274
Async XLA Ops:
  0.0 6.1 %copy-start.2 = (bf16[1024,256]{1,0:T(8,128)(2,1)S(1)}, bf16[1024,256]{1,0:T(8,128)(2,1)}, u32[]{:S(2)}) copy-start(bf16[1024,256]{1,0:T(8,128)(2,1)} %w_ref.1) | copy-start | bytes 1572868
  0.0 6.2 %copy-start.1 = (bf16[8,1,2048,128]{3,2,1,0:T(8,128)(2,1)S(1)}, bf16[8,1,2048,128]{3,2,1,0:T(8,128)(2,1)}, u32[]{:S(2)}) copy-start(bf16[8,1,2048,128]{3,2,1,0:T(8,128)(2,1)} %param.14) | copy-start | bytes 12582916
  0.0 6.2 %copy-start = (bf16[8,1,2048,128]{3,2,1,0:T(8,128)(2,1)S(1)}, bf16[8,1,2048,128]{3,2,1,0:T(8,128)(2,1)}, u32[]{:S(2)}) copy-start(bf16[8,1,2048,128]{3,2,1,0:T(8,128)(2,1)} %param.13) | copy-start | bytes 12582916
  1.0 5.1 %collective-permute-start = (bf16[32,128]{1,0:T(8,128)(2,1)S(1)}, bf16[32,128]{1,0:T(8,128)(2,1)S(1)}, u32[]{:S(2)}, u32[]{:S(2)}) collective-permute-start(bf16[32,128]{1,0:T(8,128)(2,1)S(1)} %get-tuple-element.16), channel_id=1, source_target_pairs={{0,8},{8,0},{16,24},{24,16},{32,40},{40,32},{48,56},{56,48},{64,72... | collective-permute-start | bytes 24584 | tf_op jit(solution)/shard_map/ppermute | solution.py:253
  4.3 2.9 %collective-permute-start.1 = (bf16[32,128]{1,0:T(8,128)(2,1)S(1)}, bf16[32,128]{1,0:T(8,128)(2,1)S(1)}, u32[]{:S(2)}, u32[]{:S(2)}) collective-permute-start(bf16[32,128]{1,0:T(8,128)(2,1)S(1)} %get-tuple-element.18), channel_id=1, source_target_pairs={{0,16},{8,24},{16,0},{24,8},{32,48},{40,56},{48,32},{56,40},{64,80... | collective-permute-start | bytes 24584 | tf_op jit(solution)/shard_map/ppermute | solution.py:253
  4.4 3.6 %collective-permute-start.2 = (bf16[32,128]{1,0:T(8,128)(2,1)S(1)}, bf16[32,128]{1,0:T(8,128)(2,1)S(1)}, u32[]{:S(2)}, u32[]{:S(2)}) collective-permute-start(bf16[32,128]{1,0:T(8,128)(2,1)S(1)} %get-tuple-element.19), channel_id=1, source_target_pairs={{0,24},{8,16},{16,8},{24,0},{32,56},{40,48},{48,40},{56,32},{64,88... | collective-permute-start | bytes 24584 | tf_op jit(solution)/shard_map/ppermute | solution.py:253
  6.1 13.4 %collective-permute-start.3 = (bf16[1024,256]{1,0:T(8,128)(2,1)S(1)}, bf16[1024,256]{1,0:T(8,128)(2,1)S(1)}, u32[]{:S(2)}, u32[]{:S(2)}) collective-permute-start(bf16[1024,256]{1,0:T(8,128)(2,1)S(1)} %copy-done.2), channel_id=1, source_target_pairs={{0,8},{8,0},{16,24},{24,16},{32,40},{40,32},{48,56},{56,48},{64,72... | collective-permute-start | bytes 1572872 | tf_op jit(solution)/shard_map/ppermute | solution.py:258

commit v10 on v9

--- a/solution.py
+++ b/solution.py
@@ -15,7 +15,7 @@
 OUT_COLS = Q_COLS + HEAD
 PACKED = 32
 BEAM_AXES = "beam"
-QUERY_ORDER = (5, 7, 6, 4, 3, 2, 0, 1)
+QUERY_ORDER = (5, 7, 6, 1, 3, 2, 0, 4)
 LINE_ORDER = ((5, 1), (4, 0), (5, 0), (4, 1), (6, 0), (0, 1), (6, 1), (7, 0), (7, 1), (1, 1), (0, 0), (1, 0), (3, 0), (2, 0), (2, 1), (3, 1))
 LINE_GROUPS = [[(2 * k + c) * 8 + z for z, c in LINE_ORDER] for k in range(16)]
 CHIP_GROUPS = [[4 * q + 2 * p + c for q in QUERY_ORDER for p in (1, 0)] for c in range(2)]

time: 34.6 us -> 34.6 us (level)
  no operation moved by 1% of the time
where the time goes in v10:
time: 34.6 us; the launch traced here: 34.5 us
  blocking collectives  24.7 us (71%)
  starting transfers between devices  5.2 us (15%)
  Pallas kernels  4.49 us (13%)
    all_to_all x1, blocking collectives, body(): lax.all_to_all(terms, ('beam', 'tensor'), 0, 0, axis_index_groups=LINE_GR...  13.8 us
    all_to_all x1, blocking collectives, body(): lax.all_to_all(heads, 'beam', 0, 0, axis_index_groups=CHIP_GROUPS, tiled=...  10.9 us
    ppermute x3, starting transfers between devices, body(): lax.ppermute(messages[d], BEAM_AXES, [(i, i ^ d) for i in range(32)])  5.05 us
    pallas_call x2, Pallas kernels, attend_early(): pl.pallas_call(kernel, out_shape=jax.ShapeDtypeStruct((GROUPED * SLOTS, H...  1.66 us
    pallas_call x1, Pallas kernels, pack(): pl.pallas_call(pack_kernel, out_shape=(message,) * 4 + (pltpu.VMEM((SLOTS...  1.01 us
    pallas_call x1, Pallas kernels, body(): pl.pallas_call(finish_kernel, out_shape=jax.ShapeDtypeStruct((BEAMS, 256)...  0.78 us
    pallas_call x1, Pallas kernels, attend_far(): pl.pallas_call(attend_far_kernel, out_shape=jax.ShapeDtypeStruct((16 * SL...  0.73 us
  transfers between devices with their start and end apart: 4, of which 0 were waited for; matrix products, arithmetic and copies ran while one was open for 0% of the time, Pallas kernels for 7%

profile of v10, /device:TPU:1, one launch (start us, length us, event | category | flops | bytes accessed | tf_op | source)
XLA Modules:
  0.0 34.5 jit_solution(15391938145908087549)
XLA Ops:
  0.0 0.0 copy-start.2
  0.0 0.0 copy-start.1
  0.0 0.0 copy-start
  0.0 1.0 %pack.1 = (bf16[32,128]{1,0:T(8,128)(2,1)S(1)}, bf16[32,128]{1,0:T(8,128)(2,1)S(1)}, bf16[32,128]{1,0:T(8,128)(2,1)S(1)}, bf16[32,128]{1,0:T(8,128)(2,1)S(1)}, s32[8,128]{1,0:T(8,128)S(1)}) custom-call(s32[8]{0:T(128)} %parent_hbm.1, s32[8]{0:T(128)} %len_hbm.1, bf16[8,1024]{1,0:T(8,128)(2,1)} %q_hbm.1, bf16[8,128]{1,0:T(8,128)(2,1)} %key_hbm.1, ...), custom_call_target="tpu_custom_call" | custom-call | flops 20000000000 | tf_op jit(solution)/shard_map/pack/pallas_call | solution.py:200
  1.0 3.3 %collective-permute-start = (bf16[32,128]{1,0:T(8,128)(2,1)S(1)}, bf16[32,128]{1,0:T(8,128)(2,1)S(1)}, u32[]{:S(2)}, u32[]{:S(2)}) collective-permute-start(bf16[32,128]{1,0:T(8,128)(2,1)S(1)} %get-tuple-element.16), channel_id=1, source_target_pairs={{0,8},{8,0},{16,24},{24,16},{32,40},{40,32},{48,56},{56,48},{64,72... | collective-permute-start | bytes 24584 | tf_op jit(solution)/shard_map/ppermute | solution.py:253
  4.3 0.0 collective-permute-start.1
  4.4 1.7 %collective-permute-start.2 = (bf16[32,128]{1,0:T(8,128)(2,1)S(1)}, bf16[32,128]{1,0:T(8,128)(2,1)S(1)}, u32[]{:S(2)}, u32[]{:S(2)}) collective-permute-start(bf16[32,128]{1,0:T(8,128)(2,1)S(1)} %get-tuple-element.19), channel_id=1, source_target_pairs={{0,24},{8,16},{16,8},{24,0},{32,56},{40,48},{48,40},{56,32},{64,88... | collective-permute-start | bytes 24584 | tf_op jit(solution)/shard_map/ppermute | solution.py:253
  6.1 0.0 collective-permute-done.m1
  6.1 0.0 copy-done.2
  6.1 0.1 collective-permute-start.3
  6.2 0.0 copy-done.1
  6.2 0.0 copy-done
  6.2 1.0 %attend_near.1.before_ref = f32[64,128]{1,0:T(8,128)S(1)} custom-call(s32[8,128]{1,0:T(8,128)S(1)} %get-tuple-element.14.limit_ref, bf16[32,128]{1,0:T(8,128)(2,1)S(1)} %get-tuple-element.15.m0, bf16[32,128]{1,0:T(8,128)(2,1)S(1)} %collective-permute-done.m1, bf16[8,2048,128]{2,1,0:T(8,128)(2,1)S(1)} %bitcast.6, bf16[8,2048,128]{2,1,0:T(8,128)(2,1)S(1)} %bitcast.9), custom_call_target="tpu_custom_call" | custom-call | flops 2000000000 | tf_op jit(solution)/shard_map/attend_near/pallas_call | solution.py:223
  7.2 0.0 collective-permute-done.1.m2
  7.2 0.7 %attend_next.1.before_ref = f32[64,128]{1,0:T(8,128)S(1)} custom-call(s32[8,128]{1,0:T(8,128)S(1)} %get-tuple-element.14.limit_ref, f32[64,128]{1,0:T(8,128)S(1)} %attend_near.1.before_ref, bf16[32,128]{1,0:T(8,128)(2,1)S(1)} %collective-permute-done.1.m2, bf16[8,2048,128]{2,1,0:T(8,128)(2,1)S(1)} %bitcast.7, bf16[8,2048,128]{2,1,0:T(8,128)(2,1)S(1)} %bitcast.10), custom_call_target="tpu_custom_call" | custom-call | flops 2000000000 | tf_op jit(solution)/shard_map/attend_next/pallas_call | solution.py:223
  7.9 0.0 collective-permute-done.2.m3
  7.9 0.7 %attend_far.1 = bf16[128,1152]{1,0:T(8,128)(2,1)S(1)} custom-call(s32[8,128]{1,0:T(8,128)S(1)} %get-tuple-element.14.limit_ref, f32[64,128]{1,0:T(8,128)S(1)} %attend_next.1.before_ref, bf16[32,128]{1,0:T(8,128)(2,1)S(1)} %get-tuple-element.15.m0, bf16[32,128]{1,0:T(8,128)(2,1)S(1)} %collective-permute-done.m1, ...), custom_call_target="tpu_custom_call" | custom-call | tf_op jit(solution)/shard_map/attend_far/pallas_call | solution.py:236
  8.7 10.9 %all_to_all.22 = bf16[16,8,1152]{2,1,0:T(8,128)(2,1)S(1)} all-to-all(bf16[16,8,1152]{2,1,0:T(8,128)(2,1)S(1)} %bitcast.12), channel_id=1, replica_groups={{176,160,240,224,208,192,48,32,112,96,80,64,16,0,144,128},{184,168,248,..., dimensions={0} | all-to-all | bytes 589824 | tf_op jit(solution)/shard_map/all_to_all | solution.py:262
  19.6 0.0 collective-permute-done.3.w_core_ref
  19.6 0.3 project.1
  19.9 13.8 %all_to_all.23 = bf16[16,16,256]{2,1,0:T(8,128)(2,1)S(1)} all-to-all(bf16[16,16,256]{2,1,0:T(8,128)(2,1)S(1)} %bitcast.15), channel_id=1, replica_groups={{13,4,5,12,6,8,14,7,15,9,0,1,3,2,10,11},{29,20,21,28,22,24,30,23,31,25,..., dimensions={0} | all-to-all | bytes 262144 | tf_op jit(solution)/shard_map/all_to_all | solution.py:271
  33.7 0.8 %finish.1 = bf16[32,256]{1,0:T(8,128)(2,1)} custom-call(bf16[256,256]{1,0:T(8,128)(2,1)S(1)} %bitcast.14, bf16[32,128]{1,0:T(8,128)(2,1)S(1)} %get-tuple-element.22.place_ref), custom_call_target="tpu_custom_call" | custom-call | tf_op jit(solution)/shard_map/finish/pallas_call | solution.py:274
Async XLA Ops:
  0.0 6.1 %copy-start.2 = (bf16[1024,256]{1,0:T(8,128)(2,1)S(1)}, bf16[1024,256]{1,0:T(8,128)(2,1)}, u32[]{:S(2)}) copy-start(bf16[1024,256]{1,0:T(8,128)(2,1)} %w_ref.1) | copy-start | bytes 1572868
  0.0 6.2 %copy-start.1 = (bf16[8,1,2048,128]{3,2,1,0:T(8,128)(2,1)S(1)}, bf16[8,1,2048,128]{3,2,1,0:T(8,128)(2,1)}, u32[]{:S(2)}) copy-start(bf16[8,1,2048,128]{3,2,1,0:T(8,128)(2,1)} %param.14) | copy-start | bytes 12582916
  0.0 6.2 %copy-start = (bf16[8,1,2048,128]{3,2,1,0:T(8,128)(2,1)S(1)}, bf16[8,1,2048,128]{3,2,1,0:T(8,128)(2,1)}, u32[]{:S(2)}) copy-start(bf16[8,1,2048,128]{3,2,1,0:T(8,128)(2,1)} %param.13) | copy-start | bytes 12582916
  1.0 5.1 %collective-permute-start = (bf16[32,128]{1,0:T(8,128)(2,1)S(1)}, bf16[32,128]{1,0:T(8,128)(2,1)S(1)}, u32[]{:S(2)}, u32[]{:S(2)}) collective-permute-start(bf16[32,128]{1,0:T(8,128)(2,1)S(1)} %get-tuple-element.16), channel_id=1, source_target_pairs={{0,8},{8,0},{16,24},{24,16},{32,40},{40,32},{48,56},{56,48},{64,72... | collective-permute-start | bytes 24584 | tf_op jit(solution)/shard_map/ppermute | solution.py:253
  4.3 2.9 %collective-permute-start.1 = (bf16[32,128]{1,0:T(8,128)(2,1)S(1)}, bf16[32,128]{1,0:T(8,128)(2,1)S(1)}, u32[]{:S(2)}, u32[]{:S(2)}) collective-permute-start(bf16[32,128]{1,0:T(8,128)(2,1)S(1)} %get-tuple-element.18), channel_id=1, source_target_pairs={{0,16},{8,24},{16,0},{24,8},{32,48},{40,56},{48,32},{56,40},{64,80... | collective-permute-start | bytes 24584 | tf_op jit(solution)/shard_map/ppermute | solution.py:253
  4.4 3.6 %collective-permute-start.2 = (bf16[32,128]{1,0:T(8,128)(2,1)S(1)}, bf16[32,128]{1,0:T(8,128)(2,1)S(1)}, u32[]{:S(2)}, u32[]{:S(2)}) collective-permute-start(bf16[32,128]{1,0:T(8,128)(2,1)S(1)} %get-tuple-element.19), channel_id=1, source_target_pairs={{0,24},{8,16},{16,8},{24,0},{32,56},{40,48},{48,40},{56,32},{64,88... | collective-permute-start | bytes 24584 | tf_op jit(solution)/shard_map/ppermute | solution.py:253
  6.1 13.5 %collective-permute-start.3 = (bf16[1024,256]{1,0:T(8,128)(2,1)S(1)}, bf16[1024,256]{1,0:T(8,128)(2,1)S(1)}, u32[]{:S(2)}, u32[]{:S(2)}) collective-permute-start(bf16[1024,256]{1,0:T(8,128)(2,1)S(1)} %copy-done.2), channel_id=1, source_target_pairs={{0,8},{8,0},{16,24},{24,16},{32,40},{40,32},{48,56},{56,48},{64,72... | collective-permute-start | bytes 1572872 | tf_op jit(solution)/shard_map/ppermute | solution.py:258
